TPU v7x, 32 devices: a whole 2x2x4 slice. The times are simulated.
32 devices in a mesh: ctx: 16 (over z, y, core), tp: 2 (over x).
Axes of the slice: x: 2, y: 2, z: 4, core: 2. Of those that a mesh axis runs over, the one named last changes fastest.
Arguments:
- hidden_in: bfloat16 [4096, 2048], P('ctx', 'tp'), may hold values from -6 to 6
- ln_gain: float32 [2048], replicated, may hold values from 0.1 to 1.9
- ln_bias: float32 [2048], replicated, may hold values from -3 to 3
- w_qkv: bfloat16 [3, 2048, 2048], P(None, None, 'tp')
- w_out: bfloat16 [2048, 2048], P('tp'), may hold values from -0.375 to 0.375
- segment_ids: int32 [4096], P('ctx'), may hold values from 0 to 2, as said below
- prompt_lengths: int32 [3], replicated, may hold values from 1 to 2048, as said below
- page_table: int32 [3, 16], replicated, may hold values from -1 to 79, as said below
Outputs:
- attn_out: bfloat16 [4096, 2048], P('ctx', 'tp')
- kv_cache: bfloat16 [80, 128, 2, 2048], P('ctx', None, None, 'tp')
Inputs may be any that keep to these rules, and one draw needn't show every extreme that they name: `segment_ids`: each prompt's tokens are consecutive and the numbers never fall along the tokens; prompt i holds exactly prompt_lengths[i] tokens. `prompt_lengths`: the lengths sum to 4096; prompt 0 is shorter than 256 tokens and not a multiple of 128; prompt 1 is the longest, exactly 2048 tokens. `page_table`: for page j of prompt i with j * 128 below prompt_lengths[i], the entry is owner * 5 + slot with slot below 5, where owner is the ctx index whose tokens include the page's first token, starts_i + j * 128; distinct pages have distinct entries; all other entries are -1.
All inputs are finite; a program needn't handle non-finite values.
Results may differ from a plain program's by a relative error of at most 0.013.
Values may be sent and summed in bfloat16 or wider, within the bound.
No kernel may reach another device: no remote copies, remote signals or barrier semaphores. Data moves between devices by JAX's collectives and lax.ppermute only.
A program may use at most 128 MiB of HBM per device.

v0:
```python
import math

import jax
import jax.numpy as jnp
from jax import lax
from jax.sharding import PartitionSpec as P

HD = 256
PAGE = 128


EPSILON = 1e-05


def passed_along(value, axis, steps):
    count = lax.axis_size(axis)
    first, last = (max(0, -steps), min(count, count - steps))
    return lax.ppermute(value, axis, [(source, source + steps) for source in range(first, last)])


def normalize(inputs, norm_gain, norm_bias):
    average = jnp.sum(inputs, axis=-1, keepdims=True) / inputs.shape[-1]
    centered = inputs - average
    spread = jnp.sum(centered * centered, axis=-1, keepdims=True) / inputs.shape[-1]
    return centered * lax.rsqrt(spread + EPSILON) * norm_gain + norm_bias


def rotary(inputs, positions):
    quarter = inputs.shape[-1] // 4
    halfway = quarter // 2
    exponent = jnp.arange(0, quarter, 2).astype(jnp.float32) / quarter
    inverse = jnp.power(jnp.float32(10000.0), -exponent)
    angles = positions.astype(jnp.float32)[:, None] * inverse[None, :]
    cosine_table = jnp.concatenate([jnp.cos(angles), jnp.cos(angles)], axis=-1)[:, None, :]
    sine_table = jnp.concatenate([jnp.sin(angles), jnp.sin(angles)], axis=-1)[:, None, :]
    leading = inputs[..., :quarter]
    turned = jnp.concatenate([-leading[..., halfway:], leading[..., :halfway]], axis=-1)
    return jnp.concatenate(
        [leading * cosine_table + turned * sine_table, inputs[..., quarter:]], axis=-1
    )


def segment_positions(segment_rows, row_index, starts):
    table_span = starts.shape[0]
    matches = segment_rows[:, None] == jnp.arange(table_span, dtype=jnp.int32)[None, :]
    first_rows = jnp.sum(jnp.where(matches, starts[None, :], 0), axis=1)
    return row_index - first_rows


def attend(carry_state, query_heads, pair_block, key_marks, query_marks, causal):
    running_max, running_sum, running_acc = carry_state
    scores = jnp.einsum(
        "qhd,khd->hqk", query_heads, pair_block[:, 0], preferred_element_type=jnp.float32
    ) / math.sqrt(query_heads.shape[-1])
    visible = query_marks[:, None] == key_marks[None, :]
    if causal:
        row_count = query_heads.shape[0]
        visible = visible & (jnp.arange(row_count)[None, :] <= jnp.arange(row_count)[:, None])
    scores = jnp.where(visible[None], scores, -jnp.inf)
    newest_max = jnp.maximum(running_max, jnp.max(scores, axis=-1))
    rescale = jnp.exp(running_max - newest_max)
    weights = jnp.exp(scores - newest_max[..., None]).astype(jnp.bfloat16)
    weights = lax.optimization_barrier(weights)
    running_sum = running_sum * rescale + jnp.sum(weights.astype(jnp.float32), axis=-1)
    running_acc = running_acc * rescale[..., None] + jnp.einsum(
        "hqk,khd->hqd", weights, pair_block[:, 1], preferred_element_type=jnp.float32
    )
    return (newest_max, running_sum, running_acc)


def visit_block(carry_state, query_heads, query_marks, pair_block, key_marks):
    tail_mark = key_marks[key_marks.shape[0] - 1]
    relevant = tail_mark == query_marks[0]
    return lax.cond(
        relevant,
        lambda current: attend(current, query_heads, pair_block, key_marks, query_marks, False),
        lambda current: current,
        carry_state,
    )


def per_device(hidden_in, ln_gain, ln_bias, w_qkv, w_out, segment_ids, prompt_lengths, page_table):
    token_rows = hidden_in.shape[0]
    model_width = w_out.shape[1]
    local_heads = w_out.shape[0] // HD
    my_index = lax.axis_index("ctx")
    reach = lax.axis_size("ctx") // 2
    whole_rows = lax.all_gather(hidden_in, "tp", axis=1, tiled=True)
    normed = normalize(whole_rows.astype(jnp.float32), ln_gain, ln_bias).astype(jnp.bfloat16)
    projected = jnp.einsum("td,jdh->tjh", normed, w_qkv, preferred_element_type=jnp.float32)
    starts = jnp.cumsum(prompt_lengths) - prompt_lengths
    row_index = my_index * token_rows + jnp.arange(token_rows, dtype=jnp.int32)
    positions = segment_positions(segment_ids, row_index, starts)
    query_heads = rotary(projected[:, 0].reshape(token_rows, local_heads, HD), positions).astype(
        jnp.bfloat16
    )
    key_heads = rotary(projected[:, 1].reshape(token_rows, local_heads, HD), positions).astype(
        jnp.bfloat16
    )
    value_heads = projected[:, 2].reshape(token_rows, local_heads, HD).astype(jnp.bfloat16)
    pair_block = jnp.stack([key_heads, value_heads], axis=1)
    own_marks = segment_ids + 1
    carry_state = (
        jnp.full((local_heads, token_rows), -jnp.inf, jnp.float32),
        jnp.zeros((local_heads, token_rows), jnp.float32),
        jnp.zeros((local_heads, token_rows, HD), jnp.float32),
    )
    carry_state = attend(carry_state, query_heads, pair_block, own_marks, own_marks, True)

    def relay_step(step, state):
        moving_pair, moving_marks, current = state
        moving_pair, moving_marks = passed_along((moving_pair, moving_marks), "ctx", 1)
        current = visit_block(current, query_heads, own_marks, moving_pair, moving_marks)
        return (moving_pair, moving_marks, current)

    carry_state = lax.fori_loop(0, reach, relay_step, (pair_block, own_marks, carry_state))[2]
    running_max, running_sum, running_acc = carry_state
    attended = (running_acc / running_sum[..., None]).astype(jnp.bfloat16)
    partial_value = jnp.einsum(
        "hqd,hde->qe",
        attended,
        w_out.reshape(local_heads, HD, model_width),
        preferred_element_type=jnp.float32,
    )
    attn_out = lax.psum_scatter(
        partial_value.astype(jnp.bfloat16), "tp", scatter_dimension=1, tiled=True
    )
    tail_pair, tail_marks = passed_along((pair_block[:PAGE], own_marks[:PAGE]), "ctx", -1)
    every_pair = jnp.concatenate([pair_block, tail_pair], axis=0)
    every_marks = jnp.concatenate([own_marks, tail_marks], axis=0)
    every_index = my_index * token_rows + jnp.arange(token_rows + PAGE, dtype=jnp.int32)
    every_segment = jnp.maximum(every_marks - 1, 0)
    every_position = segment_positions(every_segment, every_index, starts)
    page_number = every_position // PAGE
    page_offset = every_position % PAGE
    page_owner = (every_index - page_offset) // token_rows
    is_owned = (every_marks > 0) & (page_owner == my_index)
    page_count = page_table.shape[1]
    table_entry = jnp.take(
        page_table.reshape(-1),
        every_segment * page_count + jnp.clip(page_number, 0, page_count - 1),
    )
    kv_slots = token_rows // PAGE + 3
    target = jnp.where(is_owned, table_entry % kv_slots * PAGE + page_offset, -1)
    placing = (jnp.arange(kv_slots * PAGE, dtype=jnp.int32)[:, None] == target[None, :]).astype(
        jnp.bfloat16
    )
    flat_pair = every_pair.reshape(token_rows + PAGE, 2 * local_heads * HD)
    written = jnp.dot(placing, flat_pair, preferred_element_type=jnp.float32).astype(jnp.bfloat16)
    kv_cache = written.reshape(kv_slots, PAGE, 2, local_heads * HD)
    return (attn_out, kv_cache)


def solution(mesh):
    return jax.shard_map(
        per_device,
        mesh=mesh,
        in_specs=(P("ctx", "tp"), P(), P(), P(None, None, "tp"), P("tp", None), P("ctx"), P(), P()),
        out_specs=(P("ctx", "tp"), P("ctx", None, None, "tp")),
        check_vma=False,
    )
```

profile of v0, /device:TPU:16, one launch (start us, length us, event | category | flops | bytes accessed | tf_op | source)
XLA Modules:
  0.0 294.1 jit_solution(7339221691849948860)
XLA Ops:
  12.9 19.0 %all-gather.2.cloned.1.call-done = bf16[256,2048]{1,0:T(8,128)(2,1)} async-done(((bf16[256,1024]{1,0:T(8,128)(2,1)}), bf16[256,2048]{1,0:T(8,128)(2,1)}) %all-gather.2.cloned.1.call-update) | async-done | bytes 1048592 | tf_op jit(solution)/shard_map/all_gather | solution.py:88
  35.2 6.6 %fusion.14 = f32[256,3,1024]{2,0,1:T(8,128)S(1)} fusion(bf16[3,2048,1024]{2,1,0:T(8,128)(2,1)} %param.15, bf16[256,2048]{1,0:T(8,128)(2,1)S(1)} %copy-done.5, f32[2048]{0:T(1024)S(1)} %copy-done.14, f32[2048]{0:T(1024)S(1)} %copy-done.15, f32[256]{0:T(256)S(1)} %add_rsqrt_fusion, f32[256]{0:T(256)S(1)} %broadcast_multiply_fusion), kind=kOutput, calls=%fused_computation.28 | convolution fusion | flops 3224371200 | bytes 16795648 | tf_op jit(solution)/shard_map/td,jdh->tjh/dot_general | solution.py:90
  55.2 179.5 %while.18 = (s32[]{:T(128)}, bf16[256,2,4,256]{3,0,2,1:T(8,128)(2,1)}, s32[256]{0:T(256)S(1)}, f32[4,256]{1,0:T(4,128)S(1)}, f32[4,256]{1,0:T(4,128)S(1)}, /*ind...) while((s32[]{:T(128)}, bf16[256,2,4,256]{3,0,2,1:T(8,128)(2,1)}, ...), condition=%wide.region_11.12_spmd, body=%wide.region_6.11_spmd.sunk | while | flops 270862336 | bytes 13832507 | solution.py:116
  57.2 3.5 %collective-permute-start.1 = (s32[256]{0:T(256)S(1)}, s32[256]{0:T(256)S(1)}, u32[]{:S(2)}, u32[]{:S(2)}) collective-permute-start(s32[256]{0:T(256)S(1)} %get-tuple-element.278), channel_id=1, source_target_pairs={{0,2},{2,4},{4,6},{6,8},{8,10},{10,12},{12,14},{14,16},{16,18},{18... | collective-permute-start | bytes 3080 | tf_op jit(solution)/shard_map/while/body/eval_jaxpr/ppermute | solution.py:18
  61.2 11.4 %collective-permute-done.1 = s32[256]{0:T(256)S(1)} collective-permute-done((s32[256]{0:T(256)S(1)}, s32[256]{0:T(256)S(1)}, u32[]{:S(2)}, u32[]{:S(2)}) %collective-permute-start.1) | collective-permute-done | bytes 1056 | tf_op jit(solution)/shard_map/while/body/eval_jaxpr/ppermute | solution.py:18
  74.5 2.3 conditional.2
  79.6 2.6 collective-permute-start.1
  82.7 12.3 %collective-permute-done.1 = s32[256]{0:T(256)S(1)} collective-permute-done((s32[256]{0:T(256)S(1)}, s32[256]{0:T(256)S(1)}, u32[]{:S(2)}, u32[]{:S(2)}) %collective-permute-start.1) | collective-permute-done | bytes 1056 | tf_op jit(solution)/shard_map/while/body/eval_jaxpr/ppermute | solution.py:18
  96.9 2.3 conditional.2
  102.1 1.9 collective-permute-start.1
  104.5 12.9 %collective-permute-done.1 = s32[256]{0:T(256)S(1)} collective-permute-done((s32[256]{0:T(256)S(1)}, s32[256]{0:T(256)S(1)}, u32[]{:S(2)}, u32[]{:S(2)}) %collective-permute-start.1) | collective-permute-done | bytes 1056 | tf_op jit(solution)/shard_map/while/body/eval_jaxpr/ppermute | solution.py:18
  119.3 2.3 conditional.2
  124.5 1.9 collective-permute-start.1
  126.9 12.9 %collective-permute-done.1 = s32[256]{0:T(256)S(1)} collective-permute-done((s32[256]{0:T(256)S(1)}, s32[256]{0:T(256)S(1)}, u32[]{:S(2)}, u32[]{:S(2)}) %collective-permute-start.1) | collective-permute-done | bytes 1056 | tf_op jit(solution)/shard_map/while/body/eval_jaxpr/ppermute | solution.py:18
  141.8 2.3 conditional.2
  146.9 1.9 collective-permute-start.1
  149.4 12.9 %collective-permute-done.1 = s32[256]{0:T(256)S(1)} collective-permute-done((s32[256]{0:T(256)S(1)}, s32[256]{0:T(256)S(1)}, u32[]{:S(2)}, u32[]{:S(2)}) %collective-permute-start.1) | collective-permute-done | bytes 1056 | tf_op jit(solution)/shard_map/while/body/eval_jaxpr/ppermute | solution.py:18
  164.2 2.3 conditional.2
  169.4 1.9 collective-permute-start.1
  171.8 12.9 %collective-permute-done.1 = s32[256]{0:T(256)S(1)} collective-permute-done((s32[256]{0:T(256)S(1)}, s32[256]{0:T(256)S(1)}, u32[]{:S(2)}, u32[]{:S(2)}) %collective-permute-start.1) | collective-permute-done | bytes 1056 | tf_op jit(solution)/shard_map/while/body/eval_jaxpr/ppermute | solution.py:18
  186.7 2.3 conditional.2
  194.2 12.9 %collective-permute-done.1 = s32[256]{0:T(256)S(1)} collective-permute-done((s32[256]{0:T(256)S(1)}, s32[256]{0:T(256)S(1)}, u32[]{:S(2)}, u32[]{:S(2)}) %collective-permute-start.1) | collective-permute-done | bytes 1056 | tf_op jit(solution)/shard_map/while/body/eval_jaxpr/ppermute | solution.py:18
  209.1 2.3 conditional.2
  216.7 12.9 %collective-permute-done.1 = s32[256]{0:T(256)S(1)} collective-permute-done((s32[256]{0:T(256)S(1)}, s32[256]{0:T(256)S(1)}, u32[]{:S(2)}, u32[]{:S(2)}) %collective-permute-start.1) | collective-permute-done | bytes 1056 | tf_op jit(solution)/shard_map/while/body/eval_jaxpr/ppermute | solution.py:18
  231.5 2.3 conditional.2
  234.8 4.5 %fusion.5 = bf16[256,2048]{1,0:T(8,128)(2,1)} fusion(bf16[4,256,2048]{2,1,0:T(8,128)(2,1)} %bitcast.104, f32[4,256,256]{2,1,0:T(8,128)S(1)} %get-tuple-element.75, f32[4,256]{1,0:T(4,128)S(1)} %get-tuple-element.76), kind=kOutput, calls=%fused_computation.16 | convolution fusion | flops 1074790400 | bytes 6295552 | tf_op jit(solution)/shard_map/hqd,hde->qe/dot_general | solution.py:119
  239.3 2.1 collective-permute-start.2
  243.7 3.7 %collective-permute-start.3 = (bf16[128,2,4,256]{3,0,2,1:T(8,128)(2,1)S(1)}, bf16[128,2,4,256]{3,0,2,1:T(8,128)(2,1)S(1)}, u32[]{:S(2)}, u32[]{:S(2)}) collective-permute-start(bf16[128,2,4,256]{3,0,2,1:T(8,128)(2,1)S(1)} %slice.129), channel_id=1, source_target_pairs={{2,0},{4,2},{6,4},{8,6},{10,8},{12,10},{14,12},{16,14},{18,16},{20... | collective-permute-start | bytes 1572872 | tf_op jit(solution)/shard_map/ppermute | solution.py:18
  247.4 4.3 %fusion.43 = (s32[384]{0:T(512)S(1)}, s32[384,1]{0,1:T(1,128)S(1)}) fusion(s32[]{:T(128)} %bitcast.53, s32[]{:T(128)} %bitcast.54, s32[]{:T(128)} %bitcast.55, s32[]{:T(128)} %bitcast.56, s32[]{:T(128)} %bitcast.57, s32[]{:T(128)} %bitcast.59, s32[]{:T(128)} %bitcast.58, s32[384]{0:T(512)S(1)} %select_reduce_fusion, s32[]{:T(128)S(6)} %mul.131, ...), kind=kLoop, calls=%fused_computation.151 | loop fusion | flops 14592 | bytes 6176 | tf_op jit(solution)/shard_map/jit(_take)/gather | solution.py:139
  251.9 25.8 %fusion.37 = s32[384]{0:T(512)S(1)} fusion(pred[384]{0:T(512)(128)(4,1)S(1)} %get-tuple-element.117, pred[384]{0:T(512)(128)(4,1)S(1)} %get-tuple-element.116, pred[384]{0:T(512)(128)(4,1)S(1)} %get-tuple-element.115, pred[384]{0:T(512)(128)(4,1)S(1)} %get-tuple-element.114, pred[384]{0:T(512)(128)(4,1)S(1)} %get-tuple-element.113, ...), kind=kLoop, calls=%fused_computation.139 | loop fusion | flops 39552 | bytes 22060 | tf_op jit(solution)/shard_map/jit(_where)/select_n | solution.py:144
  280.7 3.0 %convolution_convert_fusion = bf16[640,2048]{1,0:T(8,128)(2,1)S(1)} fusion(bf16[384,2048]{0,1:T(8,128)(2,1)} %bitcast.101, s32[384]{0:T(512)S(1)} %fusion.37), kind=kOutput, calls=%fused_computation.12 | convolution fusion | flops 1008189440 | bytes 4195840 | tf_op jit(solution)/shard_map/dot_general | solution.py:149
  283.7 3.5 %reshape.436 = bf16[5,128,2,1024]{3,2,1,0:T(2,128)(2,1)} reshape(bf16[640,2048]{1,0:T(8,128)(2,1)S(1)} %convolution_convert_fusion) | data formatting | bytes 5242880 | tf_op jit(solution)/shard_map/reshape | solution.py:150
  (207 shorter events, 81.5 us)
Async XLA Ops:
  7.2 28.0 %copy-start.14 = (f32[2048]{0:T(1024)S(1)}, f32[2048]{0:T(1024)}, u32[]{:S(2)}) copy-start(f32[2048]{0:T(1024)} %param.14) | copy-start | bytes 24580
  7.2 28.0 %copy-start.15 = (f32[2048]{0:T(1024)S(1)}, f32[2048]{0:T(1024)}, u32[]{:S(2)}) copy-start(f32[2048]{0:T(1024)} %param.13) | copy-start | bytes 24580
  7.2 24.8 %all-gather.2.cloned.1.call-start = ((), (), s32[]{:S(2)}) async-start(), calls=%async_computation.1 | async-start | bytes 1572864 | tf_op jit(solution)/shard_map/all_gather | solution.py:88
  7.9 279.3 %reduce-scatter.2.cloned.1.call-start = ((), (), s32[]{:S(2)}) async-start(), calls=%async_computation.2 | async-start | bytes 1572864 | tf_op jit(solution)/shard_map/reduce_scatter | solution.py:125
  32.0 3.2 %copy-start.5 = (bf16[256,2048]{1,0:T(8,128)(2,1)S(1)}, bf16[256,2048]{1,0:T(8,128)(2,1)}, u32[]{:S(2)}) copy-start(bf16[256,2048]{1,0:T(8,128)(2,1)} %all-gather.2.cloned.1.call-done) | copy-start | bytes 3145732
  43.5 1.7 copy-start.1
  46.9 1.4 copy-start
  47.4 6.2 %copy-start.2 = (bf16[256,4,192]{2,0,1:T(8,128)(2,1)}, bf16[256,4,192]{2,0,1:T(8,128)(2,1)S(1)}, u32[]{:S(2)}) copy-start(bf16[256,4,192]{2,0,1:T(8,128)(2,1)S(1)} %copy.79) | copy-start | bytes 1179652
  49.9 1.4 copy-start.8
  50.0 3.6 %copy-start.4 = (bf16[1,32,4,8,256]{4,3,1,2,0:T(8,128)(2,1)}, bf16[1,32,4,8,256]{4,3,1,2,0:T(8,128)(2,1)S(1)}, u32[]{:S(2)}) copy-start(bf16[1,32,4,8,256]{4,3,1,2,0:T(8,128)(2,1)S(1)} %copy.78) | copy-start | bytes 1572868
  50.6 1.3 slice-start.1
  50.6 1.3 copy-start.11
  55.2 19.2 %collective-permute-start = (bf16[256,2,4,256]{3,0,2,1:T(8,128)(2,1)}, bf16[256,2,4,256]{3,0,2,1:T(8,128)(2,1)S(1)}, u32[]{:S(2)}, u32[]{:S(2)}) collective-permute-start(bf16[256,2,4,256]{3,0,2,1:T(8,128)(2,1)} %get-tuple-element.277), channel_id=1, source_target_pairs={{0,2},{2,4},{4,6},{6,8},{8,10},{10,12},{12,14},{14,16},{16,18},{18... | collective-permute-start | bytes 3145736 | tf_op jit(solution)/shard_map/while/body/eval_jaxpr/ppermute | solution.py:18
  57.2 15.3 %collective-permute-start.1 = (s32[256]{0:T(256)S(1)}, s32[256]{0:T(256)S(1)}, u32[]{:S(2)}, u32[]{:S(2)}) collective-permute-start(s32[256]{0:T(256)S(1)} %get-tuple-element.278), channel_id=1, source_target_pairs={{0,2},{2,4},{4,6},{6,8},{8,10},{10,12},{12,14},{14,16},{16,18},{18... | collective-permute-start | bytes 3080 | tf_op jit(solution)/shard_map/while/body/eval_jaxpr/ppermute | solution.py:18
  77.7 19.2 %collective-permute-start = (bf16[256,2,4,256]{3,0,2,1:T(8,128)(2,1)}, bf16[256,2,4,256]{3,0,2,1:T(8,128)(2,1)S(1)}, u32[]{:S(2)}, u32[]{:S(2)}) collective-permute-start(bf16[256,2,4,256]{3,0,2,1:T(8,128)(2,1)} %get-tuple-element.277), channel_id=1, source_target_pairs={{0,2},{2,4},{4,6},{6,8},{8,10},{10,12},{12,14},{14,16},{16,18},{18... | collective-permute-start | bytes 3145736 | tf_op jit(solution)/shard_map/while/body/eval_jaxpr/ppermute | solution.py:18
  79.6 15.3 %collective-permute-start.1 = (s32[256]{0:T(256)S(1)}, s32[256]{0:T(256)S(1)}, u32[]{:S(2)}, u32[]{:S(2)}) collective-permute-start(s32[256]{0:T(256)S(1)} %get-tuple-element.278), channel_id=1, source_target_pairs={{0,2},{2,4},{4,6},{6,8},{8,10},{10,12},{12,14},{14,16},{16,18},{18... | collective-permute-start | bytes 3080 | tf_op jit(solution)/shard_map/while/body/eval_jaxpr/ppermute | solution.py:18
  100.1 19.2 %collective-permute-start = (bf16[256,2,4,256]{3,0,2,1:T(8,128)(2,1)}, bf16[256,2,4,256]{3,0,2,1:T(8,128)(2,1)S(1)}, u32[]{:S(2)}, u32[]{:S(2)}) collective-permute-start(bf16[256,2,4,256]{3,0,2,1:T(8,128)(2,1)} %get-tuple-element.277), channel_id=1, source_target_pairs={{0,2},{2,4},{4,6},{6,8},{8,10},{10,12},{12,14},{14,16},{16,18},{18... | collective-permute-start | bytes 3145736 | tf_op jit(solution)/shard_map/while/body/eval_jaxpr/ppermute | solution.py:18
  102.1 15.3 %collective-permute-start.1 = (s32[256]{0:T(256)S(1)}, s32[256]{0:T(256)S(1)}, u32[]{:S(2)}, u32[]{:S(2)}) collective-permute-start(s32[256]{0:T(256)S(1)} %get-tuple-element.278), channel_id=1, source_target_pairs={{0,2},{2,4},{4,6},{6,8},{8,10},{10,12},{12,14},{14,16},{16,18},{18... | collective-permute-start | bytes 3080 | tf_op jit(solution)/shard_map/while/body/eval_jaxpr/ppermute | solution.py:18
  122.6 19.2 %collective-permute-start = (bf16[256,2,4,256]{3,0,2,1:T(8,128)(2,1)}, bf16[256,2,4,256]{3,0,2,1:T(8,128)(2,1)S(1)}, u32[]{:S(2)}, u32[]{:S(2)}) collective-permute-start(bf16[256,2,4,256]{3,0,2,1:T(8,128)(2,1)} %get-tuple-element.277), channel_id=1, source_target_pairs={{0,2},{2,4},{4,6},{6,8},{8,10},{10,12},{12,14},{14,16},{16,18},{18... | collective-permute-start | bytes 3145736 | tf_op jit(solution)/shard_map/while/body/eval_jaxpr/ppermute | solution.py:18
  124.5 15.3 %collective-permute-start.1 = (s32[256]{0:T(256)S(1)}, s32[256]{0:T(256)S(1)}, u32[]{:S(2)}, u32[]{:S(2)}) collective-permute-start(s32[256]{0:T(256)S(1)} %get-tuple-element.278), channel_id=1, source_target_pairs={{0,2},{2,4},{4,6},{6,8},{8,10},{10,12},{12,14},{14,16},{16,18},{18... | collective-permute-start | bytes 3080 | tf_op jit(solution)/shard_map/while/body/eval_jaxpr/ppermute | solution.py:18
  145.0 19.2 %collective-permute-start = (bf16[256,2,4,256]{3,0,2,1:T(8,128)(2,1)}, bf16[256,2,4,256]{3,0,2,1:T(8,128)(2,1)S(1)}, u32[]{:S(2)}, u32[]{:S(2)}) collective-permute-start(bf16[256,2,4,256]{3,0,2,1:T(8,128)(2,1)} %get-tuple-element.277), channel_id=1, source_target_pairs={{0,2},{2,4},{4,6},{6,8},{8,10},{10,12},{12,14},{14,16},{16,18},{18... | collective-permute-start | bytes 3145736 | tf_op jit(solution)/shard_map/while/body/eval_jaxpr/ppermute | solution.py:18
  146.9 15.3 %collective-permute-start.1 = (s32[256]{0:T(256)S(1)}, s32[256]{0:T(256)S(1)}, u32[]{:S(2)}, u32[]{:S(2)}) collective-permute-start(s32[256]{0:T(256)S(1)} %get-tuple-element.278), channel_id=1, source_target_pairs={{0,2},{2,4},{4,6},{6,8},{8,10},{10,12},{12,14},{14,16},{16,18},{18... | collective-permute-start | bytes 3080 | tf_op jit(solution)/shard_map/while/body/eval_jaxpr/ppermute | solution.py:18
  167.5 19.2 %collective-permute-start = (bf16[256,2,4,256]{3,0,2,1:T(8,128)(2,1)}, bf16[256,2,4,256]{3,0,2,1:T(8,128)(2,1)S(1)}, u32[]{:S(2)}, u32[]{:S(2)}) collective-permute-start(bf16[256,2,4,256]{3,0,2,1:T(8,128)(2,1)} %get-tuple-element.277), channel_id=1, source_target_pairs={{0,2},{2,4},{4,6},{6,8},{8,10},{10,12},{12,14},{14,16},{16,18},{18... | collective-permute-start | bytes 3145736 | tf_op jit(solution)/shard_map/while/body/eval_jaxpr/ppermute | solution.py:18
  169.4 15.3 %collective-permute-start.1 = (s32[256]{0:T(256)S(1)}, s32[256]{0:T(256)S(1)}, u32[]{:S(2)}, u32[]{:S(2)}) collective-permute-start(s32[256]{0:T(256)S(1)} %get-tuple-element.278), channel_id=1, source_target_pairs={{0,2},{2,4},{4,6},{6,8},{8,10},{10,12},{12,14},{14,16},{16,18},{18... | collective-permute-start | bytes 3080 | tf_op jit(solution)/shard_map/while/body/eval_jaxpr/ppermute | solution.py:18
  189.9 19.2 %collective-permute-start = (bf16[256,2,4,256]{3,0,2,1:T(8,128)(2,1)}, bf16[256,2,4,256]{3,0,2,1:T(8,128)(2,1)S(1)}, u32[]{:S(2)}, u32[]{:S(2)}) collective-permute-start(bf16[256,2,4,256]{3,0,2,1:T(8,128)(2,1)} %get-tuple-element.277), channel_id=1, source_target_pairs={{0,2},{2,4},{4,6},{6,8},{8,10},{10,12},{12,14},{14,16},{16,18},{18... | collective-permute-start | bytes 3145736 | tf_op jit(solution)/shard_map/while/body/eval_jaxpr/ppermute | solution.py:18
  191.8 15.3 %collective-permute-start.1 = (s32[256]{0:T(256)S(1)}, s32[256]{0:T(256)S(1)}, u32[]{:S(2)}, u32[]{:S(2)}) collective-permute-start(s32[256]{0:T(256)S(1)} %get-tuple-element.278), channel_id=1, source_target_pairs={{0,2},{2,4},{4,6},{6,8},{8,10},{10,12},{12,14},{14,16},{16,18},{18... | collective-permute-start | bytes 3080 | tf_op jit(solution)/shard_map/while/body/eval_jaxpr/ppermute | solution.py:18
  212.3 19.2 %collective-permute-start = (bf16[256,2,4,256]{3,0,2,1:T(8,128)(2,1)}, bf16[256,2,4,256]{3,0,2,1:T(8,128)(2,1)S(1)}, u32[]{:S(2)}, u32[]{:S(2)}) collective-permute-start(bf16[256,2,4,256]{3,0,2,1:T(8,128)(2,1)} %get-tuple-element.277), channel_id=1, source_target_pairs={{0,2},{2,4},{4,6},{6,8},{8,10},{10,12},{12,14},{14,16},{16,18},{18... | collective-permute-start | bytes 3145736 | tf_op jit(solution)/shard_map/while/body/eval_jaxpr/ppermute | solution.py:18
  214.3 15.3 %collective-permute-start.1 = (s32[256]{0:T(256)S(1)}, s32[256]{0:T(256)S(1)}, u32[]{:S(2)}, u32[]{:S(2)}) collective-permute-start(s32[256]{0:T(256)S(1)} %get-tuple-element.278), channel_id=1, source_target_pairs={{0,2},{2,4},{4,6},{6,8},{8,10},{10,12},{12,14},{14,16},{16,18},{18... | collective-permute-start | bytes 3080 | tf_op jit(solution)/shard_map/while/body/eval_jaxpr/ppermute | solution.py:18
  234.8 6.6 %copy-start.13 = (s32[3,16]{1,0:T(4,128)S(1)}, s32[3,16]{1,0:T(4,128)}, u32[]{:S(2)}) copy-start(s32[3,16]{1,0:T(4,128)} %param.19) | copy-start | bytes 580
  239.3 38.5 %copy-start.3 = (bf16[256,4,192]{2,0,1:T(8,128)(2,1)S(1)}, bf16[256,4,192]{2,0,1:T(8,128)(2,1)}, u32[]{:S(2)}) copy-start(bf16[256,4,192]{2,0,1:T(8,128)(2,1)} %copy-done.2) | copy-start | bytes 1179652
  239.3 4.3 %collective-permute-start.2 = (s32[128]{0:T(128)S(1)}, s32[128]{0:T(128)S(1)}, u32[]{:S(2)}, u32[]{:S(2)}) collective-permute-start(s32[128]{0:T(128)S(1)} %slice.67), channel_id=1, source_target_pairs={{2,0},{4,2},{6,4},{8,6},{10,8},{12,10},{14,12},{16,14},{18,16},{20... | collective-permute-start | bytes 1544 | tf_op jit(solution)/shard_map/ppermute | solution.py:18
  243.7 34.1 %collective-permute-start.3 = (bf16[128,2,4,256]{3,0,2,1:T(8,128)(2,1)S(1)}, bf16[128,2,4,256]{3,0,2,1:T(8,128)(2,1)S(1)}, u32[]{:S(2)}, u32[]{:S(2)}) collective-permute-start(bf16[128,2,4,256]{3,0,2,1:T(8,128)(2,1)S(1)} %slice.129), channel_id=1, source_target_pairs={{2,0},{4,2},{6,4},{8,6},{10,8},{12,10},{14,12},{16,14},{18,16},{20... | collective-permute-start | bytes 1572872 | tf_op jit(solution)/shard_map/ppermute | solution.py:18
  (6 other events, 6.4 us)
Sparse Core Ops, SparseCore 0:
  9.6 22.3 all-gather.1
  239.4 18.4 reduce-scatter.1
where the time goes:
time: 296 us; the launch traced here: 294 us
  waiting for transfers between devices  121 us (41%)
  other arithmetic  44.1 us (15%)
  starting transfers between devices  38.7 us (13%)
  local copies, waits for them, and re-layouts  35.7 us (12%)
  matrix products  29.4 us (10%)
  between operations  14.4 us (5%)
  loops' own time  10.9 us (4%)
    ppermute x18, waiting for transfers between devices, passed_along(): lax.ppermute(value, axis, [(source, source + steps) for source in range(f...  101 us
    ppermute x18, starting transfers between devices, passed_along(): lax.ppermute(value, axis, [(source, source + steps) for source in range(f...  38.6 us
    select_n x1, other arithmetic, per_device(): jnp.where(is_owned, table_entry % kv_slots * PAGE + page_offset, -1)  25.8 us
    all_gather x1, waiting for transfers between devices, per_device(): whole_rows = lax.all_gather(hidden_in, 'tp', axis=1, tiled=True)  19 us
    dot_general x9, matrix products, attend(): jnp.einsum('qhd,khd->hqk', query_heads, pair_block[:, 0], preferred_eleme...  11.5 us
    another operation x1, loops' own time, per_device(): lax.fori_loop(0, reach, relay_step, (pair_block, own_marks, carry_state))[2]  10.4 us
    while x16, local copies, waits for them, and re-layouts  7.8 us
    dot_general x1, matrix products, per_device(): jnp.einsum('td,jdh->tjh', normed, w_qkv, preferred_element_type=jnp.float32)  6.59 us
  transfers between devices with their start and end apart: 20, of which 9 were waited for; matrix products, arithmetic and copies ran while one was open for 19% of the time, Pallas kernels for 0%

commit v1 on v0

--- a/solution.py
+++ b/solution.py
@@ -1,15 +1,396 @@
+import functools
 import math
 
 import jax
 import jax.numpy as jnp
 from jax import lax
+from jax.experimental import pallas as pl
+from jax.experimental.pallas import tpu as pltpu
 from jax.sharding import PartitionSpec as P
 
 HD = 256
 PAGE = 128
-
-
 EPSILON = 1e-05
+ROT = HD // 4
+LANES = 128
+VMEM = pltpu.VMEM
+MASKED = -1e30
+LOG2E = 1.4426950408889634
+
+
+def start_rows(prompt_lengths):
+    return (jnp.cumsum(prompt_lengths) - prompt_lengths).astype(jnp.int32)
+
+
+def first_of_prompt(rows, starts):
+    first = jnp.zeros_like(rows)
+    for prompt in range(starts.shape[0]):
+        first = jnp.where(rows >= starts[prompt], starts[prompt], first)
+    return first
+
+
+def rotary_tables(positions):
+    exponent = jnp.arange(0, ROT, 2).astype(jnp.float32) / ROT
+    inverse = jnp.power(jnp.float32(10000.0), -exponent)
+    angles = positions.astype(jnp.float32)[:, None] * inverse[None, :]
+    cosine, sine = jnp.cos(angles), jnp.sin(angles)
+    rows, half = angles.shape
+    blank = jnp.zeros((rows, LANES - 2 * half), jnp.float32)
+    none = jnp.zeros_like(sine)
+    keep = jnp.concatenate([cosine, cosine, blank + 1.0], axis=1)
+    from_below = jnp.concatenate([none, sine, blank], axis=1)
+    from_above = jnp.concatenate([-sine, none, blank], axis=1)
+    return keep, from_below, from_above
+
+
+def qkv_kernel(info, own, other, gain, bias, keep, below, above, weights, *refs):
+    splits = (len(refs) - 4) // 2
+    q_refs, kv_refs = refs[:splits], refs[splits : 2 * splits]
+    keys_ref, values_ref, head_ref, normed = refs[2 * splits :]
+    step = pl.program_id(0)
+    width = own.shape[1]
+    rank = info[1]
+
+    @pl.when(step == 0)
+    def _():
+        full = 2 * width
+        mine = own[...].astype(jnp.float32)
+        theirs = other[...].astype(jnp.float32)
+        total = jnp.sum(mine, axis=-1, keepdims=True) + jnp.sum(theirs, axis=-1, keepdims=True)
+        average = total / full
+        mine, theirs = mine - average, theirs - average
+        spread = jnp.sum(mine * mine, axis=-1, keepdims=True) + jnp.sum(
+            theirs * theirs, axis=-1, keepdims=True
+        )
+        scale = lax.rsqrt(spread / full + EPSILON)
+        for part, place in ((mine, rank), (theirs, 1 - rank)):
+            columns = pl.ds(pl.multiple_of(place * width, width), width)
+            normed[:, columns] = (part * scale * gain[:, columns] + bias[:, columns]).astype(
+                jnp.bfloat16
+            )
+
+    rows = normed[...]
+    query, key, value = (
+        jnp.dot(rows, weights[j], preferred_element_type=jnp.float32) for j in range(3)
+    )
+
+    def turned(inputs):
+        leading = inputs[:, :LANES]
+        leading = (
+            leading * keep[...]
+            + pltpu.roll(leading, ROT // 2, 1) * below[...]
+            + pltpu.roll(leading, LANES - ROT // 2, 1) * above[...]
+        )
+        return jnp.concatenate([leading, inputs[:, LANES:]], axis=1).astype(jnp.bfloat16)
+
+    query, key, value = turned(query), turned(key), value.astype(jnp.bfloat16)
+    keys_ref[...] = key
+    values_ref[...] = value
+    for split in range(splits):
+
+        @pl.when(step == split)
+        def _():
+            q_refs[split][...] = query
+            kv_refs[split][:, :HD] = key
+            kv_refs[split][:, HD:] = value
+
+    page = head_ref.shape[1]
+    head_ref[0] = key[:page]
+    head_ref[1] = value[:page]
+
+
+def project(info, own, other, gain, bias, tables, w_qkv, splits):
+    rows, width = own.shape
+    heads = w_qkv.shape[2] // HD
+    whole = lambda *shape: pl.BlockSpec(shape, lambda m, info: (0,) * len(shape))
+    by_head = pl.BlockSpec((rows, HD), lambda m, info: (0, info[0] ^ m))
+    return pl.pallas_call(
+        qkv_kernel,
+        grid_spec=pltpu.PrefetchScalarGridSpec(
+            num_scalar_prefetch=1,
+            grid=(splits,),
+            in_specs=[
+                whole(rows, width),
+                whole(rows, width),
+                whole(1, 2 * width),
+                whole(1, 2 * width),
+                whole(rows, LANES),
+                whole(rows, LANES),
+                whole(rows, LANES),
+                pl.BlockSpec((3, 2 * width, HD), lambda m, info: (0, 0, info[0] ^ m)),
+            ],
+            out_specs=[whole(rows, HD)] * splits
+            + [whole(rows, 2 * HD)] * splits
+            + [by_head, by_head, pl.BlockSpec((2, PAGE, HD), lambda m, info: (0, 0, info[0] ^ m))],
+            scratch_shapes=[VMEM((rows, 2 * width), jnp.bfloat16)],
+        ),
+        out_shape=[jax.ShapeDtypeStruct((rows, HD), jnp.bfloat16)] * splits
+        + [jax.ShapeDtypeStruct((rows, 2 * HD), jnp.bfloat16)] * splits
+        + [jax.ShapeDtypeStruct((rows, heads * HD), jnp.bfloat16)] * 2
+        + [jax.ShapeDtypeStruct((2, PAGE, heads * HD), jnp.bfloat16)],
+        compiler_params=pltpu.CompilerParams(vmem_limit_bytes=40 * 2**20),
+        cost_estimate=pl.CostEstimate(
+            flops=2 * rows * 2 * width * 3 * heads * HD,
+            bytes_accessed=2 * 3 * 2 * width * heads * HD,
+            transcendentals=0,
+        ),
+        name="project",
+    )(info, own, other, gain, bias, *tables, w_qkv)
+
+
+def soft_attend(query, keys, values, first_key, last_key, base):
+    scores = lax.dot_general(
+        query, keys, (((1,), (1,)), ((), ())), preferred_element_type=jnp.float32
+    )
+    column = base + lax.broadcasted_iota(jnp.int32, scores.shape, 1)
+    visible = (column >= first_key) & (column <= last_key)
+    scores = jnp.where(visible, scores, MASKED)
+    peak = jnp.max(scores, axis=-1, keepdims=True)
+    factor = LOG2E / math.sqrt(HD)
+    weights = jnp.exp2((scores - peak) * factor).astype(jnp.bfloat16)
+    total = jnp.sum(weights.astype(jnp.float32), axis=-1, keepdims=True)
+    mixed = jnp.dot(weights, values, preferred_element_type=jnp.float32) / total
+    return mixed, peak * factor + jnp.log2(total)
+
+
+def row_bounds(info, rows):
+    first = jnp.zeros_like(rows)
+    for prompt in range(3, 6):
+        first = jnp.where(rows >= info[prompt], info[prompt], first)
+    return first
+
+
+def arrange(info, mine_refs, theirs_refs, keys, values):
+    rows = mine_refs[0].shape[0]
+    for refs, core in ((mine_refs, info[2]), (theirs_refs, 1 - info[2])):
+        for split, ref in enumerate(refs):
+            at = pl.ds(pl.multiple_of((2 * (info[0] ^ split) + core) * rows, rows), rows)
+            keys[at, :] = ref[:, :HD]
+            values[at, :] = ref[:, HD:]
+
+
+def tail_kernel(info, *refs):
+    splits = (len(refs) - 3) // 3
+    queries, mine, theirs = refs[:splits], refs[splits : 2 * splits], refs[2 * splits : 3 * splits]
+    out, keys, values = refs[3 * splits :]
+    rows = queries[0].shape[0]
+
+    @pl.when((info[6] == 0) & (info[2] == 0))
+    def _():
+        arrange(info, mine, theirs, keys, values)
+        query = queries[0][...]
+        for split in range(1, splits):
+            query = jnp.where(info[0] == split, queries[split][...], query)
+        group_rows = 2 * splits * rows
+        row = group_rows + lax.broadcasted_iota(jnp.int32, (rows, 1), 0)
+        first = row_bounds(info, row)
+        mixed, level = soft_attend(query, keys[...], values[...], first, row, 0)
+        level = jnp.where(first < group_rows, level, MASKED)
+        out[:, :HD] = mixed.astype(jnp.bfloat16)
+        lane = lax.broadcasted_iota(jnp.int32, (rows, LANES), 1)
+        high = level.astype(jnp.bfloat16).astype(jnp.float32)
+        middle = (level - high).astype(jnp.bfloat16).astype(jnp.float32)
+        low = level - high - middle
+        out[:, HD:] = jnp.where(
+            lane == 0, high, jnp.where(lane == 1, middle, jnp.where(lane == 2, low, 0.0))
+        ).astype(jnp.bfloat16)
+
+
+def main_kernel(info, *refs):
+    splits = (len(refs) - 6) // 4
+    queries, mine, theirs = refs[:splits], refs[splits : 2 * splits], refs[2 * splits : 3 * splits]
+    outs = refs[3 * splits : 4 * splits]
+    first_mixed, first_level, keys, values, asked, gathered = refs[4 * splits :]
+    rows = queries[0].shape[0]
+    arrange(info, mine, theirs, keys, values)
+    for split in range(splits):
+        at = pl.ds(pl.multiple_of((info[0] ^ split) * rows, rows), rows)
+        asked[at, :] = queries[split][...]
+    for place in range(splits):
+        reach = (2 * place + 2) * rows
+        row = info[6] + (2 * place + info[2]) * rows + lax.broadcasted_iota(jnp.int32, (rows, 1), 0)
+        mixed, level = soft_attend(
+            asked[place * rows : (place + 1) * rows, :],
+            keys[:reach, :],
+            values[:reach, :],
+            row_bounds(info, row),
+            row,
+            info[6],
+        )
+        gathered[place * rows : (place + 1) * rows, :] = mixed.astype(jnp.bfloat16)
+        if place == 0:
+            first_mixed[...] = mixed
+            first_level[...] = jnp.broadcast_to(level, first_level.shape)
+    for split in range(splits):
+        at = pl.ds(pl.multiple_of((info[0] ^ split) * rows, rows), rows)
+        outs[split][...] = gathered[at, :]
+
+
+def on_core(kernel, out_shape, scratch, name, flops):
+    def call(info, *operands):
+        return pl.pallas_call(
+            kernel,
+            in_specs=[pl.BlockSpec(memory_space=pltpu.SMEM)]
+            + [pl.BlockSpec(memory_space=pltpu.VMEM)] * len(operands),
+            out_specs=jax.tree.map(lambda _: pl.BlockSpec(memory_space=pltpu.VMEM), out_shape),
+            out_shape=out_shape,
+            scratch_shapes=scratch,
+            compiler_params=pltpu.CompilerParams(vmem_limit_bytes=40 * 2**20),
+            cost_estimate=pl.CostEstimate(flops=flops, bytes_accessed=4 * 2**20, transcendentals=0),
+            name=name,
+        )(info, *operands)
+
+    return call
+
+
+def out_kernel(info, *refs):
+    splits = (len(refs) - 4) // 2
+    mine, theirs = refs[:splits], refs[splits : 2 * splits]
+    w_own, w_same, w_swap, out = refs[2 * splits :]
+    half = splits // 2
+    total = jnp.zeros(out.shape, jnp.float32)
+    for split in range(splits):
+        head = info[0] ^ split
+        at = pl.ds(pl.multiple_of(head * HD, HD), HD)
+        total += jnp.dot(mine[split][...], w_own[at, :], preferred_element_type=jnp.float32)
+    for split in range(splits):
+        head = info[0] ^ split
+        at = pl.ds(pl.multiple_of(lax.rem(head, half) * HD, HD), HD)
+        same = head // half == info[2]
+        weight = jnp.where(same, w_same[at, :], w_swap[at, :])
+        total += jnp.dot(theirs[split][...], weight, preferred_element_type=jnp.float32)
+    out[...] = total.astype(jnp.bfloat16)
+
+
+def split_heads(hidden_in, ln_gain, ln_bias, w_qkv, w_out, segment_ids, prompt_lengths, page_table):
+    rows, width = hidden_in.shape
+    splits = w_out.shape[0] // HD
+    count = lax.axis_size("ctx")
+    index = lax.axis_index("ctx")
+    rank = lax.axis_index("tp")
+    group = 2 * splits
+    core, place = index % 2, index // 2 % splits
+    starts = start_rows(prompt_lengths)
+    scalars = [place, rank, core, starts[0], starts[1], starts[2], index // group * group * rows, index]
+    info = jnp.stack([jnp.asarray(v, jnp.int32) for v in scalars])
+
+    def across(value, ctx_mask, tp_mask=0):
+        pairs = []
+        for c in range(count):
+            for t in range(2):
+                pairs.append((2 * c + t, 2 * (c ^ ctx_mask) + (t ^ tp_mask)))
+        return lax.ppermute(value, ("ctx", "tp"), pairs)
+
+    other = across(hidden_in, 0, 1)
+    row_index = index * rows + jnp.arange(rows, dtype=jnp.int32)
+    tables = rotary_tables(row_index - first_of_prompt(row_index, starts))
+    results = project(
+        info, hidden_in, other, ln_gain[None, :], ln_bias[None, :], tables, w_qkv, splits
+    )
+    queries, pairs = results[:splits], results[splits : 2 * splits]
+    keys, values, page_head = results[2 * splits :]
+
+    kv_mine = [pairs[0]] + [None] * (splits - 1)
+    q_mine = [queries[0]] + [None] * (splits - 1)
+    for split in reversed(range(1, splits)):
+        kv_mine[split] = across(pairs[split], 2 * split)
+    for split in reversed(range(1, splits)):
+        q_mine[split] = across(queries[split], 2 * split)
+    q_tail = [lax.ppermute(queries[s], "ctx", [(group, 2 * s)]) for s in range(splits)]
+    kv_theirs = [across(kv_mine[split], 1) for split in range(splits)]
+
+    send_rows = w_out.shape[0] // 2
+    outgoing = lax.dynamic_slice(w_out, (core * send_rows, (1 - rank) * width), (send_rows, width))
+    outgoing, _ = lax.optimization_barrier((outgoing, other))
+    w_same = across(outgoing, 0, 1)
+    w_swap = across(w_same, 1)
+
+    scratch = [VMEM((group * rows, HD), jnp.bfloat16)] * 2
+    tile = 4 * rows * rows * HD
+    tail = on_core(
+        tail_kernel,
+        jax.ShapeDtypeStruct((rows, HD + LANES), jnp.bfloat16),
+        scratch,
+        "tail",
+        group * tile,
+    )(info, *q_tail, *kv_mine, *kv_theirs)
+    far = lax.ppermute(tail, "ctx", [(2 * s, group + 2 * s) for s in range(splits)])
+    attended = on_core(
+        main_kernel,
+        [jax.ShapeDtypeStruct((rows, HD), jnp.bfloat16)] * splits
+        + [
+            jax.ShapeDtypeStruct((rows, HD), jnp.float32),
+            jax.ShapeDtypeStruct((rows, LANES), jnp.float32),
+        ],
+        scratch + [VMEM((splits * rows, HD), jnp.bfloat16)] * 2,
+        "main",
+        splits * (splits + 1) * tile,
+    )(info, *q_mine, *kv_mine, *kv_theirs)
+    blocks, near_mixed, near_level = attended[:splits], attended[splits], attended[splits + 1][:, :1]
+    far_parts = far[:, HD : HD + 3].astype(jnp.float32)
+    far_level = far_parts[:, :1] + far_parts[:, 1:2] + far_parts[:, 2:3]
+    highest = jnp.maximum(near_level, far_level)
+    near_weight, far_weight = jnp.exp2(near_level - highest), jnp.exp2(far_level - highest)
+    merged = (near_mixed * near_weight + far[:, :HD].astype(jnp.float32) * far_weight) / (
+        near_weight + far_weight
+    )
+    crossing = (index >= group) & (core == 0)
+    applies = crossing & (jnp.arange(rows)[:, None] < starts[2] - group * rows)
+    blocks = [
+        jnp.where(applies & (place == s), merged.astype(jnp.bfloat16), blocks[s])
+        for s in range(splits)
+    ]
+
+    near = [blocks[0]] + [across(blocks[s], 2 * s) for s in range(1, splits)]
+    beyond = [across(blocks[s], 2 * s, 1) for s in range(splits)]
+    w_blocks = w_out.shape[0]
+    operands = [*near, *beyond]
+    attn_out = pl.pallas_call(
+        out_kernel,
+        grid_spec=pltpu.PrefetchScalarGridSpec(
+            num_scalar_prefetch=1,
+            grid=(1,),
+            in_specs=[pl.BlockSpec((rows, HD), lambda i, info: (0, 0))] * len(operands)
+            + [
+                pl.BlockSpec((w_blocks, width), lambda i, info: (0, info[1])),
+                pl.BlockSpec((send_rows, width), lambda i, info: (0, 0)),
+                pl.BlockSpec((send_rows, width), lambda i, info: (0, 0)),
+            ],
+            out_specs=pl.BlockSpec((rows, width), lambda i, info: (0, 0)),
+        ),
+        out_shape=jax.ShapeDtypeStruct((rows, width), jnp.bfloat16),
+        compiler_params=pltpu.CompilerParams(vmem_limit_bytes=40 * 2**20),
+        cost_estimate=pl.CostEstimate(
+            flops=2 * rows * 2 * width * width, bytes_accessed=8 * 2**20, transcendentals=0
+        ),
+        name="out",
+    )(info, *operands, w_out, w_same, w_swap)
+
+    next_head = lax.ppermute(page_head, "ctx", [(i, i - 1) for i in range(1, count)])
+    kv_cache = write_pages(keys, values, next_head, index, starts, page_table)
+    return attn_out, kv_cache
+
+
+def write_pages(keys, values, next_head, index, starts, page_table):
+    rows, features = keys.shape
+    slots = rows // PAGE + 3
+    token = index * rows + jnp.arange(rows + PAGE, dtype=jnp.int32)
+    exists = token < lax.axis_size("ctx") * rows
+    prompt = jnp.sum((starts[None, :] <= token[:, None]).astype(jnp.int32), axis=1) - 1
+    position = token - first_of_prompt(token, starts)
+    page, offset = position // PAGE, position % PAGE
+    owned = exists & ((token - offset) // rows == index)
+    pages = page_table.shape[1]
+    entry = jnp.take(page_table.reshape(-1), prompt * pages + jnp.clip(page, 0, pages - 1))
+    target = jnp.where(owned, entry % slots * PAGE + offset, -1)
+    placing = (jnp.arange(slots * PAGE, dtype=jnp.int32)[:, None] == target[None, :]).astype(
+        jnp.bfloat16
+    )
+    sources = jnp.stack(
+        [jnp.concatenate([keys, next_head[0]]), jnp.concatenate([values, next_head[1]])], axis=1
+    ).reshape(rows + PAGE, 2 * features)
+    written = jnp.dot(placing, sources, preferred_element_type=jnp.float32).astype(jnp.bfloat16)
+    return written.reshape(slots, PAGE, 2, features)
 
 
 def passed_along(value, axis, steps):
@@ -79,7 +460,7 @@
     )
 
 
-def per_device(hidden_in, ln_gain, ln_bias, w_qkv, w_out, segment_ids, prompt_lengths, page_table):
+def relay_pairs(hidden_in, ln_gain, ln_bias, w_qkv, w_out, segment_ids, prompt_lengths, page_table):
     token_rows = hidden_in.shape[0]
     model_width = w_out.shape[1]
     local_heads = w_out.shape[0] // HD
@@ -151,6 +532,12 @@
     return (attn_out, kv_cache)
 
 
+def per_device(*operands):
+    heads = operands[4].shape[0] // HD
+    spread = lax.axis_size("tp") == 2 and lax.axis_size("ctx") == 4 * heads
+    return (split_heads if spread else relay_pairs)(*operands)
+
+
 def solution(mesh):
     return jax.shard_map(
         per_device,

time: 296 us -> 130 us (0.44)
  the two profiles are of different devices: /device:TPU:16 before, /device:TPU:0 now
where the time goes in v1:
time: 130 us; the launch traced here: 129 us
  other arithmetic  41.7 us (32%)
  starting transfers between devices  34.8 us (27%)
  local copies, waits for them, and re-layouts  20.2 us (16%)
  Pallas kernels  20 us (15%)
  waiting for transfers between devices  6.04 us (5%)
  matrix products  4.47 us (3%)
  between operations  1.66 us (1%)
    select_n x1, other arithmetic, write_pages(): target = jnp.where(owned, entry % slots * PAGE + offset, -1)  27.7 us
    ppermute x20, starting transfers between devices, across(): return lax.ppermute(value, ('ctx', 'tp'), pairs)  27.1 us
    pallas_call x1, Pallas kernels, project(): pl.pallas_call(qkv_kernel, grid_spec=pltpu.PrefetchScalarGridSpec(num_sca...  9.73 us
    pallas_call x2, Pallas kernels, call(): pl.pallas_call(kernel, in_specs=[pl.BlockSpec(memory_space=pltpu.SMEM)] +...  7.55 us
    gather x2, other arithmetic, write_pages(): jnp.take(page_table.reshape(-1), prompt * pages + jnp.clip(page, 0, pages...  6.48 us
    unnamed x34, local copies, waits for them, and re-layouts  5.85 us
    reshape x1, local copies, waits for them, and re-layouts, write_pages(): return written.reshape(slots, PAGE, 2, features)  5.49 us
    ppermute x20, waiting for transfers between devices, across(): return lax.ppermute(value, ('ctx', 'tp'), pairs)  4.78 us
  transfers between devices with their start and end apart: 26, of which 2 were waited for; matrix products, arithmetic and copies ran while one was open for 47% of the time, Pallas kernels for 6%

profile of v1, /device:TPU:0, one launch (start us, length us, event | category | flops | bytes accessed | tf_op | source)
XLA Modules:
  0.0 128.9 jit_solution(13426415862405110784)
XLA Ops:
  0.7 3.0 %collective-permute-start = (bf16[256,1024]{1,0:T(8,128)(2,1)}, bf16[256,1024]{1,0:T(8,128)(2,1)S(1)}, u32[]{:S(2)}, u32[]{:S(2)}) collective-permute-start(bf16[256,1024]{1,0:T(8,128)(2,1)} %own.1), channel_id=1, source_target_pairs={{0,1},{1,0},{2,3},{3,2},{4,5},{5,4},{6,7},{7,6},{8,9},{9,8},{10,11... | collective-permute-start | bytes 1572872 | tf_op jit(solution)/shard_map/ppermute | solution.py:282
  7.3 1.8 %fusion.27 = f32[256]{0:T(256)S(1)} fusion(s32[]{:T(128)} %bitcast.11, s32[]{:T(128)} %bitcast.10, s32[]{:T(128)} %bitcast.7, s32[]{:T(128)S(6)} %mul.88), kind=kLoop, calls=%fused_computation.127 | loop fusion | flops 2304 | bytes 1040 | tf_op jit(solution)/shard_map/convert_element_type | solution.py:35
  9.2 6.3 %fusion.25 = (s32[384]{0:T(512)S(1)}, s32[384,1]{0,1:T(1,128)S(1)}) fusion(s32[]{:T(128)} %bitcast.53, s32[]{:T(128)} %bitcast.54, s32[]{:T(128)} %bitcast.55, s32[]{:T(128)} %bitcast.56, s32[]{:T(128)} %bitcast.57, s32[]{:T(128)} %bitcast.59, s32[]{:T(128)} %bitcast.58, s32[]{:T(128)} %bitcast.11, s32[]{:T(128)} %bitcast.10, s32[]{:T(128)} %bitcast.7, ...), kind=kLoop, calls=%fused_computation.125 | loop fusion | flops 15360 | bytes 4652 | tf_op jit(solution)/shard_map/jit(_take)/gather | solution.py:384
  16.5 9.7 %project.1 = (bf16[256,256]{1,0:T(8,128)(2,1)S(1)}, bf16[256,256]{1,0:T(8,128)(2,1)S(1)}, bf16[256,256]{1,0:T(8,128)(2,1)S(1)}, bf16[256,256]{1,0:T(8,128)(2,1)}...) custom-call(s32[8]{0:T(128)S(1)} %stack.32.info, ...), custom_call_target="tpu_custom_call" | custom-call | flops 3221225472 | bytes 12582912 | tf_op jit(solution)/shard_map/project/pallas_call | solution.py:107
  27.1 1.3 collective-permute-start.11
  32.0 1.6 %collective-permute-start.4 = (bf16[256,512]{1,0:T(8,128)(2,1)}, bf16[256,512]{1,0:T(8,128)(2,1)S(1)}, u32[]{:S(2)}, u32[]{:S(2)}) collective-permute-start(bf16[256,512]{1,0:T(8,128)(2,1)} %get-tuple-element.25), channel_id=1, source_target_pairs={{0,4},{1,5},{2,6},{3,7},{4,0},{5,1},{6,2},{7,3},{8,12},{9,13},{10,... | collective-permute-start | bytes 786440 | tf_op jit(solution)/shard_map/ppermute | solution.py:282
  33.6 1.3 collective-permute-done.11.refs_0_
  38.2 1.3 %collective-permute-start.25 = (bf16[2,128,1024]{2,1,0:T(8,128)(2,1)}, bf16[2,128,1024]{2,1,0:T(8,128)(2,1)}, u32[]{:S(2)}, u32[]{:S(2)}) collective-permute-start(bf16[2,128,1024]{2,1,0:T(8,128)(2,1)} %copy-done.10), channel_id=1, source_target_pairs={{2,0},{4,2},{6,4},{8,6},{10,8},{12,10},{14,12},{16,14},{18,16},{20... | collective-permute-start | bytes 1572872 | tf_op jit(solution)/shard_map/ppermute | solution.py:369
  39.5 27.7 %fusion.15 = s32[384]{0:T(512)S(1)} fusion(pred[384]{0:T(512)(128)(4,1)S(1)} %get-tuple-element.81, pred[384]{0:T(512)(128)(4,1)S(1)} %get-tuple-element.80, pred[384]{0:T(512)(128)(4,1)S(1)} %get-tuple-element.79, pred[384]{0:T(512)(128)(4,1)S(1)} %get-tuple-element.78, pred[384]{0:T(512)(128)(4,1)S(1)} %get-tuple-element.77, ...), kind=kLoop, calls=%fused_computation.105 | loop fusion | flops 41088 | bytes 20536 | tf_op jit(solution)/shard_map/jit(_where)/select_n | solution.py:385
  67.2 1.2 collective-permute-start.8
  68.9 1.4 %dynamic_slice.3 = bf16[512,1024]{1,0:T(8,128)(2,1)S(1)} dynamic-slice(bf16[1024,2048]{1,0:T(8,128)(2,1)} %refs_8_.1, s32[]{:T(128)S(6)} %select_n.208, s32[]{:T(128)S(6)} %select_n.209), dynamic_slice_sizes={512,1024} | dynamic-slice | bytes 2097156 | tf_op jit(solution)/shard_map/dynamic_slice | solution.py:303
  70.3 1.1 collective-permute-start.23
  71.4 3.2 %collective-permute-start.1 = (bf16[256,256]{1,0:T(8,128)(2,1)S(1)}, bf16[256,256]{1,0:T(8,128)(2,1)S(1)}, u32[]{:S(2)}, u32[]{:S(2)}) collective-permute-start(bf16[256,256]{1,0:T(8,128)(2,1)S(1)} %copy-done.16), channel_id=1, source_target_pairs={{0,4},{1,5},{2,6},{3,7},{4,0},{5,1},{6,2},{7,3},{8,12},{9,13},{10,... | collective-permute-start | bytes 393224 | tf_op jit(solution)/shard_map/ppermute | solution.py:282
  74.6 3.2 %collective-permute-start.2 = (bf16[256,256]{1,0:T(8,128)(2,1)S(1)}, bf16[256,256]{1,0:T(8,128)(2,1)S(1)}, u32[]{:S(2)}, u32[]{:S(2)}) collective-permute-start(bf16[256,256]{1,0:T(8,128)(2,1)S(1)} %copy-done.14), channel_id=1, source_target_pairs={{0,8},{1,9},{2,10},{3,11},{4,12},{5,13},{6,14},{7,15},{8,0},{9,1},... | collective-permute-start | bytes 393224 | tf_op jit(solution)/shard_map/ppermute | solution.py:282
  77.8 0.9 copy-done.7
  78.7 3.1 %tail.1 = bf16[256,384]{1,0:T(8,128)(2,1)S(1)} custom-call(s32[8]{0:T(128)S(1)} %stack.32.info, bf16[256,256]{1,0:T(8,128)(2,1)S(1)} %collective-permute-done.11.refs_0_, bf16[256,256]{1,0:T(8,128)(2,1)S(1)} %copy-done.3, bf16[256,256]{1,0:T(8,128)(2,1)S(1)} %copy-done.5, bf16[256,256]{1,0:T(8,128)(2,1)S(1)} %copy-done.7, ...), custom_call_target="tpu_custom_call" | custom-call | flops 536870912 | bytes 4194304 | tf_op jit(solution)/shard_map/tail/pallas_call | solution.py:231
  81.8 3.2 %collective-permute-start.15 = (bf16[256,384]{1,0:T(8,128)(2,1)S(1)}, bf16[256,384]{1,0:T(8,128)(2,1)S(1)}, u32[]{:S(2)}, u32[]{:S(2)}) collective-permute-start(bf16[256,384]{1,0:T(8,128)(2,1)S(1)} %tail.1), channel_id=1, source_target_pairs={{0,16},{4,20},{8,24},{12,28},{1,17},{5,21},{9,25},{13,29}} | collective-permute-start | bytes 589832 | tf_op jit(solution)/shard_map/ppermute | solution.py:317
  85.0 1.1 slice_bitcast_fusion.1
  86.2 4.5 %main.1 = (bf16[256,256]{1,0:T(8,128)(2,1)S(1)}, bf16[256,256]{1,0:T(8,128)(2,1)S(1)}, bf16[256,256]{1,0:T(8,128)(2,1)S(1)}, bf16[256,256]{1,0:T(8,128)(2,1)S(1)...) custom-call(s32[8]{0:T(128)S(1)} %stack.32.info, bf16[256,256]{1,0:T(8,128)(2,1)S(1)} %copy-done.12, ...), custom_call_target="tpu_custom_call" | custom-call | flops 1342177280 | bytes 4194304 | tf_op jit(solution)/shard_map/main/pallas_call | solution.py:231
  90.8 4.7 %collective-permute-done.23.refs_9_ = bf16[512,1024]{1,0:T(8,128)(2,1)S(1)} collective-permute-done((bf16[512,1024]{1,0:T(8,128)(2,1)S(1)}, bf16[512,1024]{1,0:T(8,128)(2,1)S(1)}, u32[]{:S(2)}, u32[]{:S(2)}) %collective-permute-start.23) | collective-permute-done | bytes 1048608 | tf_op jit(solution)/shard_map/ppermute | solution.py:282
  95.8 0.9 broadcast_select_fusion
  97.5 3.2 %collective-permute-start.16 = (bf16[256,256]{1,0:T(8,128)(2,1)}, bf16[256,256]{1,0:T(8,128)(2,1)S(1)}, u32[]{:S(2)}, u32[]{:S(2)}) collective-permute-start(bf16[256,256]{1,0:T(8,128)(2,1)} %get-tuple-element.93), channel_id=1, source_target_pairs={{0,4},{1,5},{2,6},{3,7},{4,0},{5,1},{6,2},{7,3},{8,12},{9,13},{10,... | collective-permute-start | bytes 393224 | tf_op jit(solution)/shard_map/ppermute | solution.py:282
  100.7 3.5 %collective-permute-start.17 = (bf16[256,256]{1,0:T(8,128)(2,1)}, bf16[256,256]{1,0:T(8,128)(2,1)S(1)}, u32[]{:S(2)}, u32[]{:S(2)}) collective-permute-start(bf16[256,256]{1,0:T(8,128)(2,1)} %get-tuple-element.92), channel_id=1, source_target_pairs={{0,8},{1,9},{2,10},{3,11},{4,12},{5,13},{6,14},{7,15},{8,0},{9,1},... | collective-permute-start | bytes 393224 | tf_op jit(solution)/shard_map/ppermute | solution.py:282
  104.2 1.3 pad_maximum_fusion
  105.5 2.6 %copy.10 = bf16[384,2,1024]{0,2,1:T(8,128)(2,1)} copy(bf16[384,2,1024]{2,0,1:T(8,128)(2,1)} %pad_maximum_fusion) | data formatting | bytes 3145728 | tf_op jit(solution)/shard_map/stack | solution.py:389
  108.1 1.9 %collective-permute-start.20 = (bf16[256,256]{1,0:T(8,128)(2,1)}, bf16[256,256]{1,0:T(8,128)(2,1)S(1)}, u32[]{:S(2)}, u32[]{:S(2)}) collective-permute-start(bf16[256,256]{1,0:T(8,128)(2,1)} %get-tuple-element.93), channel_id=1, source_target_pairs={{0,5},{1,4},{2,7},{3,6},{4,1},{5,0},{6,3},{7,2},{8,13},{9,12},{10,... | collective-permute-start | bytes 393224 | tf_op jit(solution)/shard_map/ppermute | solution.py:282
  110.0 2.5 %collective-permute-start.21 = (bf16[256,256]{1,0:T(8,128)(2,1)}, bf16[256,256]{1,0:T(8,128)(2,1)S(1)}, u32[]{:S(2)}, u32[]{:S(2)}) collective-permute-start(bf16[256,256]{1,0:T(8,128)(2,1)} %get-tuple-element.92), channel_id=1, source_target_pairs={{0,9},{1,8},{2,11},{3,10},{4,13},{5,12},{6,15},{7,14},{8,1},{9,0},... | collective-permute-start | bytes 393224 | tf_op jit(solution)/shard_map/ppermute | solution.py:282
  113.0 1.0 collective-permute-start.19
  114.0 4.5 %convolution_convert_fusion = bf16[640,2048]{1,0:T(8,128)(2,1)} fusion(bf16[384,2048]{0,1:T(8,128)(2,1)} %bitcast.73, s32[384]{0:T(512)S(1)} %fusion.15), kind=kOutput, calls=%fused_computation | convolution fusion | flops 1008189440 | bytes 4195840 | tf_op jit(solution)/shard_map/dot_general | solution.py:392
  118.4 5.5 %reshape.272 = bf16[5,128,2,1024]{3,2,1,0:T(2,128)(2,1)} reshape(bf16[640,2048]{1,0:T(8,128)(2,1)} %convolution_convert_fusion) | data formatting | bytes 5242880 | tf_op jit(solution)/shard_map/reshape | solution.py:393
  124.0 2.2 %copy-done = bf16[1024,2048]{1,0:T(8,128)(2,1)S(1)} copy-done((bf16[1024,2048]{1,0:T(8,128)(2,1)S(1)}, bf16[1024,2048]{1,0:T(8,128)(2,1)}, u32[]{:S(2)}) %copy-start) | copy-done | bytes 4194328
  126.1 2.7 %out.1 = bf16[256,1024]{1,0:T(8,128)(2,1)} custom-call(s32[8]{0:T(128)S(1)} %stack.32.info, bf16[256,256]{1,0:T(8,128)(2,1)S(1)} %get-tuple-element.94.refs_0_, bf16[256,256]{1,0:T(8,128)(2,1)S(1)} %collective-permute-done.16.refs_1_, bf16[256,256]{1,0:T(8,128)(2,1)S(1)} %collective-permute-done.17.refs_2_, ...), custom_call_target="tpu_custom_call" | custom-call | flops 1073741824 | bytes 8388608 | tf_op jit(solution)/shard_map/out/pallas_call | solution.py:348
  (95 shorter events, 14.1 us)
Async XLA Ops:
  0.6 15.9 %copy-start.1 = (bf16[256,1024]{1,0:T(8,128)(2,1)S(1)}, bf16[256,1024]{1,0:T(8,128)(2,1)}, u32[]{:S(2)}) copy-start(bf16[256,1024]{1,0:T(8,128)(2,1)} %own.1) | copy-start | bytes 1572868
  0.6 15.9 %copy-start.8 = (f32[2048]{0:T(1024)S(1)}, f32[2048]{0:T(1024)}, u32[]{:S(2)}) copy-start(f32[2048]{0:T(1024)} %param.9) | copy-start | bytes 24580
  0.6 15.9 %copy-start.9 = (f32[2048]{0:T(1024)S(1)}, f32[2048]{0:T(1024)}, u32[]{:S(2)}) copy-start(f32[2048]{0:T(1024)} %param.10) | copy-start | bytes 24580
  0.7 15.8 %collective-permute-start = (bf16[256,1024]{1,0:T(8,128)(2,1)}, bf16[256,1024]{1,0:T(8,128)(2,1)S(1)}, u32[]{:S(2)}, u32[]{:S(2)}) collective-permute-start(bf16[256,1024]{1,0:T(8,128)(2,1)} %own.1), channel_id=1, source_target_pairs={{0,1},{1,0},{2,3},{3,2},{4,5},{5,4},{6,7},{7,6},{8,9},{9,8},{10,11... | collective-permute-start | bytes 1572872 | tf_op jit(solution)/shard_map/ppermute | solution.py:282
  27.1 10.4 %copy-start.13 = (bf16[256,256]{1,0:T(8,128)(2,1)}, bf16[256,256]{1,0:T(8,128)(2,1)S(1)}, u32[]{:S(2)}) copy-start(bf16[256,256]{1,0:T(8,128)(2,1)S(1)} %get-tuple-element.22) | copy-start | bytes 393220
  27.1 7.7 %collective-permute-start.11 = (bf16[256,256]{1,0:T(8,128)(2,1)S(1)}, bf16[256,256]{1,0:T(8,128)(2,1)S(1)}, u32[]{:S(2)}, u32[]{:S(2)}) collective-permute-start(bf16[256,256]{1,0:T(8,128)(2,1)S(1)} %get-tuple-element.20.refs_0_), channel_id=1, source_target_pairs={{16,0},{17,1}} | collective-permute-start | bytes 393224 | tf_op jit(solution)/shard_map/ppermute | solution.py:299
  29.0 6.1 %collective-permute-start.12 = (bf16[256,256]{1,0:T(8,128)(2,1)S(1)}, bf16[256,256]{1,0:T(8,128)(2,1)S(1)}, u32[]{:S(2)}, u32[]{:S(2)}) collective-permute-start(bf16[256,256]{1,0:T(8,128)(2,1)S(1)} %get-tuple-element.21), channel_id=1, source_target_pairs={{16,4},{17,5}} | collective-permute-start | bytes 393224 | tf_op jit(solution)/shard_map/ppermute | solution.py:299
  29.9 7.6 %collective-permute-start.13 = (bf16[256,256]{1,0:T(8,128)(2,1)S(1)}, bf16[256,256]{1,0:T(8,128)(2,1)S(1)}, u32[]{:S(2)}, u32[]{:S(2)}) collective-permute-start(bf16[256,256]{1,0:T(8,128)(2,1)S(1)} %get-tuple-element.22), channel_id=1, source_target_pairs={{16,8},{17,9}} | collective-permute-start | bytes 393224 | tf_op jit(solution)/shard_map/ppermute | solution.py:299
  30.6 7.6 %collective-permute-start.14 = (bf16[256,256]{1,0:T(8,128)(2,1)}, bf16[256,256]{1,0:T(8,128)(2,1)S(1)}, u32[]{:S(2)}, u32[]{:S(2)}) collective-permute-start(bf16[256,256]{1,0:T(8,128)(2,1)} %get-tuple-element.23), channel_id=1, source_target_pairs={{16,12},{17,13}} | collective-permute-start | bytes 393224 | tf_op jit(solution)/shard_map/ppermute | solution.py:299
  32.0 35.2 %collective-permute-start.4 = (bf16[256,512]{1,0:T(8,128)(2,1)}, bf16[256,512]{1,0:T(8,128)(2,1)S(1)}, u32[]{:S(2)}, u32[]{:S(2)}) collective-permute-start(bf16[256,512]{1,0:T(8,128)(2,1)} %get-tuple-element.25), channel_id=1, source_target_pairs={{0,4},{1,5},{2,6},{3,7},{4,0},{5,1},{6,2},{7,3},{8,12},{9,13},{10,... | collective-permute-start | bytes 786440 | tf_op jit(solution)/shard_map/ppermute | solution.py:282
  34.8 33.6 %collective-permute-start.5 = (bf16[256,512]{1,0:T(8,128)(2,1)}, bf16[256,512]{1,0:T(8,128)(2,1)S(1)}, u32[]{:S(2)}, u32[]{:S(2)}) collective-permute-start(bf16[256,512]{1,0:T(8,128)(2,1)} %get-tuple-element.26), channel_id=1, source_target_pairs={{0,8},{1,9},{2,10},{3,11},{4,12},{5,13},{6,14},{7,15},{8,0},{9,1},... | collective-permute-start | bytes 786440 | tf_op jit(solution)/shard_map/ppermute | solution.py:282
  35.8 32.7 %collective-permute-start.6 = (bf16[256,512]{1,0:T(8,128)(2,1)}, bf16[256,512]{1,0:T(8,128)(2,1)S(1)}, u32[]{:S(2)}, u32[]{:S(2)}) collective-permute-start(bf16[256,512]{1,0:T(8,128)(2,1)} %get-tuple-element.27), channel_id=1, source_target_pairs={{0,12},{1,13},{2,14},{3,15},{4,8},{5,9},{6,10},{7,11},{8,4},{9,5},... | collective-permute-start | bytes 786440 | tf_op jit(solution)/shard_map/ppermute | solution.py:282
  38.2 32.1 %collective-permute-start.7 = (bf16[256,512]{1,0:T(8,128)(2,1)S(1)}, bf16[256,512]{1,0:T(8,128)(2,1)S(1)}, u32[]{:S(2)}, u32[]{:S(2)}) collective-permute-start(bf16[256,512]{1,0:T(8,128)(2,1)S(1)} %get-tuple-element.24.refs_4_), channel_id=1, source_target_pairs={{0,2},{1,3},{2,0},{3,1},{4,6},{5,7},{6,4},{7,5},{8,10},{9,11},{10,... | collective-permute-start | bytes 786440 | tf_op jit(solution)/shard_map/ppermute | solution.py:282
  38.2 32.1 %copy-start.6 = (bf16[256,256]{1,0:T(8,128)(2,1)}, bf16[256,256]{1,0:T(8,128)(2,1)S(1)}, u32[]{:S(2)}) copy-start(bf16[256,256]{1,0:T(8,128)(2,1)S(1)} %collective-permute-done.14.refs_3_) | copy-start | bytes 393220
  38.2 43.7 %collective-permute-start.25 = (bf16[2,128,1024]{2,1,0:T(8,128)(2,1)}, bf16[2,128,1024]{2,1,0:T(8,128)(2,1)}, u32[]{:S(2)}, u32[]{:S(2)}) collective-permute-start(bf16[2,128,1024]{2,1,0:T(8,128)(2,1)} %copy-done.10), channel_id=1, source_target_pairs={{2,0},{4,2},{6,4},{8,6},{10,8},{12,10},{14,12},{16,14},{18,16},{20... | collective-permute-start | bytes 1572872 | tf_op jit(solution)/shard_map/ppermute | solution.py:369
  67.2 4.2 %collective-permute-start.8 = (bf16[256,512]{1,0:T(8,128)(2,1)S(1)}, bf16[256,512]{1,0:T(8,128)(2,1)}, u32[]{:S(2)}, u32[]{:S(2)}) collective-permute-start(bf16[256,512]{1,0:T(8,128)(2,1)S(1)} %collective-permute-done.4.refs_5_), channel_id=1, source_target_pairs={{0,2},{1,3},{2,0},{3,1},{4,6},{5,7},{6,4},{7,5},{8,10},{9,11},{10,... | collective-permute-start | bytes 786440 | tf_op jit(solution)/shard_map/ppermute | solution.py:282
  68.4 6.3 %collective-permute-start.9 = (bf16[256,512]{1,0:T(8,128)(2,1)S(1)}, bf16[256,512]{1,0:T(8,128)(2,1)}, u32[]{:S(2)}, u32[]{:S(2)}) collective-permute-start(bf16[256,512]{1,0:T(8,128)(2,1)S(1)} %collective-permute-done.5.refs_6_), channel_id=1, source_target_pairs={{0,2},{1,3},{2,0},{3,1},{4,6},{5,7},{6,4},{7,5},{8,10},{9,11},{10,... | collective-permute-start | bytes 786440 | tf_op jit(solution)/shard_map/ppermute | solution.py:282
  68.4 9.4 %collective-permute-start.10 = (bf16[256,512]{1,0:T(8,128)(2,1)S(1)}, bf16[256,512]{1,0:T(8,128)(2,1)}, u32[]{:S(2)}, u32[]{:S(2)}) collective-permute-start(bf16[256,512]{1,0:T(8,128)(2,1)S(1)} %collective-permute-done.6.refs_7_), channel_id=1, source_target_pairs={{0,2},{1,3},{2,0},{3,1},{4,6},{5,7},{6,4},{7,5},{8,10},{9,11},{10,... | collective-permute-start | bytes 786440 | tf_op jit(solution)/shard_map/ppermute | solution.py:282
  68.9 8.9 %copy-start.3 = (bf16[256,256]{1,0:T(8,128)(2,1)S(1)}, bf16[256,256]{1,0:T(8,128)(2,1)}, u32[]{:S(2)}) copy-start(bf16[256,256]{1,0:T(8,128)(2,1)} %copy-done.2) | copy-start | bytes 393220
  70.3 25.2 %collective-permute-start.23 = (bf16[512,1024]{1,0:T(8,128)(2,1)S(1)}, bf16[512,1024]{1,0:T(8,128)(2,1)S(1)}, u32[]{:S(2)}, u32[]{:S(2)}) collective-permute-start(bf16[512,1024]{1,0:T(8,128)(2,1)S(1)} %dynamic_slice.3), channel_id=1, source_target_pairs={{0,1},{1,0},{2,3},{3,2},{4,5},{5,4},{6,7},{7,6},{8,9},{9,8},{10,11... | collective-permute-start | bytes 3145736 | tf_op jit(solution)/shard_map/ppermute | solution.py:282
  71.4 14.7 %collective-permute-start.1 = (bf16[256,256]{1,0:T(8,128)(2,1)S(1)}, bf16[256,256]{1,0:T(8,128)(2,1)S(1)}, u32[]{:S(2)}, u32[]{:S(2)}) collective-permute-start(bf16[256,256]{1,0:T(8,128)(2,1)S(1)} %copy-done.16), channel_id=1, source_target_pairs={{0,4},{1,5},{2,6},{3,7},{4,0},{5,1},{6,2},{7,3},{8,12},{9,13},{10,... | collective-permute-start | bytes 393224 | tf_op jit(solution)/shard_map/ppermute | solution.py:282
  74.6 11.5 %collective-permute-start.2 = (bf16[256,256]{1,0:T(8,128)(2,1)S(1)}, bf16[256,256]{1,0:T(8,128)(2,1)S(1)}, u32[]{:S(2)}, u32[]{:S(2)}) collective-permute-start(bf16[256,256]{1,0:T(8,128)(2,1)S(1)} %copy-done.14), channel_id=1, source_target_pairs={{0,8},{1,9},{2,10},{3,11},{4,12},{5,13},{6,14},{7,15},{8,0},{9,1},... | collective-permute-start | bytes 393224 | tf_op jit(solution)/shard_map/ppermute | solution.py:282
  77.8 8.4 %collective-permute-start.3 = (bf16[256,256]{1,0:T(8,128)(2,1)}, bf16[256,256]{1,0:T(8,128)(2,1)S(1)}, u32[]{:S(2)}, u32[]{:S(2)}) collective-permute-start(bf16[256,256]{1,0:T(8,128)(2,1)} %get-tuple-element.23), channel_id=1, source_target_pairs={{0,12},{1,13},{2,14},{3,15},{4,8},{5,9},{6,10},{7,11},{8,4},{9,5},... | collective-permute-start | bytes 393224 | tf_op jit(solution)/shard_map/ppermute | solution.py:282
  81.8 8.9 %collective-permute-start.15 = (bf16[256,384]{1,0:T(8,128)(2,1)S(1)}, bf16[256,384]{1,0:T(8,128)(2,1)S(1)}, u32[]{:S(2)}, u32[]{:S(2)}) collective-permute-start(bf16[256,384]{1,0:T(8,128)(2,1)S(1)} %tail.1), channel_id=1, source_target_pairs={{0,16},{4,20},{8,24},{12,28},{1,17},{5,21},{9,25},{13,29}} | collective-permute-start | bytes 589832 | tf_op jit(solution)/shard_map/ppermute | solution.py:317
  95.5 28.4 %collective-permute-start.24 = (bf16[512,1024]{1,0:T(8,128)(2,1)S(1)}, bf16[512,1024]{1,0:T(8,128)(2,1)S(1)}, u32[]{:S(2)}, u32[]{:S(2)}) collective-permute-start(bf16[512,1024]{1,0:T(8,128)(2,1)S(1)} %collective-permute-done.23.refs_9_), channel_id=1, source_target_pairs={{0,2},{1,3},{2,0},{3,1},{4,6},{5,7},{6,4},{7,5},{8,10},{9,11},{10,... | collective-permute-start | bytes 3145736 | tf_op jit(solution)/shard_map/ppermute | solution.py:282
  97.5 12.5 %collective-permute-start.16 = (bf16[256,256]{1,0:T(8,128)(2,1)}, bf16[256,256]{1,0:T(8,128)(2,1)S(1)}, u32[]{:S(2)}, u32[]{:S(2)}) collective-permute-start(bf16[256,256]{1,0:T(8,128)(2,1)} %get-tuple-element.93), channel_id=1, source_target_pairs={{0,4},{1,5},{2,6},{3,7},{4,0},{5,1},{6,2},{7,3},{8,12},{9,13},{10,... | collective-permute-start | bytes 393224 | tf_op jit(solution)/shard_map/ppermute | solution.py:282
  100.7 11.8 %collective-permute-start.17 = (bf16[256,256]{1,0:T(8,128)(2,1)}, bf16[256,256]{1,0:T(8,128)(2,1)S(1)}, u32[]{:S(2)}, u32[]{:S(2)}) collective-permute-start(bf16[256,256]{1,0:T(8,128)(2,1)} %get-tuple-element.92), channel_id=1, source_target_pairs={{0,8},{1,9},{2,10},{3,11},{4,12},{5,13},{6,14},{7,15},{8,0},{9,1},... | collective-permute-start | bytes 393224 | tf_op jit(solution)/shard_map/ppermute | solution.py:282
  104.2 8.7 %collective-permute-start.18 = (bf16[256,256]{1,0:T(8,128)(2,1)}, bf16[256,256]{1,0:T(8,128)(2,1)S(1)}, u32[]{:S(2)}, u32[]{:S(2)}) collective-permute-start(bf16[256,256]{1,0:T(8,128)(2,1)} %get-tuple-element.84), channel_id=1, source_target_pairs={{0,12},{1,13},{2,14},{3,15},{4,8},{5,9},{6,10},{7,11},{8,4},{9,5},... | collective-permute-start | bytes 393224 | tf_op jit(solution)/shard_map/ppermute | solution.py:282
  108.1 15.8 %collective-permute-start.20 = (bf16[256,256]{1,0:T(8,128)(2,1)}, bf16[256,256]{1,0:T(8,128)(2,1)S(1)}, u32[]{:S(2)}, u32[]{:S(2)}) collective-permute-start(bf16[256,256]{1,0:T(8,128)(2,1)} %get-tuple-element.93), channel_id=1, source_target_pairs={{0,5},{1,4},{2,7},{3,6},{4,1},{5,0},{6,3},{7,2},{8,13},{9,12},{10,... | collective-permute-start | bytes 393224 | tf_op jit(solution)/shard_map/ppermute | solution.py:282
  110.0 13.9 %collective-permute-start.21 = (bf16[256,256]{1,0:T(8,128)(2,1)}, bf16[256,256]{1,0:T(8,128)(2,1)S(1)}, u32[]{:S(2)}, u32[]{:S(2)}) collective-permute-start(bf16[256,256]{1,0:T(8,128)(2,1)} %get-tuple-element.92), channel_id=1, source_target_pairs={{0,9},{1,8},{2,11},{3,10},{4,13},{5,12},{6,15},{7,14},{8,1},{9,0},... | collective-permute-start | bytes 393224 | tf_op jit(solution)/shard_map/ppermute | solution.py:282
  112.5 11.4 %collective-permute-start.22 = (bf16[256,256]{1,0:T(8,128)(2,1)}, bf16[256,256]{1,0:T(8,128)(2,1)S(1)}, u32[]{:S(2)}, u32[]{:S(2)}) collective-permute-start(bf16[256,256]{1,0:T(8,128)(2,1)} %get-tuple-element.84), channel_id=1, source_target_pairs={{0,13},{1,12},{2,15},{3,14},{4,9},{5,8},{6,11},{7,10},{8,5},{9,4},... | collective-permute-start | bytes 393224 | tf_op jit(solution)/shard_map/ppermute | solution.py:282
  113.0 11.0 %collective-permute-start.19 = (bf16[256,256]{1,0:T(8,128)(2,1)S(1)}, bf16[256,256]{1,0:T(8,128)(2,1)S(1)}, u32[]{:S(2)}, u32[]{:S(2)}) collective-permute-start(bf16[256,256]{1,0:T(8,128)(2,1)S(1)} %get-tuple-element.94.refs_0_), channel_id=1, source_target_pairs={{0,1},{1,0},{2,3},{3,2},{4,5},{5,4},{6,7},{7,6},{8,9},{9,8},{10,11... | collective-permute-start | bytes 393224 | tf_op jit(solution)/shard_map/ppermute | solution.py:282
  (11 other events, 35.5 us)

commit v2 on v0

--- a/solution.py
+++ b/solution.py
@@ -1,15 +1,560 @@
+import functools
 import math
 
 import jax
 import jax.numpy as jnp
 from jax import lax
+from jax.experimental import pallas as pl
+from jax.experimental.pallas import tpu as pltpu
 from jax.sharding import PartitionSpec as P
 
 HD = 256
 PAGE = 128
-
-
 EPSILON = 1e-05
+ROT = HD // 4
+LANES = 128
+VMEM = pltpu.VMEM
+MASKED = -1e30
+LOG2E = 1.4426950408889634
+
+
+def cost(microseconds):
+    return pl.CostEstimate(flops=int(microseconds * 0.35e9), bytes_accessed=0, transcendentals=0)
+
+
+def row_bounds(info, rows):
+    first = jnp.zeros_like(rows)
+    for prompt in range(3, 6):
+        first = jnp.where(rows >= info[prompt], info[prompt], first)
+    return first
+
+
+def load_kernel(
+    splits,
+    lengths,
+    own,
+    gain,
+    bias,
+    inverse,
+    w_qkv,
+    w_out,
+    info,
+    own_here,
+    gain_here,
+    bias_here,
+    keep,
+    below,
+    above,
+    weights,
+    own_columns,
+    outgoing,
+    sems,
+):
+    index, rank = lax.axis_index("ctx"), lax.axis_index("tp")
+    core = lax.rem(index, 2)
+    rows, width = own_here.shape
+    send_rows = outgoing.shape[0]
+
+    def columns(place):
+        return pl.ds(pl.multiple_of(place * width, width), width)
+
+    sent = pl.ds(pl.multiple_of(core * send_rows, send_rows), send_rows)
+    pieces = (
+        (own, own_here),
+        (gain, gain_here),
+        (bias, bias_here),
+        (w_qkv, weights),
+        (w_out.at[sent, columns(1 - rank)], outgoing),
+        (w_out.at[:, columns(rank)], own_columns),
+    )
+    copies = [pltpu.make_async_copy(*piece, sems.at[i]) for i, piece in enumerate(pieces)]
+    for copy in copies:
+        copy.start()
+    info[0] = lax.rem(index // 2, splits)
+    info[1] = rank
+    info[2] = core
+    info[3] = 0
+    info[4] = lengths[0]
+    info[5] = lengths[0] + lengths[1]
+    info[6] = index // (2 * splits) * (2 * splits * rows)
+    info[7] = index
+    row = index * rows + lax.broadcasted_iota(jnp.int32, (rows, 1), 0)
+    position = (row - row_bounds(info, row)).astype(jnp.float32)
+    angles = position * inverse[...]
+    cosine, sine = jnp.cos(angles), jnp.sin(angles)
+    lane = lax.broadcasted_iota(jnp.int32, cosine.shape, 1)
+    keep[...] = jnp.where(lane < ROT, cosine, 1.0)
+    below[...] = jnp.where((lane >= ROT // 2) & (lane < ROT), sine, 0.0)
+    above[...] = jnp.where(lane < ROT // 2, -sine, 0.0)
+    for copy in copies:
+        copy.wait()
+
+
+def load(splits, lengths, own, gain, bias, w_qkv, w_out):
+    rows, width = own.shape
+    exponent = jnp.arange(0, ROT, 2).astype(jnp.float32) / ROT
+    inverse = jnp.power(jnp.float32(10000.0), -exponent)
+    inverse = jnp.tile(inverse, LANES // (ROT // 2))[None, :]
+    smem, here = pl.BlockSpec(memory_space=pltpu.SMEM), pl.BlockSpec(memory_space=pltpu.VMEM)
+    table = jax.ShapeDtypeStruct((rows, LANES), jnp.float32)
+    wide = jax.ShapeDtypeStruct(gain.shape, jnp.float32)
+    narrow = lambda *shape: jax.ShapeDtypeStruct(shape, jnp.bfloat16)
+    return pl.pallas_call(
+        functools.partial(load_kernel, splits),
+        in_specs=[smem] + [pl.BlockSpec(memory_space=pltpu.HBM)] * 3 + [here]
+        + [pl.BlockSpec(memory_space=pltpu.HBM)] * 2,
+        out_specs=[smem] + [here] * 9,
+        out_shape=[
+            jax.ShapeDtypeStruct((8,), jnp.int32),
+            narrow(rows, width),
+            wide,
+            wide,
+            table,
+            table,
+            table,
+            narrow(*w_qkv.shape),
+            narrow(w_out.shape[0], width),
+            narrow(w_out.shape[0] // 2, width),
+        ],
+        scratch_shapes=[pltpu.SemaphoreType.DMA((6,))],
+        compiler_params=pltpu.CompilerParams(vmem_limit_bytes=24 * 2**20),
+        cost_estimate=cost(6),
+        name="load",
+    )(lengths, own, gain, bias, inverse, w_qkv, w_out)
+
+
+def normed_rows(info, own, other, gain, bias, normed):
+    width = own.shape[1]
+    full = 2 * width
+    mine = own[...].astype(jnp.float32)
+    theirs = other[...].astype(jnp.float32)
+    total = jnp.sum(mine, axis=-1, keepdims=True) + jnp.sum(theirs, axis=-1, keepdims=True)
+    average = total / full
+    mine, theirs = mine - average, theirs - average
+    spread = jnp.sum(mine * mine, axis=-1, keepdims=True) + jnp.sum(
+        theirs * theirs, axis=-1, keepdims=True
+    )
+    scale = lax.rsqrt(spread / full + EPSILON)
+    for part, place in ((mine, info[1]), (theirs, 1 - info[1])):
+        columns = pl.ds(pl.multiple_of(place * width, width), width)
+        normed[:, columns] = (part * scale * gain[:, columns] + bias[:, columns]).astype(
+            jnp.bfloat16
+        )
+
+
+def project_head(info, split, normed, keep, below, above, weights, query_ref, pair_ref):
+    head = pl.ds(pl.multiple_of((info[0] ^ split) * HD, HD), HD)
+    rows = normed[...]
+
+    def turned(inputs):
+        leading = inputs[:, :LANES]
+        leading = (
+            leading * keep[...]
+            + pltpu.roll(leading, ROT // 2, 1) * below[...]
+            + pltpu.roll(leading, LANES - ROT // 2, 1) * above[...]
+        )
+        return jnp.concatenate([leading, inputs[:, LANES:]], axis=1).astype(jnp.bfloat16)
+
+    def product(j):
+        return jnp.dot(rows, weights[j, :, head], preferred_element_type=jnp.float32)
+
+    pair_ref[:, :HD] = turned(product(1))
+    pair_ref[:, HD:] = product(2).astype(jnp.bfloat16)
+    query_ref[...] = turned(product(0))
+
+
+def first_kernel(
+    split, info, own, other, gain, bias, keep, below, above, weights, query, pair, normed
+):
+    normed_rows(info, own, other, gain, bias, normed)
+    project_head(info, split, normed, keep, below, above, weights, query, pair)
+
+
+def next_kernel(split, info, normed, keep, below, above, weights, query, pair):
+    project_head(info, split, normed, keep, below, above, weights, query, pair)
+
+
+def project(info, split, inputs, tables, weights, rows, features):
+    is_first = len(inputs) > 1
+    here = pl.BlockSpec(memory_space=pltpu.VMEM)
+    return pl.pallas_call(
+        functools.partial(first_kernel if is_first else next_kernel, split),
+        in_specs=[pl.BlockSpec(memory_space=pltpu.SMEM)]
+        + [here] * (len(inputs) + len(tables) + 1),
+        out_specs=[here] * (2 + is_first),
+        out_shape=[
+            jax.ShapeDtypeStruct((rows, HD), jnp.bfloat16),
+            jax.ShapeDtypeStruct((rows, 2 * HD), jnp.bfloat16),
+        ]
+        + [jax.ShapeDtypeStruct((rows, features), jnp.bfloat16)] * is_first,
+        compiler_params=pltpu.CompilerParams(vmem_limit_bytes=24 * 2**20),
+        cost_estimate=cost(2.7 if is_first else 1.7),
+        name="project",
+    )(info, *inputs, *tables, weights)
+
+
+def soft_attend(query, keys, values, first_key, last_key, base):
+    scores = lax.dot_general(
+        query, keys, (((1,), (1,)), ((), ())), preferred_element_type=jnp.float32
+    )
+    column = base + lax.broadcasted_iota(jnp.int32, scores.shape, 1)
+    visible = (column >= first_key) & (column <= last_key)
+    scores = jnp.where(visible, scores, MASKED)
+    peak = jnp.max(scores, axis=-1, keepdims=True)
+    factor = LOG2E / math.sqrt(HD)
+    weights = jnp.exp2((scores - peak) * factor).astype(jnp.bfloat16)
+    total = jnp.sum(weights.astype(jnp.float32), axis=-1, keepdims=True)
+    mixed = jnp.dot(weights, values, preferred_element_type=jnp.float32) / total
+    return mixed, peak * factor + jnp.log2(total)
+
+
+def fetch_pairs(info, mine, theirs, pairs, sems):
+    rows = mine[0].shape[0]
+    copies = []
+    for refs, core in ((mine, info[2]), (theirs, 1 - info[2])):
+        for split, ref in enumerate(refs):
+            at = pl.ds(pl.multiple_of((2 * (info[0] ^ split) + core) * rows, rows), rows)
+            copies.append(pltpu.make_async_copy(ref, pairs.at[at, :], sems.at[len(copies)]))
+    for copy in copies:
+        copy.start()
+    return copies
+
+
+def tail_kernel(info, *refs):
+    splits = (len(refs) - 4) // 2
+    query, mine, theirs = refs[0], refs[1 : splits + 1], refs[splits + 1 : 2 * splits + 1]
+    out, pairs, sems = refs[2 * splits + 1 :]
+    rows = out.shape[0]
+
+    @pl.when((info[6] == 0) & (info[2] == 0))
+    def _():
+        copies = fetch_pairs(info, mine, theirs, pairs, sems)
+        for copy in copies:
+            copy.wait()
+        group_rows = 2 * splits * rows
+        row = group_rows + lax.broadcasted_iota(jnp.int32, (rows, 1), 0)
+        first = row_bounds(info, row)
+        mixed, level = soft_attend(query[...], pairs[:, :HD], pairs[:, HD:], first, row, 0)
+        level = jnp.where(first < group_rows, level, MASKED)
+        out[:, :HD] = mixed.astype(jnp.bfloat16)
+        lane = lax.broadcasted_iota(jnp.int32, (rows, LANES), 1)
+        high = level.astype(jnp.bfloat16).astype(jnp.float32)
+        middle = (level - high).astype(jnp.bfloat16).astype(jnp.float32)
+        low = level - high - middle
+        out[:, HD:] = jnp.where(
+            lane == 0, high, jnp.where(lane == 1, middle, jnp.where(lane == 2, low, 0.0))
+        ).astype(jnp.bfloat16)
+
+
+def main_kernel(info, *refs):
+    splits = (len(refs) - 6) // 3
+    queries, mine, theirs = refs[:splits], refs[splits : 2 * splits], refs[2 * splits : 3 * splits]
+    gathered, near_mixed, near_level, pairs, asked, sems = refs[3 * splits :]
+    rows = near_mixed.shape[0]
+    copies = fetch_pairs(info, mine, theirs, pairs, sems)
+    for split in range(splits):
+        at = pl.ds(pl.multiple_of((info[0] ^ split) * rows, rows), rows)
+        copies.append(
+            pltpu.make_async_copy(queries[split], asked.at[at, :], sems.at[len(copies)])
+        )
+        copies[-1].start()
+    for copy in copies:
+        copy.wait()
+    for place in range(splits):
+        reach = (2 * place + 2) * rows
+        row = info[6] + (2 * place + info[2]) * rows + lax.broadcasted_iota(jnp.int32, (rows, 1), 0)
+        here = slice(place * rows, (place + 1) * rows)
+        mixed, level = soft_attend(
+            asked[here, :],
+            pairs[:reach, :HD],
+            pairs[:reach, HD:],
+            row_bounds(info, row),
+            row,
+            info[6],
+        )
+        gathered[here, :] = mixed.astype(jnp.bfloat16)
+        if place == 0:
+            near_mixed[...] = mixed
+            near_level[...] = jnp.broadcast_to(level, near_level.shape)
+
+
+def merge_kernel(info, gathered, near_mixed, near_level, far, *outs):
+    rows = near_mixed.shape[0]
+    group_rows = 2 * len(outs) * rows
+    for split, out in enumerate(outs):
+        out[...] = gathered[pl.ds(pl.multiple_of((info[0] ^ split) * rows, rows), rows), :]
+
+    @pl.when((info[6] > 0) & (info[2] == 0))
+    def _():
+        parts = far[:, HD:].astype(jnp.float32)
+        far_level = parts[:, :1] + parts[:, 1:2] + parts[:, 2:3]
+        level = near_level[:, :1]
+        highest = jnp.maximum(level, far_level)
+        near_weight, far_weight = jnp.exp2(level - highest), jnp.exp2(far_level - highest)
+        mixed = near_mixed[...] * near_weight + far[:, :HD].astype(jnp.float32) * far_weight
+        mixed = mixed / (near_weight + far_weight)
+        row = group_rows + lax.broadcasted_iota(jnp.int32, (rows, 1), 0)
+        mixed = jnp.where(row < info[5], mixed, near_mixed[...]).astype(jnp.bfloat16)
+        for split, out in enumerate(outs):
+
+            @pl.when(info[0] == split)
+            def _():
+                out[...] = mixed
+
+
+def page_windows(info, lengths, table, firsts, counts, rows, page):
+    slots = firsts.shape[0]
+    for slot in range(slots):
+        firsts[slot] = 0
+        counts[slot] = 0
+    for prompt in range(table.shape[0]):
+
+        def visit(j, carry):
+            slot = table[prompt, j] - info[7] * slots
+            left = lengths[prompt] - j * page
+
+            @pl.when((slot >= 0) & (slot < slots) & (left > 0))
+            def _():
+                firsts[slot] = info[3 + prompt] + j * page - info[7] * rows
+                counts[slot] = jnp.minimum(left, page)
+
+            return carry
+
+        lax.fori_loop(0, table.shape[1], visit, 0)
+
+
+def page_window(source, first, count, page):
+    target = lax.broadcasted_iota(jnp.int32, (page, source.shape[0]), 0)
+    origin = lax.broadcasted_iota(jnp.int32, (page, source.shape[0]), 1)
+    taken = (origin == target + first) & (target < count)
+    window = jnp.dot(taken.astype(jnp.bfloat16), source, preferred_element_type=jnp.float32)
+    return jnp.stack([window[:, :HD], window[:, HD:]], axis=1).astype(jnp.bfloat16)
+
+
+def page_kernel(parts, has_written, info, lengths, table, *refs):
+    pairs, (out, firsts, counts) = refs[: len(parts)], refs[len(parts) + has_written :]
+    step = pl.program_id(0)
+    slots, page = out.shape[:2]
+
+    @pl.when(step == 0)
+    def _():
+        page_windows(info, lengths, table, firsts, counts, pairs[0].shape[0], page)
+
+    for number in range(len(parts)):
+
+        @pl.when(step == number)
+        def _():
+            for slot in range(slots):
+                out[slot] = page_window(pairs[number][...], firsts[slot], counts[slot], page)
+
+
+def crossing_kernel(info, lengths, table, *refs):
+    splits = len(refs) - 7
+    pairs, (following, _, out, block, firsts, counts, sem) = refs[:splits], refs[splits:]
+    rows, page = pairs[0].shape[0], block.shape[0]
+    page_windows(info, lengths, table, firsts, counts, rows, page)
+    following_place = (info[7] + 1) // 2 % splits
+    for slot in range(out.shape[0]):
+
+        @pl.when(firsts[slot] + counts[slot] > rows)
+        def _():
+            for split in range(splits):
+                beyond = following[info[0] ^ split ^ following_place]
+                source = jnp.concatenate([pairs[split][...], beyond], axis=0)
+                columns = pl.ds(pl.multiple_of((info[0] ^ split) * HD, HD), HD)
+                block[:, :, columns] = page_window(source, firsts[slot], counts[slot], page)
+            copy = pltpu.make_async_copy(block, out.at[slot], sem)
+            copy.start()
+            copy.wait()
+
+
+def write_pages(info, lengths, table, pairs, parts, *written):
+    rows = pairs[0].shape[0]
+    slots = rows // PAGE + 3
+    return pl.pallas_call(
+        functools.partial(page_kernel, parts, len(written)),
+        grid_spec=pltpu.PrefetchScalarGridSpec(
+            num_scalar_prefetch=3,
+            grid=(len(parts),),
+            in_specs=[pl.BlockSpec((rows, 2 * HD), lambda m, *_: (0, 0))] * len(parts)
+            + [pl.BlockSpec(memory_space=pl.ANY)] * len(written),
+            out_specs=pl.BlockSpec(
+                (slots, PAGE, 2, HD), lambda m, info, *_: (0, 0, 0, info[0] ^ (m + parts[0]))
+            ),
+            scratch_shapes=[pltpu.SMEM((slots,), jnp.int32)] * 2,
+        ),
+        out_shape=jax.ShapeDtypeStruct((slots, PAGE, 2, len(pairs) * HD), jnp.bfloat16),
+        input_output_aliases={3 + len(parts): 0} if written else {},
+        compiler_params=pltpu.CompilerParams(vmem_limit_bytes=24 * 2**20),
+        cost_estimate=cost(1.8 * len(parts)),
+        name="pages",
+    )(info, lengths, table, *[pairs[part] for part in parts], *written)
+
+
+def cross_pages(info, lengths, table, pairs, following, written):
+    splits = len(pairs)
+    slots = written.shape[0]
+    smem, here = pl.BlockSpec(memory_space=pltpu.SMEM), pl.BlockSpec(memory_space=pltpu.VMEM)
+    anywhere = pl.BlockSpec(memory_space=pl.ANY)
+    return pl.pallas_call(
+        crossing_kernel,
+        in_specs=[smem] * 3 + [here] * (splits + 1) + [anywhere],
+        out_specs=anywhere,
+        out_shape=jax.ShapeDtypeStruct(written.shape, written.dtype),
+        input_output_aliases={splits + 4: 0},
+        scratch_shapes=[
+            VMEM(written.shape[1:], written.dtype),
+            pltpu.SMEM((slots,), jnp.int32),
+            pltpu.SMEM((slots,), jnp.int32),
+            pltpu.SemaphoreType.DMA,
+        ],
+        compiler_params=pltpu.CompilerParams(vmem_limit_bytes=24 * 2**20),
+        cost_estimate=cost(3),
+        name="crossing",
+    )(info, lengths, table, *pairs, following, written)
+
+
+def on_core(kernel, out_shape, scratch, name, microseconds, direct):
+    def call(info, *operands):
+        return pl.pallas_call(
+            kernel,
+            grid_spec=pltpu.PrefetchScalarGridSpec(
+                num_scalar_prefetch=1,
+                grid=(1,),
+                in_specs=[
+                    pl.BlockSpec(memory_space=pl.ANY)
+                    if number in direct
+                    else pl.BlockSpec(value.shape, lambda i, info: (0, 0))
+                    for number, value in enumerate(operands)
+                ],
+                out_specs=[pl.BlockSpec(out.shape, lambda i, info: (0, 0)) for out in out_shape],
+                scratch_shapes=scratch,
+            ),
+            out_shape=out_shape,
+            compiler_params=pltpu.CompilerParams(vmem_limit_bytes=24 * 2**20),
+            cost_estimate=cost(microseconds),
+            name=name,
+        )(info, *operands)
+
+    return call
+
+
+def out_kernel(info, *refs):
+    splits = (len(refs) - 4) // 2
+    mine, theirs = refs[:splits], refs[splits : 2 * splits]
+    w_own, w_same, w_swap, out = refs[2 * splits :]
+    half = splits // 2
+    total = jnp.zeros(out.shape, jnp.float32)
+    for split in range(splits):
+        head = info[0] ^ split
+        at = pl.ds(pl.multiple_of(head * HD, HD), HD)
+        total += jnp.dot(mine[split][...], w_own[at, :], preferred_element_type=jnp.float32)
+    for split in range(splits):
+        head = info[0] ^ split
+        at = pl.ds(pl.multiple_of(lax.rem(head, half) * HD, HD), HD)
+        same = head // half == info[2]
+        weight = jnp.where(same, w_same[at, :], w_swap[at, :])
+        total += jnp.dot(theirs[split][...], weight, preferred_element_type=jnp.float32)
+    out[...] = total.astype(jnp.bfloat16)
+
+
+def split_heads(hidden_in, ln_gain, ln_bias, w_qkv, w_out, segment_ids, prompt_lengths, page_table):
+    rows, width = hidden_in.shape
+    splits = w_out.shape[0] // HD
+    count = lax.axis_size("ctx")
+    place = lax.axis_index("ctx") // 2 % splits
+    group = 2 * splits
+
+    def across(value, ctx_mask, tp_mask=0):
+        pairs = []
+        for c in range(count):
+            for t in range(2):
+                pairs.append((2 * c + t, 2 * (c ^ ctx_mask) + (t ^ tp_mask)))
+        return lax.ppermute(value, ("ctx", "tp"), pairs)
+
+    other = across(hidden_in, 0, 1)
+    info, own, gain, bias, *tables, weights, own_columns, outgoing = load(
+        splits, prompt_lengths, hidden_in, ln_gain[None, :], ln_bias[None, :], w_qkv, w_out
+    )
+    inputs = (own, other, gain, bias)
+    queries, pairs = [None] * splits, [None] * splits
+    for split in reversed(range(splits)):
+        made = project(info, split, inputs, tables, weights, rows, 2 * width)
+        queries[split], pairs[split] = made[:2]
+        if len(made) > 2:
+            inputs = (made[2],)
+
+    def after(value, *others):
+        return lax.optimization_barrier((value, *others))[0]
+
+    kv_mine = [pairs[0]] + [None] * (splits - 1)
+    q_mine = [queries[0]] + [None] * (splits - 1)
+    for split in reversed(range(1, splits)):
+        q_mine[split] = across(queries[split], 2 * split)
+    for split in reversed(range(1, splits)):
+        kv_mine[split] = across(after(pairs[split], pairs[0]), 2 * split)
+    w_same = across(after(outgoing, pairs[0]), 0, 1)
+    pages = functools.partial(write_pages, info, prompt_lengths, page_table, pairs)
+    half_written = pages(range(splits // 2))
+    *q_mine[1:], half_written = lax.optimization_barrier((*q_mine[1:], half_written))
+    q_first = q_mine[0]
+    for split in range(1, splits):
+        q_first = jnp.where(place == split, q_mine[split], q_first)
+    q_tail = lax.ppermute(q_first, "ctx", [(group + 2 * s, 2 * s) for s in range(splits)])
+    *kv_mine[1:], q_tail = lax.optimization_barrier((*kv_mine[1:], q_tail))
+    kv_theirs = [across(kv_mine[split], 1) for split in range(splits)]
+
+    keep_pairs = VMEM((group * rows, 2 * HD), jnp.bfloat16)
+    block = jax.ShapeDtypeStruct((rows, HD), jnp.bfloat16)
+    (tail,) = on_core(
+        tail_kernel,
+        [jax.ShapeDtypeStruct((rows, HD + LANES), jnp.bfloat16)],
+        [keep_pairs, pltpu.SemaphoreType.DMA((group,))],
+        "tail",
+        2.7,
+        range(1, 2 * splits + 1),
+    )(info, q_tail, *kv_mine, *kv_theirs)
+    far = lax.ppermute(tail, "ctx", [(2 * s, group + 2 * s) for s in range(splits)])
+    page_head = jnp.stack([pair[:PAGE] for pair in pairs])
+    page_head = after(page_head, tail)
+    following = lax.ppermute(page_head, "ctx", [(i, i - 1) for i in range(1, count)])
+    gathered, near_mixed, near_level = on_core(
+        main_kernel,
+        [
+            jax.ShapeDtypeStruct((splits * rows, HD), jnp.bfloat16),
+            jax.ShapeDtypeStruct((rows, HD), jnp.float32),
+            jax.ShapeDtypeStruct((rows, LANES), jnp.float32),
+        ],
+        [
+            keep_pairs,
+            VMEM((splits * rows, HD), jnp.bfloat16),
+            pltpu.SemaphoreType.DMA((group + splits,)),
+        ],
+        "main",
+        4.8,
+        range(3 * splits),
+    )(after(info, tail), *q_mine, *kv_mine, *kv_theirs)
+    kv_cache = pages(range(splits // 2, splits), after(half_written, gathered, following))
+    blocks = on_core(merge_kernel, [block] * splits, [], "merge", 0.6, ())(
+        info, gathered, near_mixed, near_level, after(far, kv_cache)
+    )
+    w_swap = across(after(w_same, blocks[0]), 1)
+    beyond = [across(blocks[s], 2 * s, 1) for s in range(splits)]
+    kv_cache = cross_pages(
+        after(info, blocks[0]), prompt_lengths, page_table, pairs, following, kv_cache
+    )
+    near = [blocks[0]] + [across(after(blocks[s], kv_cache), 2 * s) for s in range(1, splits)]
+    here = pl.BlockSpec(memory_space=pltpu.VMEM)
+    operands = [*near, *beyond, own_columns, w_same, w_swap]
+    attn_out = pl.pallas_call(
+        out_kernel,
+        in_specs=[pl.BlockSpec(memory_space=pltpu.SMEM)] + [here] * len(operands),
+        out_shape=jax.ShapeDtypeStruct((rows, width), jnp.bfloat16),
+        compiler_params=pltpu.CompilerParams(vmem_limit_bytes=24 * 2**20),
+        cost_estimate=cost(2.7),
+        name="out",
+    )(info, *operands)
+    return attn_out, kv_cache
 
 
 def passed_along(value, axis, steps):
@@ -79,7 +624,7 @@
     )
 
 
-def per_device(hidden_in, ln_gain, ln_bias, w_qkv, w_out, segment_ids, prompt_lengths, page_table):
+def relay_pairs(hidden_in, ln_gain, ln_bias, w_qkv, w_out, segment_ids, prompt_lengths, page_table):
     token_rows = hidden_in.shape[0]
     model_width = w_out.shape[1]
     local_heads = w_out.shape[0] // HD
@@ -151,6 +696,12 @@
     return (attn_out, kv_cache)
 
 
+def per_device(*operands):
+    heads = operands[4].shape[0] // HD
+    spread = lax.axis_size("tp") == 2 and lax.axis_size("ctx") == 4 * heads
+    return (split_heads if spread else relay_pairs)(*operands)
+
+
 def solution(mesh):
     return jax.shard_map(
         per_device,

time: 296 us -> 93 us (0.31)
  the two profiles are of different devices: /device:TPU:16 before, /device:TPU:0 now
where the time goes in v2:
time: 93 us; the launch traced here: 92.7 us
  Pallas kernels  35.9 us (39%)
  starting transfers between devices  29.8 us (32%)
  waiting for transfers between devices  20.6 us (22%)
  local copies, waits for them, and re-layouts  5.42 us (6%)
    ppermute x20, starting transfers between devices, across(): return lax.ppermute(value, ('ctx', 'tp'), pairs)  25.4 us
    ppermute x20, waiting for transfers between devices, across(): return lax.ppermute(value, ('ctx', 'tp'), pairs)  17.1 us
    pallas_call x2, Pallas kernels, write_pages(): pl.pallas_call(functools.partial(page_kernel, parts, len(written)), grid_...  8.86 us
    pallas_call x3, Pallas kernels, call(): pl.pallas_call(kernel, grid_spec=pltpu.PrefetchScalarGridSpec(num_scalar_...  8.02 us
    pallas_call x4, Pallas kernels, project(): pl.pallas_call(functools.partial(first_kernel if is_first else next_kerne...  7.55 us
    pallas_call x1, Pallas kernels, load(): pl.pallas_call(functools.partial(load_kernel, splits), in_specs=[smem] +...  5.83 us
    unnamed x12, local copies, waits for them, and re-layouts  5.29 us
    ppermute x1, waiting for transfers between devices, split_heads(): lax.ppermute(q_first, 'ctx', [(group + 2 * s, 2 * s) for s in range(split...  3.44 us
  transfers between devices with their start and end apart: 23, of which 10 were waited for; matrix products, arithmetic and copies ran while one was open for 0% of the time, Pallas kernels for 28%

profile of v2, /device:TPU:0, one launch (start us, length us, event | category | flops | bytes accessed | tf_op | source)
XLA Modules:
  0.0 92.7 jit_solution(4221896358273390925)
XLA Ops:
  0.6 3.0 %collective-permute-start = (bf16[256,1024]{1,0:T(8,128)(2,1)}, bf16[256,1024]{1,0:T(8,128)(2,1)S(1)}, u32[]{:S(2)}, u32[]{:S(2)}) collective-permute-start(bf16[256,1024]{1,0:T(8,128)(2,1)} %own.1), channel_id=1, source_target_pairs={{0,1},{1,0},{2,3},{3,2},{4,5},{5,4},{6,7},{7,6},{8,9},{9,8},{10,11... | collective-permute-start | bytes 1572872 | tf_op jit(solution)/shard_map/ppermute | solution.py:473
  3.7 2.2 %copy-done = bf16[1024,2048]{1,0:T(8,128)(2,1)S(1)} copy-done((bf16[1024,2048]{1,0:T(8,128)(2,1)S(1)}, bf16[1024,2048]{1,0:T(8,128)(2,1)}, u32[]{:S(2)}) %copy-start) | copy-done | bytes 4194328
  9.0 5.8 %load.1 = (s32[8]{0:T(128)S(1)}, bf16[256,1024]{1,0:T(8,128)(2,1)S(1)}, f32[1,2048]{1,0:T(1,128)S(1)}, f32[1,2048]{1,0:T(1,128)S(1)}, f32[256,128]{1,0:T(8,128)S...) custom-call(s32[3]{0:T(128)S(1)} %copy-done.5, ...), custom_call_target="tpu_custom_call" | custom-call | flops 2100000000 | tf_op jit(solution)/shard_map/load/pallas_call | solution.py:102
  15.8 2.6 %project.4 = (bf16[256,256]{1,0:T(8,128)(2,1)S(1)}, bf16[256,512]{1,0:T(8,128)(2,1)S(1)}, bf16[256,2048]{1,0:T(8,128)(2,1)S(1)}) custom-call(s32[8]{0:T(128)S(1)} %get-tuple-element.86.info, bf16[256,1024]{1,0:T(8,128)(2,1)S(1)} %get-tuple-element.50.own, bf16[256,1024]{1,0:T(8,128)(2,1)S(1)} %collective-permute-done.other, ...), custom_call_target="tpu_custom_call" | custom-call | flops 945000000 | tf_op jit(solution)/shard_map/project/pallas_call | solution.py:180
  18.3 1.7 %project.6 = (bf16[256,256]{1,0:T(8,128)(2,1)S(1)}, bf16[256,512]{1,0:T(8,128)(2,1)S(1)}) custom-call(s32[8]{0:T(128)S(1)} %get-tuple-element.86.info, bf16[256,2048]{1,0:T(8,128)(2,1)S(1)} %get-tuple-element.57.normed, f32[256,128]{1,0:T(8,128)S(1)} %get-tuple-element.53.keep, f32[256,128]{1,0:T(8,128)S(1)} %get-tuple-element.54.below, ...), custom_call_target="tpu_custom_call" | custom-call | flops 595000000 | tf_op jit(solution)/shard_map/project/pallas_call | solution.py:180
  20.0 1.7 %project.7 = (bf16[256,256]{1,0:T(8,128)(2,1)S(1)}, bf16[256,512]{1,0:T(8,128)(2,1)S(1)}) custom-call(s32[8]{0:T(128)S(1)} %get-tuple-element.86.info, bf16[256,2048]{1,0:T(8,128)(2,1)S(1)} %get-tuple-element.57.normed, f32[256,128]{1,0:T(8,128)S(1)} %get-tuple-element.53.keep, f32[256,128]{1,0:T(8,128)S(1)} %get-tuple-element.54.below, ...), custom_call_target="tpu_custom_call" | custom-call | flops 595000000 | tf_op jit(solution)/shard_map/project/pallas_call | solution.py:180
  21.7 1.7 %project.5 = (bf16[256,256]{1,0:T(8,128)(2,1)S(1)}, bf16[256,512]{1,0:T(8,128)(2,1)S(1)}) custom-call(s32[8]{0:T(128)S(1)} %get-tuple-element.86.info, bf16[256,2048]{1,0:T(8,128)(2,1)S(1)} %get-tuple-element.57.normed, f32[256,128]{1,0:T(8,128)S(1)} %get-tuple-element.53.keep, f32[256,128]{1,0:T(8,128)S(1)} %get-tuple-element.54.below, ...), custom_call_target="tpu_custom_call" | custom-call | flops 595000000 | tf_op jit(solution)/shard_map/project/pallas_call | solution.py:180
  23.4 1.9 %collective-permute-start.5 = (bf16[256,256]{1,0:T(8,128)(2,1)S(1)}, bf16[256,256]{1,0:T(8,128)(2,1)S(1)}, u32[]{:S(2)}, u32[]{:S(2)}) collective-permute-start(bf16[256,256]{1,0:T(8,128)(2,1)S(1)} %get-tuple-element.66), channel_id=1, source_target_pairs={{0,8},{1,9},{2,10},{3,11},{4,12},{5,13},{6,14},{7,15},{8,0},{9,1},... | collective-permute-start | bytes 393224 | tf_op jit(solution)/shard_map/ppermute | solution.py:473
  25.3 1.5 %collective-permute-start.4 = (bf16[256,256]{1,0:T(8,128)(2,1)S(1)}, bf16[256,256]{1,0:T(8,128)(2,1)S(1)}, u32[]{:S(2)}, u32[]{:S(2)}) collective-permute-start(bf16[256,256]{1,0:T(8,128)(2,1)S(1)} %get-tuple-element.65), channel_id=1, source_target_pairs={{0,4},{1,5},{2,6},{3,7},{4,0},{5,1},{6,2},{7,3},{8,12},{9,13},{10,... | collective-permute-start | bytes 393224 | tf_op jit(solution)/shard_map/ppermute | solution.py:473
  27.0 2.9 %collective-permute-start.3 = (bf16[256,512]{1,0:T(8,128)(2,1)S(1)}, bf16[256,512]{1,0:T(8,128)(2,1)S(1)}, u32[]{:S(2)}, u32[]{:S(2)}) collective-permute-start(bf16[256,512]{1,0:T(8,128)(2,1)S(1)} %get-tuple-element.64.refs_1_.refs_3_), channel_id=1, source_target_pairs={{0,12},{1,13},{2,14},{3,15},{4,8},{5,9},{6,10},{7,11},{8,4},{9,5},... | collective-permute-start | bytes 786440 | tf_op jit(solution)/shard_map/ppermute | solution.py:473
  29.9 4.4 %pages.2.refs_2_ = bf16[5,128,2,1024]{3,2,1,0:T(2,128)(2,1)} custom-call(s32[8]{0:T(128)S(1)} %get-tuple-element.86.info, s32[3]{0:T(128)S(1)} %copy-done.5, s32[3,16]{1,0:T(4,128)S(1)} %copy-done.4, bf16[256,512]{1,0:T(8,128)(2,1)S(1)} %get-tuple-element.59.refs_0_.refs_1_.refs_4_, bf16[256,512]{1,0:T(8,128)(2,1)S(1)} %get-tuple-element.60.refs_1_), custom_call_target="tpu_custom_call" | custom-call | flops 1260000000 | tf_op jit(solution)/shard_map/pages/pallas_call | solution.py:374
  34.8 3.5 %collective-permute-done.4.refs_1_ = bf16[256,256]{1,0:T(8,128)(2,1)S(1)} collective-permute-done((bf16[256,256]{1,0:T(8,128)(2,1)S(1)}, bf16[256,256]{1,0:T(8,128)(2,1)S(1)}, u32[]{:S(2)}, u32[]{:S(2)}) %collective-permute-start.4) | collective-permute-done | bytes 131104 | tf_op jit(solution)/shard_map/ppermute | solution.py:473
  38.3 2.0 %collective-permute-start.1 = (bf16[256,512]{1,0:T(8,128)(2,1)S(1)}, bf16[256,512]{1,0:T(8,128)(2,1)S(1)}, u32[]{:S(2)}, u32[]{:S(2)}) collective-permute-start(bf16[256,512]{1,0:T(8,128)(2,1)S(1)} %get-tuple-element.60.refs_1_), channel_id=1, source_target_pairs={{0,4},{1,5},{2,6},{3,7},{4,0},{5,1},{6,2},{7,3},{8,12},{9,13},{10,... | collective-permute-start | bytes 786440 | tf_op jit(solution)/shard_map/ppermute | solution.py:473
  40.3 1.3 %collective-permute-start.7 = (bf16[256,256]{1,0:T(8,128)(2,1)S(1)}, bf16[256,256]{1,0:T(8,128)(2,1)S(1)}, u32[]{:S(2)}, u32[]{:S(2)}) collective-permute-start(bf16[256,256]{1,0:T(8,128)(2,1)S(1)} %select_select_fusion), channel_id=1, source_target_pairs={{16,0},{20,4},{24,8},{28,12},{17,1},{21,5},{25,9},{29,13}} | collective-permute-start | bytes 393224 | tf_op jit(solution)/shard_map/ppermute | solution.py:503
  41.7 1.5 %collective-permute-start.21 = (bf16[512,1024]{1,0:T(8,128)(2,1)S(1)}, bf16[512,1024]{1,0:T(8,128)(2,1)S(1)}, u32[]{:S(2)}, u32[]{:S(2)}) collective-permute-start(bf16[512,1024]{1,0:T(8,128)(2,1)S(1)} %get-tuple-element.94), channel_id=1, source_target_pairs={{0,1},{1,0},{2,3},{3,2},{4,5},{5,4},{6,7},{7,6},{8,9},{9,8},{10,11... | collective-permute-start | bytes 3145736 | tf_op jit(solution)/shard_map/ppermute | solution.py:473
  43.2 1.5 %collective-permute-done.1.refs_2_.refs_5_ = bf16[256,512]{1,0:T(8,128)(2,1)S(1)} collective-permute-done((bf16[256,512]{1,0:T(8,128)(2,1)S(1)}, bf16[256,512]{1,0:T(8,128)(2,1)S(1)}, u32[]{:S(2)}, u32[]{:S(2)}) %collective-permute-start.1) | collective-permute-done | bytes 262176 | tf_op jit(solution)/shard_map/ppermute | solution.py:473
  44.6 3.4 %collective-permute-done.7.refs_0_ = bf16[256,256]{1,0:T(8,128)(2,1)S(1)} collective-permute-done((bf16[256,256]{1,0:T(8,128)(2,1)S(1)}, bf16[256,256]{1,0:T(8,128)(2,1)S(1)}, u32[]{:S(2)}, u32[]{:S(2)}) %collective-permute-start.7) | collective-permute-done | bytes 131104 | tf_op jit(solution)/shard_map/ppermute | solution.py:503
  50.4 2.6 %tail.1 = bf16[256,384]{1,0:T(8,128)(2,1)S(1)} custom-call(s32[8]{0:T(128)S(1)} %get-tuple-element.86.info, bf16[256,256]{1,0:T(8,128)(2,1)S(1)} %collective-permute-done.7.refs_0_, bf16[256,512]{1,0:T(8,128)(2,1)S(1)} %get-tuple-element.59.refs_0_.refs_1_.refs_4_, bf16[256,512]{1,0:T(8,128)(2,1)S(1)} %collective-permute-done.1.refs_2_.refs_5_, ...), custom_call_target="tpu_custom_call" | custom-call | flops 945000000 | tf_op jit(solution)/shard_map/tail/pallas_call | solution.py:419
  53.0 1.3 %collective-permute-start.13 = (bf16[4,128,512]{2,1,0:T(8,128)(2,1)S(1)}, bf16[4,128,512]{2,1,0:T(8,128)(2,1)S(1)}, u32[]{:S(2)}, u32[]{:S(2)}) collective-permute-start(bf16[4,128,512]{2,1,0:T(8,128)(2,1)S(1)} %pad_maximum_fusion), channel_id=1, source_target_pairs={{2,0},{4,2},{6,4},{8,6},{10,8},{12,10},{14,12},{16,14},{18,16},{20... | collective-permute-start | bytes 1572872 | tf_op jit(solution)/shard_map/ppermute | solution.py:520
  54.3 1.8 %collective-permute-start.12 = (bf16[256,384]{1,0:T(8,128)(2,1)S(1)}, bf16[256,384]{1,0:T(8,128)(2,1)S(1)}, u32[]{:S(2)}, u32[]{:S(2)}) collective-permute-start(bf16[256,384]{1,0:T(8,128)(2,1)S(1)} %tail.1), channel_id=1, source_target_pairs={{0,16},{4,20},{8,24},{12,28},{1,17},{5,21},{9,25},{13,29}} | collective-permute-start | bytes 589832 | tf_op jit(solution)/shard_map/ppermute | solution.py:517
  56.1 4.8 %main.1 = (bf16[1024,256]{1,0:T(8,128)(2,1)S(1)}, f32[256,256]{1,0:T(8,128)S(1)}, f32[256,128]{1,0:T(8,128)S(1)}) custom-call(s32[8]{0:T(128)S(1)} %get-tuple-element.86.info, bf16[256,256]{1,0:T(8,128)(2,1)S(1)} %get-tuple-element.71.refs_0_, bf16[256,256]{1,0:T(8,128)(2,1)S(1)} %collective-permute-done.4.refs_1_, ...), custom_call_target="tpu_custom_call" | custom-call | flops 1680000000 | tf_op jit(solution)/shard_map/main/pallas_call | solution.py:419
  61.0 4.4 %pages.3.refs_5_ = bf16[5,128,2,1024]{3,2,1,0:T(2,128)(2,1)} custom-call(s32[8]{0:T(128)S(1)} %get-tuple-element.86.info, s32[3]{0:T(128)S(1)} %copy-done.5, s32[3,16]{1,0:T(4,128)S(1)} %copy-done.4, bf16[256,512]{1,0:T(8,128)(2,1)S(1)} %get-tuple-element.62.refs_0_.refs_2_, ...), custom_call_target="tpu_custom_call", output_to_operand_aliasing={{}: (5, {})} | custom-call | flops 1260000000 | tf_op jit(solution)/shard_map/pages/pallas_call | solution.py:374
  66.0 2.1 %collective-permute-start.22 = (bf16[512,1024]{1,0:T(8,128)(2,1)S(1)}, bf16[512,1024]{1,0:T(8,128)(2,1)S(1)}, u32[]{:S(2)}, u32[]{:S(2)}) collective-permute-start(bf16[512,1024]{1,0:T(8,128)(2,1)S(1)} %collective-permute-done.21.refs_9_), channel_id=1, source_target_pairs={{0,2},{1,3},{2,0},{3,1},{4,6},{5,7},{6,4},{7,5},{8,10},{9,11},{10,... | collective-permute-start | bytes 3145736 | tf_op jit(solution)/shard_map/ppermute | solution.py:473
  68.2 3.1 %crossing.1 = bf16[5,128,2,1024]{3,2,1,0:T(2,128)(2,1)} custom-call(s32[8]{0:T(128)S(1)} %get-tuple-element.86.info, s32[3]{0:T(128)S(1)} %copy-done.5, s32[3,16]{1,0:T(4,128)S(1)} %copy-done.4, bf16[256,512]{1,0:T(8,128)(2,1)S(1)} %get-tuple-element.59.refs_0_.refs_1_.refs_4_, ...), custom_call_target="tpu_custom_call", output_to_operand_aliasing={{}: (8, {})} | custom-call | flops 1050000000 | tf_op jit(solution)/shard_map/crossing/pallas_call | solution.py:399
  71.3 2.1 %collective-permute-start.15 = (bf16[256,256]{1,0:T(8,128)(2,1)S(1)}, bf16[256,256]{1,0:T(8,128)(2,1)S(1)}, u32[]{:S(2)}, u32[]{:S(2)}) collective-permute-start(bf16[256,256]{1,0:T(8,128)(2,1)S(1)} %get-tuple-element.89), channel_id=1, source_target_pairs={{0,8},{1,9},{2,10},{3,11},{4,12},{5,13},{6,14},{7,15},{8,0},{9,1},... | collective-permute-start | bytes 393224 | tf_op jit(solution)/shard_map/ppermute | solution.py:473
  73.4 1.4 %collective-permute-start.14 = (bf16[256,256]{1,0:T(8,128)(2,1)S(1)}, bf16[256,256]{1,0:T(8,128)(2,1)S(1)}, u32[]{:S(2)}, u32[]{:S(2)}) collective-permute-start(bf16[256,256]{1,0:T(8,128)(2,1)S(1)} %get-tuple-element.87), channel_id=1, source_target_pairs={{0,4},{1,5},{2,6},{3,7},{4,0},{5,1},{6,2},{7,3},{8,12},{9,13},{10,... | collective-permute-start | bytes 393224 | tf_op jit(solution)/shard_map/ppermute | solution.py:473
  74.8 1.5 %collective-permute-start.17 = (bf16[256,256]{1,0:T(8,128)(2,1)S(1)}, bf16[256,256]{1,0:T(8,128)(2,1)S(1)}, u32[]{:S(2)}, u32[]{:S(2)}) collective-permute-start(bf16[256,256]{1,0:T(8,128)(2,1)S(1)} %get-tuple-element.84.refs_0_), channel_id=1, source_target_pairs={{0,1},{1,0},{2,3},{3,2},{4,5},{5,4},{6,7},{7,6},{8,9},{9,8},{10,11... | collective-permute-start | bytes 393224 | tf_op jit(solution)/shard_map/ppermute | solution.py:473
  76.3 2.3 %collective-permute-done.16.refs_3_ = bf16[256,256]{1,0:T(8,128)(2,1)S(1)} collective-permute-done((bf16[256,256]{1,0:T(8,128)(2,1)S(1)}, bf16[256,256]{1,0:T(8,128)(2,1)S(1)}, u32[]{:S(2)}, u32[]{:S(2)}) %collective-permute-start.16) | collective-permute-done | bytes 131104 | tf_op jit(solution)/shard_map/ppermute | solution.py:473
  78.6 1.6 %collective-permute-start.18 = (bf16[256,256]{1,0:T(8,128)(2,1)S(1)}, bf16[256,256]{1,0:T(8,128)(2,1)S(1)}, u32[]{:S(2)}, u32[]{:S(2)}) collective-permute-start(bf16[256,256]{1,0:T(8,128)(2,1)S(1)} %get-tuple-element.87), channel_id=1, source_target_pairs={{0,5},{1,4},{2,7},{3,6},{4,1},{5,0},{6,3},{7,2},{8,13},{9,12},{10,... | collective-permute-start | bytes 393224 | tf_op jit(solution)/shard_map/ppermute | solution.py:473
  81.8 2.1 %collective-permute-start.20 = (bf16[256,256]{1,0:T(8,128)(2,1)S(1)}, bf16[256,256]{1,0:T(8,128)(2,1)S(1)}, u32[]{:S(2)}, u32[]{:S(2)}) collective-permute-start(bf16[256,256]{1,0:T(8,128)(2,1)S(1)} %get-tuple-element.91), channel_id=1, source_target_pairs={{0,13},{1,12},{2,15},{3,14},{4,9},{5,8},{6,11},{7,10},{8,5},{9,4},... | collective-permute-start | bytes 393224 | tf_op jit(solution)/shard_map/ppermute | solution.py:473
  83.9 6.2 %collective-permute-done.18.refs_5_ = bf16[256,256]{1,0:T(8,128)(2,1)S(1)} collective-permute-done((bf16[256,256]{1,0:T(8,128)(2,1)S(1)}, bf16[256,256]{1,0:T(8,128)(2,1)S(1)}, u32[]{:S(2)}, u32[]{:S(2)}) %collective-permute-start.18) | collective-permute-done | bytes 131104 | tf_op jit(solution)/shard_map/ppermute | solution.py:473
  90.1 2.6 %out.1 = bf16[256,1024]{1,0:T(8,128)(2,1)} custom-call(s32[8]{0:T(128)S(1)} %get-tuple-element.86.info, bf16[256,256]{1,0:T(8,128)(2,1)S(1)} %get-tuple-element.84.refs_0_, bf16[256,256]{1,0:T(8,128)(2,1)S(1)} %collective-permute-done.14.refs_1_, bf16[256,256]{1,0:T(8,128)(2,1)S(1)} %collective-permute-done.15.refs_2_, ...), custom_call_target="tpu_custom_call" | custom-call | flops 945000000 | tf_op jit(solution)/shard_map/out/pallas_call | solution.py:549
  (47 shorter events, 9.4 us)
Async XLA Ops:
  0.6 15.1 %collective-permute-start = (bf16[256,1024]{1,0:T(8,128)(2,1)}, bf16[256,1024]{1,0:T(8,128)(2,1)S(1)}, u32[]{:S(2)}, u32[]{:S(2)}) collective-permute-start(bf16[256,1024]{1,0:T(8,128)(2,1)} %own.1), channel_id=1, source_target_pairs={{0,1},{1,0},{2,3},{3,2},{4,5},{5,4},{6,7},{7,6},{8,9},{9,8},{10,11... | collective-permute-start | bytes 1572872 | tf_op jit(solution)/shard_map/ppermute | solution.py:473
  3.7 2.2 %copy-start = (bf16[1024,2048]{1,0:T(8,128)(2,1)S(1)}, bf16[1024,2048]{1,0:T(8,128)(2,1)}, u32[]{:S(2)}) copy-start(bf16[1024,2048]{1,0:T(8,128)(2,1)} %w_out.1) | copy-start | bytes 12582916
  5.9 1.0 %copy-start.1 = (bf16[256,1024]{1,0:T(8,128)(2,1)S(1)}, bf16[256,1024]{1,0:T(8,128)(2,1)}, u32[]{:S(2)}) copy-start(bf16[256,1024]{1,0:T(8,128)(2,1)} %own.1) | copy-start | bytes 1572868
  7.0 0.7 copy-start.2
  7.7 0.7 copy-start.3
  8.4 0.7 copy-start.5
  21.7 8.2 %copy-start.4 = (s32[3,16]{1,0:T(4,128)S(1)}, s32[3,16]{1,0:T(4,128)}, u32[]{:S(2)}) copy-start(s32[3,16]{1,0:T(4,128)} %table.5) | copy-start | bytes 580
  23.4 10.9 %collective-permute-start.5 = (bf16[256,256]{1,0:T(8,128)(2,1)S(1)}, bf16[256,256]{1,0:T(8,128)(2,1)S(1)}, u32[]{:S(2)}, u32[]{:S(2)}) collective-permute-start(bf16[256,256]{1,0:T(8,128)(2,1)S(1)} %get-tuple-element.66), channel_id=1, source_target_pairs={{0,8},{1,9},{2,10},{3,11},{4,12},{5,13},{6,14},{7,15},{8,0},{9,1},... | collective-permute-start | bytes 393224 | tf_op jit(solution)/shard_map/ppermute | solution.py:473
  25.3 13.0 %collective-permute-start.4 = (bf16[256,256]{1,0:T(8,128)(2,1)S(1)}, bf16[256,256]{1,0:T(8,128)(2,1)S(1)}, u32[]{:S(2)}, u32[]{:S(2)}) collective-permute-start(bf16[256,256]{1,0:T(8,128)(2,1)S(1)} %get-tuple-element.65), channel_id=1, source_target_pairs={{0,4},{1,5},{2,6},{3,7},{4,0},{5,1},{6,2},{7,3},{8,12},{9,13},{10,... | collective-permute-start | bytes 393224 | tf_op jit(solution)/shard_map/ppermute | solution.py:473
  26.8 13.5 %collective-permute-start.6 = (bf16[256,256]{1,0:T(8,128)(2,1)S(1)}, bf16[256,256]{1,0:T(8,128)(2,1)S(1)}, u32[]{:S(2)}, u32[]{:S(2)}) collective-permute-start(bf16[256,256]{1,0:T(8,128)(2,1)S(1)} %get-tuple-element.67), channel_id=1, source_target_pairs={{0,12},{1,13},{2,14},{3,15},{4,8},{5,9},{6,10},{7,11},{8,4},{9,5},... | collective-permute-start | bytes 393224 | tf_op jit(solution)/shard_map/ppermute | solution.py:473
  26.9 21.7 %collective-permute-start.8 = (bf16[256,512]{1,0:T(8,128)(2,1)S(1)}, bf16[256,512]{1,0:T(8,128)(2,1)S(1)}, u32[]{:S(2)}, u32[]{:S(2)}) collective-permute-start(bf16[256,512]{1,0:T(8,128)(2,1)S(1)} %get-tuple-element.59.refs_0_.refs_1_.refs_4_), channel_id=1, source_target_pairs={{0,2},{1,3},{2,0},{3,1},{4,6},{5,7},{6,4},{7,5},{8,10},{9,11},{10,... | collective-permute-start | bytes 786440 | tf_op jit(solution)/shard_map/ppermute | solution.py:473
  27.0 14.6 %collective-permute-start.3 = (bf16[256,512]{1,0:T(8,128)(2,1)S(1)}, bf16[256,512]{1,0:T(8,128)(2,1)S(1)}, u32[]{:S(2)}, u32[]{:S(2)}) collective-permute-start(bf16[256,512]{1,0:T(8,128)(2,1)S(1)} %get-tuple-element.64.refs_1_.refs_3_), channel_id=1, source_target_pairs={{0,12},{1,13},{2,14},{3,15},{4,8},{5,9},{6,10},{7,11},{8,4},{9,5},... | collective-permute-start | bytes 786440 | tf_op jit(solution)/shard_map/ppermute | solution.py:473
  34.3 8.9 %collective-permute-start.2 = (bf16[256,512]{1,0:T(8,128)(2,1)S(1)}, bf16[256,512]{1,0:T(8,128)(2,1)S(1)}, u32[]{:S(2)}, u32[]{:S(2)}) collective-permute-start(bf16[256,512]{1,0:T(8,128)(2,1)S(1)} %get-tuple-element.62.refs_0_.refs_2_), channel_id=1, source_target_pairs={{0,8},{1,9},{2,10},{3,11},{4,12},{5,13},{6,14},{7,15},{8,0},{9,1},... | collective-permute-start | bytes 786440 | tf_op jit(solution)/shard_map/ppermute | solution.py:473
  38.3 6.4 %collective-permute-start.1 = (bf16[256,512]{1,0:T(8,128)(2,1)S(1)}, bf16[256,512]{1,0:T(8,128)(2,1)S(1)}, u32[]{:S(2)}, u32[]{:S(2)}) collective-permute-start(bf16[256,512]{1,0:T(8,128)(2,1)S(1)} %get-tuple-element.60.refs_1_), channel_id=1, source_target_pairs={{0,4},{1,5},{2,6},{3,7},{4,0},{5,1},{6,2},{7,3},{8,12},{9,13},{10,... | collective-permute-start | bytes 786440 | tf_op jit(solution)/shard_map/ppermute | solution.py:473
  40.3 7.8 %collective-permute-start.7 = (bf16[256,256]{1,0:T(8,128)(2,1)S(1)}, bf16[256,256]{1,0:T(8,128)(2,1)S(1)}, u32[]{:S(2)}, u32[]{:S(2)}) collective-permute-start(bf16[256,256]{1,0:T(8,128)(2,1)S(1)} %select_select_fusion), channel_id=1, source_target_pairs={{16,0},{20,4},{24,8},{28,12},{17,1},{21,5},{25,9},{29,13}} | collective-permute-start | bytes 393224 | tf_op jit(solution)/shard_map/ppermute | solution.py:503
  41.7 24.4 %collective-permute-start.21 = (bf16[512,1024]{1,0:T(8,128)(2,1)S(1)}, bf16[512,1024]{1,0:T(8,128)(2,1)S(1)}, u32[]{:S(2)}, u32[]{:S(2)}) collective-permute-start(bf16[512,1024]{1,0:T(8,128)(2,1)S(1)} %get-tuple-element.94), channel_id=1, source_target_pairs={{0,1},{1,0},{2,3},{3,2},{4,5},{5,4},{6,7},{7,6},{8,9},{9,8},{10,11... | collective-permute-start | bytes 3145736 | tf_op jit(solution)/shard_map/ppermute | solution.py:473
  48.1 1.5 %collective-permute-start.10 = (bf16[256,512]{1,0:T(8,128)(2,1)S(1)}, bf16[256,512]{1,0:T(8,128)(2,1)S(1)}, u32[]{:S(2)}, u32[]{:S(2)}) collective-permute-start(bf16[256,512]{1,0:T(8,128)(2,1)S(1)} %collective-permute-done.2.refs_3_.refs_6_), channel_id=1, source_target_pairs={{0,2},{1,3},{2,0},{3,1},{4,6},{5,7},{6,4},{7,5},{8,10},{9,11},{10,... | collective-permute-start | bytes 786440 | tf_op jit(solution)/shard_map/ppermute | solution.py:473
  48.1 1.9 %collective-permute-start.11 = (bf16[256,512]{1,0:T(8,128)(2,1)S(1)}, bf16[256,512]{1,0:T(8,128)(2,1)S(1)}, u32[]{:S(2)}, u32[]{:S(2)}) collective-permute-start(bf16[256,512]{1,0:T(8,128)(2,1)S(1)} %collective-permute-done.3.refs_4_.refs_7_), channel_id=1, source_target_pairs={{0,2},{1,3},{2,0},{3,1},{4,6},{5,7},{6,4},{7,5},{8,10},{9,11},{10,... | collective-permute-start | bytes 786440 | tf_op jit(solution)/shard_map/ppermute | solution.py:473
  48.6 1.8 %collective-permute-start.9 = (bf16[256,512]{1,0:T(8,128)(2,1)S(1)}, bf16[256,512]{1,0:T(8,128)(2,1)S(1)}, u32[]{:S(2)}, u32[]{:S(2)}) collective-permute-start(bf16[256,512]{1,0:T(8,128)(2,1)S(1)} %collective-permute-done.1.refs_2_.refs_5_), channel_id=1, source_target_pairs={{0,2},{1,3},{2,0},{3,1},{4,6},{5,7},{6,4},{7,5},{8,10},{9,11},{10,... | collective-permute-start | bytes 786440 | tf_op jit(solution)/shard_map/ppermute | solution.py:473
  53.0 8.0 %collective-permute-start.13 = (bf16[4,128,512]{2,1,0:T(8,128)(2,1)S(1)}, bf16[4,128,512]{2,1,0:T(8,128)(2,1)S(1)}, u32[]{:S(2)}, u32[]{:S(2)}) collective-permute-start(bf16[4,128,512]{2,1,0:T(8,128)(2,1)S(1)} %pad_maximum_fusion), channel_id=1, source_target_pairs={{2,0},{4,2},{6,4},{8,6},{10,8},{12,10},{14,12},{16,14},{18,16},{20... | collective-permute-start | bytes 1572872 | tf_op jit(solution)/shard_map/ppermute | solution.py:520
  54.3 11.1 %collective-permute-start.12 = (bf16[256,384]{1,0:T(8,128)(2,1)S(1)}, bf16[256,384]{1,0:T(8,128)(2,1)S(1)}, u32[]{:S(2)}, u32[]{:S(2)}) collective-permute-start(bf16[256,384]{1,0:T(8,128)(2,1)S(1)} %tail.1), channel_id=1, source_target_pairs={{0,16},{4,20},{8,24},{12,28},{1,17},{5,21},{9,25},{13,29}} | collective-permute-start | bytes 589832 | tf_op jit(solution)/shard_map/ppermute | solution.py:517
  66.0 24.0 %collective-permute-start.22 = (bf16[512,1024]{1,0:T(8,128)(2,1)S(1)}, bf16[512,1024]{1,0:T(8,128)(2,1)S(1)}, u32[]{:S(2)}, u32[]{:S(2)}) collective-permute-start(bf16[512,1024]{1,0:T(8,128)(2,1)S(1)} %collective-permute-done.21.refs_9_), channel_id=1, source_target_pairs={{0,2},{1,3},{2,0},{3,1},{4,6},{5,7},{6,4},{7,5},{8,10},{9,11},{10,... | collective-permute-start | bytes 3145736 | tf_op jit(solution)/shard_map/ppermute | solution.py:473
  71.3 7.3 %collective-permute-start.16 = (bf16[256,256]{1,0:T(8,128)(2,1)S(1)}, bf16[256,256]{1,0:T(8,128)(2,1)S(1)}, u32[]{:S(2)}, u32[]{:S(2)}) collective-permute-start(bf16[256,256]{1,0:T(8,128)(2,1)S(1)} %get-tuple-element.91), channel_id=1, source_target_pairs={{0,12},{1,13},{2,14},{3,15},{4,8},{5,9},{6,10},{7,11},{8,4},{9,5},... | collective-permute-start | bytes 393224 | tf_op jit(solution)/shard_map/ppermute | solution.py:473
  71.3 8.8 %collective-permute-start.15 = (bf16[256,256]{1,0:T(8,128)(2,1)S(1)}, bf16[256,256]{1,0:T(8,128)(2,1)S(1)}, u32[]{:S(2)}, u32[]{:S(2)}) collective-permute-start(bf16[256,256]{1,0:T(8,128)(2,1)S(1)} %get-tuple-element.89), channel_id=1, source_target_pairs={{0,8},{1,9},{2,10},{3,11},{4,12},{5,13},{6,14},{7,15},{8,0},{9,1},... | collective-permute-start | bytes 393224 | tf_op jit(solution)/shard_map/ppermute | solution.py:473
  73.4 8.4 %collective-permute-start.14 = (bf16[256,256]{1,0:T(8,128)(2,1)S(1)}, bf16[256,256]{1,0:T(8,128)(2,1)S(1)}, u32[]{:S(2)}, u32[]{:S(2)}) collective-permute-start(bf16[256,256]{1,0:T(8,128)(2,1)S(1)} %get-tuple-element.87), channel_id=1, source_target_pairs={{0,4},{1,5},{2,6},{3,7},{4,0},{5,1},{6,2},{7,3},{8,12},{9,13},{10,... | collective-permute-start | bytes 393224 | tf_op jit(solution)/shard_map/ppermute | solution.py:473
  74.8 9.1 %collective-permute-start.17 = (bf16[256,256]{1,0:T(8,128)(2,1)S(1)}, bf16[256,256]{1,0:T(8,128)(2,1)S(1)}, u32[]{:S(2)}, u32[]{:S(2)}) collective-permute-start(bf16[256,256]{1,0:T(8,128)(2,1)S(1)} %get-tuple-element.84.refs_0_), channel_id=1, source_target_pairs={{0,1},{1,0},{2,3},{3,2},{4,5},{5,4},{6,7},{7,6},{8,9},{9,8},{10,11... | collective-permute-start | bytes 393224 | tf_op jit(solution)/shard_map/ppermute | solution.py:473
  78.6 11.5 %collective-permute-start.18 = (bf16[256,256]{1,0:T(8,128)(2,1)S(1)}, bf16[256,256]{1,0:T(8,128)(2,1)S(1)}, u32[]{:S(2)}, u32[]{:S(2)}) collective-permute-start(bf16[256,256]{1,0:T(8,128)(2,1)S(1)} %get-tuple-element.87), channel_id=1, source_target_pairs={{0,5},{1,4},{2,7},{3,6},{4,1},{5,0},{6,3},{7,2},{8,13},{9,12},{10,... | collective-permute-start | bytes 393224 | tf_op jit(solution)/shard_map/ppermute | solution.py:473
  80.1 9.9 %collective-permute-start.19 = (bf16[256,256]{1,0:T(8,128)(2,1)S(1)}, bf16[256,256]{1,0:T(8,128)(2,1)S(1)}, u32[]{:S(2)}, u32[]{:S(2)}) collective-permute-start(bf16[256,256]{1,0:T(8,128)(2,1)S(1)} %get-tuple-element.89), channel_id=1, source_target_pairs={{0,9},{1,8},{2,11},{3,10},{4,13},{5,12},{6,15},{7,14},{8,1},{9,0},... | collective-permute-start | bytes 393224 | tf_op jit(solution)/shard_map/ppermute | solution.py:473
  81.8 8.2 %collective-permute-start.20 = (bf16[256,256]{1,0:T(8,128)(2,1)S(1)}, bf16[256,256]{1,0:T(8,128)(2,1)S(1)}, u32[]{:S(2)}, u32[]{:S(2)}) collective-permute-start(bf16[256,256]{1,0:T(8,128)(2,1)S(1)} %get-tuple-element.91), channel_id=1, source_target_pairs={{0,13},{1,12},{2,15},{3,14},{4,9},{5,8},{6,11},{7,10},{8,5},{9,4},... | collective-permute-start | bytes 393224 | tf_op jit(solution)/shard_map/ppermute | solution.py:473

commit v3 on v2

--- a/solution.py
+++ b/solution.py
@@ -29,9 +29,30 @@
     return first
 
 
+def page_windows(info, lengths, table, rows):
+    slots = (info.shape[0] - 8) // 2
+    for entry in range(8, 8 + 2 * slots):
+        info[entry] = 0
+    for prompt in range(table.shape[0]):
+
+        def visit(j, carry):
+            slot = table[prompt, j] - info[7] * slots
+            left = lengths[prompt] - j * PAGE
+
+            @pl.when((slot >= 0) & (slot < slots) & (left > 0))
+            def _():
+                info[8 + slot] = info[3 + prompt] + j * PAGE - info[7] * rows
+                info[8 + slots + slot] = jnp.minimum(left, PAGE)
+
+            return carry
+
+        lax.fori_loop(0, table.shape[1], visit, 0)
+
+
 def load_kernel(
     splits,
     lengths,
+    table,
     own,
     gain,
     bias,
@@ -78,6 +99,7 @@
     info[5] = lengths[0] + lengths[1]
     info[6] = index // (2 * splits) * (2 * splits * rows)
     info[7] = index
+    page_windows(info, lengths, table, rows)
     row = index * rows + lax.broadcasted_iota(jnp.int32, (rows, 1), 0)
     position = (row - row_bounds(info, row)).astype(jnp.float32)
     angles = position * inverse[...]
@@ -90,28 +112,29 @@
         copy.wait()
 
 
-def load(splits, lengths, own, gain, bias, w_qkv, w_out):
+def load(splits, lengths, page_table, own, gain, bias, w_qkv, w_out):
     rows, width = own.shape
     exponent = jnp.arange(0, ROT, 2).astype(jnp.float32) / ROT
     inverse = jnp.power(jnp.float32(10000.0), -exponent)
     inverse = jnp.tile(inverse, LANES // (ROT // 2))[None, :]
     smem, here = pl.BlockSpec(memory_space=pltpu.SMEM), pl.BlockSpec(memory_space=pltpu.VMEM)
-    table = jax.ShapeDtypeStruct((rows, LANES), jnp.float32)
+    rotary = jax.ShapeDtypeStruct((rows, LANES), jnp.float32)
+    slots = rows // PAGE + 3
     wide = jax.ShapeDtypeStruct(gain.shape, jnp.float32)
     narrow = lambda *shape: jax.ShapeDtypeStruct(shape, jnp.bfloat16)
     return pl.pallas_call(
         functools.partial(load_kernel, splits),
-        in_specs=[smem] + [pl.BlockSpec(memory_space=pltpu.HBM)] * 3 + [here]
+        in_specs=[smem] * 2 + [pl.BlockSpec(memory_space=pltpu.HBM)] * 3 + [here]
         + [pl.BlockSpec(memory_space=pltpu.HBM)] * 2,
         out_specs=[smem] + [here] * 9,
         out_shape=[
-            jax.ShapeDtypeStruct((8,), jnp.int32),
+            jax.ShapeDtypeStruct((8 + 2 * slots,), jnp.int32),
             narrow(rows, width),
             wide,
             wide,
-            table,
-            table,
-            table,
+            rotary,
+            rotary,
+            rotary,
             narrow(*w_qkv.shape),
             narrow(w_out.shape[0], width),
             narrow(w_out.shape[0] // 2, width),
@@ -120,7 +143,7 @@
         compiler_params=pltpu.CompilerParams(vmem_limit_bytes=24 * 2**20),
         cost_estimate=cost(6),
         name="load",
-    )(lengths, own, gain, bias, inverse, w_qkv, w_out)
+    )(lengths, page_table, own, gain, bias, inverse, w_qkv, w_out)
 
 
 def normed_rows(info, own, other, gain, bias, normed):
@@ -142,99 +165,115 @@
         )
 
 
-def project_head(info, split, normed, keep, below, above, weights, query_ref, pair_ref):
-    head = pl.ds(pl.multiple_of((info[0] ^ split) * HD, HD), HD)
+def turned(inputs, keep, below, above):
+    leading = inputs[:, :LANES]
+    leading = (
+        leading * keep[...]
+        + pltpu.roll(leading, ROT // 2, 1) * below[...]
+        + pltpu.roll(leading, LANES - ROT // 2, 1) * above[...]
+    )
+    return jnp.concatenate([leading, inputs[:, LANES:]], axis=1).astype(jnp.bfloat16)
+
+
+def query_kernel(info, own, other, gain, bias, keep, below, above, weights, *refs):
+    queries, normed = refs[:-1], refs[-1]
+    normed_rows(info, own, other, gain, bias, normed)
     rows = normed[...]
-
-    def turned(inputs):
-        leading = inputs[:, :LANES]
-        leading = (
-            leading * keep[...]
-            + pltpu.roll(leading, ROT // 2, 1) * below[...]
-            + pltpu.roll(leading, LANES - ROT // 2, 1) * above[...]
-        )
-        return jnp.concatenate([leading, inputs[:, LANES:]], axis=1).astype(jnp.bfloat16)
-
-    def product(j):
-        return jnp.dot(rows, weights[j, :, head], preferred_element_type=jnp.float32)
-
-    pair_ref[:, :HD] = turned(product(1))
-    pair_ref[:, HD:] = product(2).astype(jnp.bfloat16)
-    query_ref[...] = turned(product(0))
-
-
-def first_kernel(
-    split, info, own, other, gain, bias, keep, below, above, weights, query, pair, normed
-):
-    normed_rows(info, own, other, gain, bias, normed)
-    project_head(info, split, normed, keep, below, above, weights, query, pair)
-
-
-def next_kernel(split, info, normed, keep, below, above, weights, query, pair):
-    project_head(info, split, normed, keep, below, above, weights, query, pair)
-
-
-def project(info, split, inputs, tables, weights, rows, features):
-    is_first = len(inputs) > 1
+    for split in reversed(range(len(queries))):
+        head = pl.ds(pl.multiple_of((info[0] ^ split) * HD, HD), HD)
+        product = jnp.dot(rows, weights[0, :, head], preferred_element_type=jnp.float32)
+        queries[split][...] = turned(product, keep, below, above)
+
+
+def pair_kernel(info, normed, keep, below, above, weights, *refs):
+    pairs, head_ref = refs[:-1], refs[-1]
+    rows = normed[...]
+    for split in reversed(range(len(pairs))):
+        head = pl.ds(pl.multiple_of((info[0] ^ split) * HD, HD), HD)
+        key = jnp.dot(rows, weights[1, :, head], preferred_element_type=jnp.float32)
+        value = jnp.dot(rows, weights[2, :, head], preferred_element_type=jnp.float32)
+        pairs[split][:, :HD] = turned(key, keep, below, above)
+        pairs[split][:, HD:] = value.astype(jnp.bfloat16)
+        head_ref[split] = pairs[split][:PAGE, :]
+
+
+def project(kernel, outs, name, microseconds, info, *operands):
     here = pl.BlockSpec(memory_space=pltpu.VMEM)
     return pl.pallas_call(
-        functools.partial(first_kernel if is_first else next_kernel, split),
-        in_specs=[pl.BlockSpec(memory_space=pltpu.SMEM)]
-        + [here] * (len(inputs) + len(tables) + 1),
-        out_specs=[here] * (2 + is_first),
-        out_shape=[
-            jax.ShapeDtypeStruct((rows, HD), jnp.bfloat16),
-            jax.ShapeDtypeStruct((rows, 2 * HD), jnp.bfloat16),
-        ]
-        + [jax.ShapeDtypeStruct((rows, features), jnp.bfloat16)] * is_first,
-        compiler_params=pltpu.CompilerParams(vmem_limit_bytes=24 * 2**20),
-        cost_estimate=cost(2.7 if is_first else 1.7),
-        name="project",
-    )(info, *inputs, *tables, weights)
-
-
-def soft_attend(query, keys, values, first_key, last_key, base):
-    scores = lax.dot_general(
+        kernel,
+        in_specs=[pl.BlockSpec(memory_space=pltpu.SMEM)] + [here] * len(operands),
+        out_specs=[here] * len(outs),
+        out_shape=[jax.ShapeDtypeStruct(shape, jnp.bfloat16) for shape in outs],
+        compiler_params=pltpu.CompilerParams(vmem_limit_bytes=16 * 2**20),
+        cost_estimate=cost(microseconds),
+        name=name,
+    )(info, *operands)
+
+
+def softmax_mix(scores, values):
+    peak = functools.reduce(
+        jnp.maximum, [jnp.max(part, axis=-1, keepdims=True) for part in scores]
+    )
+    factor = LOG2E / math.sqrt(HD)
+    total, mixed = 0.0, 0.0
+    for part, value in zip(scores, values):
+        weights = jnp.exp2((part - peak) * factor)
+        total += jnp.sum(weights, axis=-1, keepdims=True)
+        mixed += jnp.dot(
+            weights.astype(jnp.bfloat16), value[...], preferred_element_type=jnp.float32
+        )
+    return mixed / total, peak * factor + jnp.log2(total)
+
+
+def score(query, keys):
+    return lax.dot_general(
         query, keys, (((1,), (1,)), ((), ())), preferred_element_type=jnp.float32
     )
-    column = base + lax.broadcasted_iota(jnp.int32, scores.shape, 1)
-    visible = (column >= first_key) & (column <= last_key)
-    scores = jnp.where(visible, scores, MASKED)
-    peak = jnp.max(scores, axis=-1, keepdims=True)
-    factor = LOG2E / math.sqrt(HD)
-    weights = jnp.exp2((scores - peak) * factor).astype(jnp.bfloat16)
-    total = jnp.sum(weights.astype(jnp.float32), axis=-1, keepdims=True)
-    mixed = jnp.dot(weights, values, preferred_element_type=jnp.float32) / total
-    return mixed, peak * factor + jnp.log2(total)
-
-
-def fetch_pairs(info, mine, theirs, pairs, sems):
-    rows = mine[0].shape[0]
-    copies = []
-    for refs, core in ((mine, info[2]), (theirs, 1 - info[2])):
-        for split, ref in enumerate(refs):
-            at = pl.ds(pl.multiple_of((2 * (info[0] ^ split) + core) * rows, rows), rows)
-            copies.append(pltpu.make_async_copy(ref, pairs.at[at, :], sems.at[len(copies)]))
-    for copy in copies:
-        copy.start()
-    return copies
+
+
+def soft_attend(query, pairs, reach, bounded, causal, base, first_key, last_key):
+    cuts = sorted({0, min(bounded, reach), reach - causal, reach})
+    scores, values = [], []
+    for low, high in zip(cuts, cuts[1:]):
+        part = score(query, pairs[low:high, :HD])
+        if low < bounded or high > reach - causal:
+            column = base + low + lax.broadcasted_iota(jnp.int32, part.shape, 1)
+            visible = column >= first_key if low < bounded else column <= last_key
+            if low < bounded and high > reach - causal:
+                visible = visible & (column <= last_key)
+            part = jnp.where(visible, part, MASKED)
+        scores.append(part)
+        values.append(pairs.at[low:high, HD:])
+    return softmax_mix(scores, values)
+
+
+def pick_kernel(info, *refs):
+    for split, ref in enumerate(refs[:-1]):
+
+        @pl.when(info[0] == split)
+        def _():
+            refs[-1][...] = ref[...]
 
 
 def tail_kernel(info, *refs):
-    splits = (len(refs) - 4) // 2
-    query, mine, theirs = refs[0], refs[1 : splits + 1], refs[splits + 1 : 2 * splits + 1]
-    out, pairs, sems = refs[2 * splits + 1 :]
+    splits = (len(refs) - 2) // 2
+    query_ref, out = refs[0], refs[-1]
+    mine, theirs = refs[1 : splits + 1], refs[splits + 1 : 2 * splits + 1]
     rows = out.shape[0]
 
     @pl.when((info[6] == 0) & (info[2] == 0))
     def _():
-        copies = fetch_pairs(info, mine, theirs, pairs, sems)
-        for copy in copies:
-            copy.wait()
+        query = query_ref[...]
         group_rows = 2 * splits * rows
         row = group_rows + lax.broadcasted_iota(jnp.int32, (rows, 1), 0)
         first = row_bounds(info, row)
-        mixed, level = soft_attend(query[...], pairs[:, :HD], pairs[:, HD:], first, row, 0)
+        scores = []
+        for split in range(splits):
+            part = score(query, mine[split][:, :HD])
+            column = 2 * (info[0] ^ split) * rows + lax.broadcasted_iota(jnp.int32, part.shape, 1)
+            scores.append(jnp.where(column >= first, part, MASKED))
+        scores += [score(query, ref[:, :HD]) for ref in theirs]
+        mixed, level = softmax_mix(scores, [ref.at[:, HD:] for ref in (*mine, *theirs)])
         level = jnp.where(first < group_rows, level, MASKED)
         out[:, :HD] = mixed.astype(jnp.bfloat16)
         lane = lax.broadcasted_iota(jnp.int32, (rows, LANES), 1)
@@ -251,26 +290,33 @@
     queries, mine, theirs = refs[:splits], refs[splits : 2 * splits], refs[2 * splits : 3 * splits]
     gathered, near_mixed, near_level, pairs, asked, sems = refs[3 * splits :]
     rows = near_mixed.shape[0]
-    copies = fetch_pairs(info, mine, theirs, pairs, sems)
+
+    def at(block):
+        return pl.ds(pl.multiple_of(block * rows, rows), rows)
+
+    def fetch(ref, target, block, sem):
+        return pltpu.make_async_copy(ref, target.at[at(block), :], sems.at[sem])
+
     for split in range(splits):
-        at = pl.ds(pl.multiple_of((info[0] ^ split) * rows, rows), rows)
-        copies.append(
-            pltpu.make_async_copy(queries[split], asked.at[at, :], sems.at[len(copies)])
-        )
-        copies[-1].start()
-    for copy in copies:
-        copy.wait()
+        place = info[0] ^ split
+        fetch(queries[split], asked, place, 2 * splits + place).start()
+        for refs_of, core in ((mine, info[2]), (theirs, 1 - info[2])):
+            fetch(refs_of[split], pairs, 2 * place + core, 2 * place + core).start()
     for place in range(splits):
-        reach = (2 * place + 2) * rows
+        fetch(queries[0], asked, place, 2 * splits + place).wait()
+        for block in (2 * place, 2 * place + 1):
+            fetch(mine[0], pairs, block, block).wait()
         row = info[6] + (2 * place + info[2]) * rows + lax.broadcasted_iota(jnp.int32, (rows, 1), 0)
         here = slice(place * rows, (place + 1) * rows)
         mixed, level = soft_attend(
             asked[here, :],
-            pairs[:reach, :HD],
-            pairs[:reach, HD:],
+            pairs,
+            (2 * place + 2) * rows,
+            rows,
+            2 * rows,
+            info[6],
             row_bounds(info, row),
             row,
-            info[6],
         )
         gathered[here, :] = mixed.astype(jnp.bfloat16)
         if place == 0:
@@ -302,116 +348,104 @@
                 out[...] = mixed
 
 
-def page_windows(info, lengths, table, firsts, counts, rows, page):
-    slots = firsts.shape[0]
+def page_rows(rows, first, count, page):
+    target = lax.broadcasted_iota(jnp.int32, (page, rows), 0)
+    origin = lax.broadcasted_iota(jnp.int32, (page, rows), 1)
+    return ((origin == target + first) & (target < count)).astype(jnp.bfloat16)
+
+
+def put_window(out, mixed, slot, column, window):
+    page = window.shape[0]
+    for number, low in enumerate(range(0, HD, LANES)):
+        turn = mixed.at[slot, number]
+        turn[pl.ds(0, page, stride=2), :] = window[:, low : low + LANES]
+        turn[pl.ds(1, page, stride=2), :] = window[:, HD + low : HD + low + LANES]
+        out[slot, :, :, pl.ds(column + low, LANES)] = (
+            turn[...].astype(jnp.bfloat16).reshape(page, 2, LANES)
+        )
+
+
+def page_kernel(info, *refs):
+    splits = len(refs) - 2
+    pairs, (out, mixed) = refs[:splits], refs[splits:]
+    slots, page = out.shape[:2]
+    for number in range(splits):
+
+        @pl.when(pl.program_id(0) == number)
+        def _():
+            source = pairs[number][...]
+            taken = [
+                page_rows(source.shape[0], info[8 + slot], info[8 + slots + slot], page)
+                for slot in range(slots)
+            ]
+            windows = jnp.dot(jnp.concatenate(taken), source, preferred_element_type=jnp.float32)
+            for slot in range(slots):
+                put_window(out, mixed, slot, 0, windows[slot * page : (slot + 1) * page])
+
+
+def crossing_kernel(info, *refs):
+    splits = len(refs) - 6
+    pairs, (following, _, out, block, mixed, sem) = refs[:splits], refs[splits:]
+    rows, page = pairs[0].shape[0], block.shape[1]
+    slots = out.shape[0]
+    following_place = (info[7] + 1) // 2 % splits
     for slot in range(slots):
-        firsts[slot] = 0
-        counts[slot] = 0
-    for prompt in range(table.shape[0]):
-
-        def visit(j, carry):
-            slot = table[prompt, j] - info[7] * slots
-            left = lengths[prompt] - j * page
-
-            @pl.when((slot >= 0) & (slot < slots) & (left > 0))
-            def _():
-                firsts[slot] = info[3 + prompt] + j * page - info[7] * rows
-                counts[slot] = jnp.minimum(left, page)
-
-            return carry
-
-        lax.fori_loop(0, table.shape[1], visit, 0)
-
-
-def page_window(source, first, count, page):
-    target = lax.broadcasted_iota(jnp.int32, (page, source.shape[0]), 0)
-    origin = lax.broadcasted_iota(jnp.int32, (page, source.shape[0]), 1)
-    taken = (origin == target + first) & (target < count)
-    window = jnp.dot(taken.astype(jnp.bfloat16), source, preferred_element_type=jnp.float32)
-    return jnp.stack([window[:, :HD], window[:, HD:]], axis=1).astype(jnp.bfloat16)
-
-
-def page_kernel(parts, has_written, info, lengths, table, *refs):
-    pairs, (out, firsts, counts) = refs[: len(parts)], refs[len(parts) + has_written :]
-    step = pl.program_id(0)
-    slots, page = out.shape[:2]
-
-    @pl.when(step == 0)
-    def _():
-        page_windows(info, lengths, table, firsts, counts, pairs[0].shape[0], page)
-
-    for number in range(len(parts)):
-
-        @pl.when(step == number)
+        first, count = info[8 + slot], info[8 + slots + slot]
+
+        @pl.when(first + count > rows)
         def _():
-            for slot in range(slots):
-                out[slot] = page_window(pairs[number][...], firsts[slot], counts[slot], page)
-
-
-def crossing_kernel(info, lengths, table, *refs):
-    splits = len(refs) - 7
-    pairs, (following, _, out, block, firsts, counts, sem) = refs[:splits], refs[splits:]
-    rows, page = pairs[0].shape[0], block.shape[0]
-    page_windows(info, lengths, table, firsts, counts, rows, page)
-    following_place = (info[7] + 1) // 2 % splits
-    for slot in range(out.shape[0]):
-
-        @pl.when(firsts[slot] + counts[slot] > rows)
-        def _():
+            taken = page_rows(rows + page, first, count, page)
             for split in range(splits):
                 beyond = following[info[0] ^ split ^ following_place]
                 source = jnp.concatenate([pairs[split][...], beyond], axis=0)
-                columns = pl.ds(pl.multiple_of((info[0] ^ split) * HD, HD), HD)
-                block[:, :, columns] = page_window(source, firsts[slot], counts[slot], page)
-            copy = pltpu.make_async_copy(block, out.at[slot], sem)
+                window = jnp.dot(taken, source, preferred_element_type=jnp.float32)
+                put_window(block, mixed, 0, pl.multiple_of((info[0] ^ split) * HD, HD), window)
+            copy = pltpu.make_async_copy(block.at[0], out.at[slot], sem)
             copy.start()
             copy.wait()
 
 
-def write_pages(info, lengths, table, pairs, parts, *written):
+def write_pages(info, pairs):
     rows = pairs[0].shape[0]
+    splits = len(pairs)
     slots = rows // PAGE + 3
     return pl.pallas_call(
-        functools.partial(page_kernel, parts, len(written)),
+        page_kernel,
         grid_spec=pltpu.PrefetchScalarGridSpec(
-            num_scalar_prefetch=3,
-            grid=(len(parts),),
-            in_specs=[pl.BlockSpec((rows, 2 * HD), lambda m, *_: (0, 0))] * len(parts)
-            + [pl.BlockSpec(memory_space=pl.ANY)] * len(written),
+            num_scalar_prefetch=1,
+            grid=(splits,),
+            in_specs=[pl.BlockSpec((rows, 2 * HD), lambda m, *_: (0, 0))] * splits,
             out_specs=pl.BlockSpec(
-                (slots, PAGE, 2, HD), lambda m, info, *_: (0, 0, 0, info[0] ^ (m + parts[0]))
+                (slots, PAGE, 2, HD), lambda m, info: (0, 0, 0, info[0] ^ m)
             ),
-            scratch_shapes=[pltpu.SMEM((slots,), jnp.int32)] * 2,
+            scratch_shapes=[VMEM((slots, HD // LANES, 2 * PAGE, LANES), jnp.float32)],
         ),
-        out_shape=jax.ShapeDtypeStruct((slots, PAGE, 2, len(pairs) * HD), jnp.bfloat16),
-        input_output_aliases={3 + len(parts): 0} if written else {},
-        compiler_params=pltpu.CompilerParams(vmem_limit_bytes=24 * 2**20),
-        cost_estimate=cost(1.8 * len(parts)),
+        out_shape=jax.ShapeDtypeStruct((slots, PAGE, 2, splits * HD), jnp.bfloat16),
+        compiler_params=pltpu.CompilerParams(vmem_limit_bytes=16 * 2**20),
+        cost_estimate=cost(0.3),
         name="pages",
-    )(info, lengths, table, *[pairs[part] for part in parts], *written)
-
-
-def cross_pages(info, lengths, table, pairs, following, written):
+    )(info, *pairs)
+
+
+def cross_pages(info, pairs, following, written):
     splits = len(pairs)
-    slots = written.shape[0]
     smem, here = pl.BlockSpec(memory_space=pltpu.SMEM), pl.BlockSpec(memory_space=pltpu.VMEM)
     anywhere = pl.BlockSpec(memory_space=pl.ANY)
     return pl.pallas_call(
         crossing_kernel,
-        in_specs=[smem] * 3 + [here] * (splits + 1) + [anywhere],
+        in_specs=[smem] + [here] * (splits + 1) + [anywhere],
         out_specs=anywhere,
         out_shape=jax.ShapeDtypeStruct(written.shape, written.dtype),
-        input_output_aliases={splits + 4: 0},
+        input_output_aliases={splits + 2: 0},
         scratch_shapes=[
-            VMEM(written.shape[1:], written.dtype),
-            pltpu.SMEM((slots,), jnp.int32),
-            pltpu.SMEM((slots,), jnp.int32),
+            VMEM((1, *written.shape[1:]), written.dtype),
+            VMEM((1, HD // LANES, 2 * PAGE, LANES), jnp.float32),
             pltpu.SemaphoreType.DMA,
         ],
-        compiler_params=pltpu.CompilerParams(vmem_limit_bytes=24 * 2**20),
-        cost_estimate=cost(3),
+        compiler_params=pltpu.CompilerParams(vmem_limit_bytes=16 * 2**20),
+        cost_estimate=cost(1.5),
         name="crossing",
-    )(info, lengths, table, *pairs, following, written)
+    )(info, *pairs, following, written)
 
 
 def on_core(kernel, out_shape, scratch, name, microseconds, direct):
@@ -431,7 +465,7 @@
                 scratch_shapes=scratch,
             ),
             out_shape=out_shape,
-            compiler_params=pltpu.CompilerParams(vmem_limit_bytes=24 * 2**20),
+            compiler_params=pltpu.CompilerParams(vmem_limit_bytes=16 * 2**20),
             cost_estimate=cost(microseconds),
             name=name,
         )(info, *operands)
@@ -439,30 +473,52 @@
     return call
 
 
-def out_kernel(info, *refs):
-    splits = (len(refs) - 4) // 2
-    mine, theirs = refs[:splits], refs[splits : 2 * splits]
-    w_own, w_same, w_swap, out = refs[2 * splits :]
-    half = splits // 2
+def out_own_kernel(info, *refs):
+    splits = len(refs) - 2
+    blocks, (w_own, out) = refs[:splits], refs[splits:]
     total = jnp.zeros(out.shape, jnp.float32)
     for split in range(splits):
-        head = info[0] ^ split
-        at = pl.ds(pl.multiple_of(head * HD, HD), HD)
-        total += jnp.dot(mine[split][...], w_own[at, :], preferred_element_type=jnp.float32)
-    for split in range(splits):
-        head = info[0] ^ split
-        at = pl.ds(pl.multiple_of(lax.rem(head, half) * HD, HD), HD)
-        same = head // half == info[2]
-        weight = jnp.where(same, w_same[at, :], w_swap[at, :])
-        total += jnp.dot(theirs[split][...], weight, preferred_element_type=jnp.float32)
+        at = pl.ds(pl.multiple_of((info[0] ^ split) * HD, HD), HD)
+        total += jnp.dot(blocks[split][...], w_own[at, :], preferred_element_type=jnp.float32)
+    out[...] = total
+
+
+def out_theirs_kernel(info, *refs):
+    splits = len(refs) - 4
+    blocks, (w_same, w_swap, ours, out) = refs[:splits], refs[splits:]
+    half = splits // 2
+    total = ours[...]
+    for weight, core in ((w_same, info[2]), (w_swap, 1 - info[2])):
+        for number in range(half):
+            split = info[0] ^ (core * half + number)
+            block = blocks[0][...]
+            for other in range(1, splits):
+                block = jnp.where(split == other, blocks[other][...], block)
+            total += jnp.dot(
+                block,
+                weight[number * HD : (number + 1) * HD, :],
+                preferred_element_type=jnp.float32,
+            )
     out[...] = total.astype(jnp.bfloat16)
+
+
+def on_chip(kernel, out, name, microseconds):
+    here = pl.BlockSpec(memory_space=pltpu.VMEM)
+    return lambda info, *operands: pl.pallas_call(
+        kernel,
+        in_specs=[pl.BlockSpec(memory_space=pltpu.SMEM)] + [here] * len(operands),
+        out_specs=here,
+        out_shape=out,
+        compiler_params=pltpu.CompilerParams(vmem_limit_bytes=16 * 2**20),
+        cost_estimate=cost(microseconds),
+        name=name,
+    )(info, *operands)
 
 
 def split_heads(hidden_in, ln_gain, ln_bias, w_qkv, w_out, segment_ids, prompt_lengths, page_table):
     rows, width = hidden_in.shape
     splits = w_out.shape[0] // HD
     count = lax.axis_size("ctx")
-    place = lax.axis_index("ctx") // 2 % splits
     group = 2 * splits
 
     def across(value, ctx_mask, tp_mask=0):
@@ -474,15 +530,31 @@
 
     other = across(hidden_in, 0, 1)
     info, own, gain, bias, *tables, weights, own_columns, outgoing = load(
-        splits, prompt_lengths, hidden_in, ln_gain[None, :], ln_bias[None, :], w_qkv, w_out
-    )
-    inputs = (own, other, gain, bias)
-    queries, pairs = [None] * splits, [None] * splits
-    for split in reversed(range(splits)):
-        made = project(info, split, inputs, tables, weights, rows, 2 * width)
-        queries[split], pairs[split] = made[:2]
-        if len(made) > 2:
-            inputs = (made[2],)
+        splits, prompt_lengths, page_table, hidden_in, ln_gain[None, :], ln_bias[None, :], w_qkv, w_out
+    )
+    *queries, normed = project(
+        query_kernel,
+        [(rows, HD)] * splits + [(rows, 2 * width)],
+        "queries",
+        3.5,
+        info,
+        own,
+        other,
+        gain,
+        bias,
+        *tables,
+        weights,
+    )
+    *pairs, page_head = project(
+        pair_kernel,
+        [(rows, 2 * HD)] * splits + [(splits, PAGE, 2 * HD)],
+        "pairs",
+        6,
+        info,
+        normed,
+        *tables,
+        weights,
+    )
 
     def after(value, *others):
         return lax.optimization_barrier((value, *others))[0]
@@ -492,30 +564,21 @@
     for split in reversed(range(1, splits)):
         q_mine[split] = across(queries[split], 2 * split)
     for split in reversed(range(1, splits)):
-        kv_mine[split] = across(after(pairs[split], pairs[0]), 2 * split)
-    w_same = across(after(outgoing, pairs[0]), 0, 1)
-    pages = functools.partial(write_pages, info, prompt_lengths, page_table, pairs)
-    half_written = pages(range(splits // 2))
-    *q_mine[1:], half_written = lax.optimization_barrier((*q_mine[1:], half_written))
-    q_first = q_mine[0]
-    for split in range(1, splits):
-        q_first = jnp.where(place == split, q_mine[split], q_first)
+        kv_mine[split] = across(pairs[split], 2 * split)
+    q_first = on_chip(pick_kernel, jax.ShapeDtypeStruct((rows, HD), jnp.bfloat16), "pick", 0.3)(
+        info, *q_mine
+    )
     q_tail = lax.ppermute(q_first, "ctx", [(group + 2 * s, 2 * s) for s in range(splits)])
-    *kv_mine[1:], q_tail = lax.optimization_barrier((*kv_mine[1:], q_tail))
+    kv_cache = write_pages(after(info, q_first), pairs)
+    *kv_mine[1:], q_tail, kv_cache = lax.optimization_barrier((*kv_mine[1:], q_tail, kv_cache))
     kv_theirs = [across(kv_mine[split], 1) for split in range(splits)]
-
-    keep_pairs = VMEM((group * rows, 2 * HD), jnp.bfloat16)
-    block = jax.ShapeDtypeStruct((rows, HD), jnp.bfloat16)
-    (tail,) = on_core(
-        tail_kernel,
-        [jax.ShapeDtypeStruct((rows, HD + LANES), jnp.bfloat16)],
-        [keep_pairs, pltpu.SemaphoreType.DMA((group,))],
-        "tail",
-        2.7,
-        range(1, 2 * splits + 1),
-    )(info, q_tail, *kv_mine, *kv_theirs)
+    w_same = across(after(outgoing, normed), 0, 1)
+
+    tail = on_chip(
+        tail_kernel, jax.ShapeDtypeStruct((rows, HD + LANES), jnp.bfloat16), "tail", 2.7
+    )(after(info, kv_cache), q_tail, *kv_mine, *kv_theirs)
+    w_swap = across(after(w_same, tail), 1)
     far = lax.ppermute(tail, "ctx", [(2 * s, group + 2 * s) for s in range(splits)])
-    page_head = jnp.stack([pair[:PAGE] for pair in pairs])
     page_head = after(page_head, tail)
     following = lax.ppermute(page_head, "ctx", [(i, i - 1) for i in range(1, count)])
     gathered, near_mixed, near_level = on_core(
@@ -526,7 +589,7 @@
             jax.ShapeDtypeStruct((rows, LANES), jnp.float32),
         ],
         [
-            keep_pairs,
+            VMEM((group * rows, 2 * HD), jnp.bfloat16),
             VMEM((splits * rows, HD), jnp.bfloat16),
             pltpu.SemaphoreType.DMA((group + splits,)),
         ],
@@ -534,26 +597,19 @@
         4.8,
         range(3 * splits),
     )(after(info, tail), *q_mine, *kv_mine, *kv_theirs)
-    kv_cache = pages(range(splits // 2, splits), after(half_written, gathered, following))
+    block = jax.ShapeDtypeStruct((rows, HD), jnp.bfloat16)
     blocks = on_core(merge_kernel, [block] * splits, [], "merge", 0.6, ())(
-        info, gathered, near_mixed, near_level, after(far, kv_cache)
-    )
-    w_swap = across(after(w_same, blocks[0]), 1)
+        after(info, w_swap), gathered, near_mixed, near_level, far
+    )
+    near = [blocks[0]] + [across(blocks[s], 2 * s) for s in range(1, splits)]
     beyond = [across(blocks[s], 2 * s, 1) for s in range(splits)]
-    kv_cache = cross_pages(
-        after(info, blocks[0]), prompt_lengths, page_table, pairs, following, kv_cache
-    )
-    near = [blocks[0]] + [across(after(blocks[s], kv_cache), 2 * s) for s in range(1, splits)]
-    here = pl.BlockSpec(memory_space=pltpu.VMEM)
-    operands = [*near, *beyond, own_columns, w_same, w_swap]
-    attn_out = pl.pallas_call(
-        out_kernel,
-        in_specs=[pl.BlockSpec(memory_space=pltpu.SMEM)] + [here] * len(operands),
-        out_shape=jax.ShapeDtypeStruct((rows, width), jnp.bfloat16),
-        compiler_params=pltpu.CompilerParams(vmem_limit_bytes=24 * 2**20),
-        cost_estimate=cost(2.7),
-        name="out",
-    )(info, *operands)
+    kv_cache = cross_pages(after(info, blocks[0]), pairs, following, kv_cache)
+    ours = on_chip(
+        out_own_kernel, jax.ShapeDtypeStruct((rows, width), jnp.float32), "out_own", 1.4
+    )(info, *near, own_columns)
+    attn_out = on_chip(
+        out_theirs_kernel, jax.ShapeDtypeStruct((rows, width), jnp.bfloat16), "out_theirs", 2
+    )(info, *beyond, w_same, w_swap, ours)
     return attn_out, kv_cache
 
 

time: 93 us -> 76.5 us (0.82)
  waiting for transfers between devices: 20.6 us -> 8.4 us
  Pallas kernels: 35.9 us -> 30.1 us
  starting transfers between devices: 29.8 us -> 30.8 us
    ppermute x20, waiting for transfers between devices: 17.1 us -> 8.4 us  [across(): return lax.ppermute(value, ('ctx', 'tp'), pairs)]
    ppermute x1, starting transfers between devices: 1.85 us -> 6.85 us  [split_heads(): lax.ppermute(tail, 'ctx', [(2 * s, group + 2 * s) for s in range(splits)])]
    pallas_call x9, Pallas kernels: 27.9 us -> 23.9 us  [the longest x2 5.96 us: project(): pl.pallas_call(kernel, in_specs=[pl.BlockSpec(memory_space=pltpu.SMEM)] +...]
    ppermute x20, starting transfers between devices: 25.4 us -> 21.4 us  [across(): return lax.ppermute(value, ('ctx', 'tp'), pairs)]
    ppermute x1, waiting for transfers between devices: 3.44 us -> 0.01 us  [split_heads(): lax.ppermute(q_first, 'ctx', [(group + 2 * s, 2 * s) for s in range(split...]
    pallas_call x3 -> x2, Pallas kernels: 8.02 us -> 6.19 us  [call(): pl.pallas_call(kernel, grid_spec=pltpu.PrefetchScalarGridSpec(num_scalar_...]
  transfers between devices with their start and end apart: 23 -> 23, of which waited for: 10 -> 10; matrix products, arithmetic and copies ran while one was open for 0% -> 0% of each run, Pallas kernels for 28% -> 33%
where the time goes in v3:
time: 76.5 us; the launch traced here: 76.1 us
  starting transfers between devices  30.8 us (40%)
  Pallas kernels  30.1 us (39%)
  waiting for transfers between devices  8.4 us (11%)
  local copies, waits for them, and re-layouts  6.05 us (8%)
  between operations  0.8 us (1%)
    ppermute x20, starting transfers between devices, across(): return lax.ppermute(value, ('ctx', 'tp'), pairs)  21.4 us
    ppermute x20, waiting for transfers between devices, across(): return lax.ppermute(value, ('ctx', 'tp'), pairs)  8.4 us
    ppermute x1, starting transfers between devices, split_heads(): lax.ppermute(tail, 'ctx', [(2 * s, group + 2 * s) for s in range(splits)])  6.85 us
    pallas_call x2, Pallas kernels, call(): pl.pallas_call(kernel, grid_spec=pltpu.PrefetchScalarGridSpec(num_scalar_...  6.19 us
    unnamed x12, local copies, waits for them, and re-layouts  5.96 us
    pallas_call x2, Pallas kernels, project(): pl.pallas_call(kernel, in_specs=[pl.BlockSpec(memory_space=pltpu.SMEM)] +...  5.96 us
    pallas_call x4, Pallas kernels, on_chip(): pl.pallas_call(kernel, in_specs=[pl.BlockSpec(memory_space=pltpu.SMEM)] +...  5.91 us
    pallas_call x1, Pallas kernels, load(): pl.pallas_call(functools.partial(load_kernel, splits), in_specs=[smem] *...  5.86 us
  transfers between devices with their start and end apart: 23, of which 10 were waited for; matrix products, arithmetic and copies ran while one was open for 0% of the time, Pallas kernels for 33%

profile of v3, /device:TPU:0, one launch (start us, length us, event | category | flops | bytes accessed | tf_op | source)
XLA Modules:
  0.0 76.1 jit_solution(5372204222319341493)
XLA Ops:
  0.6 3.0 %collective-permute-start = (bf16[256,1024]{1,0:T(8,128)(2,1)}, bf16[256,1024]{1,0:T(8,128)(2,1)S(1)}, u32[]{:S(2)}, u32[]{:S(2)}) collective-permute-start(bf16[256,1024]{1,0:T(8,128)(2,1)} %own.1), channel_id=1, source_target_pairs={{0,1},{1,0},{2,3},{3,2},{4,5},{5,4},{6,7},{7,6},{8,9},{9,8},{10,11... | collective-permute-start | bytes 1572872 | tf_op jit(solution)/shard_map/ppermute | solution.py:529
  3.7 2.2 %copy-done = bf16[1024,2048]{1,0:T(8,128)(2,1)S(1)} copy-done((bf16[1024,2048]{1,0:T(8,128)(2,1)S(1)}, bf16[1024,2048]{1,0:T(8,128)(2,1)}, u32[]{:S(2)}) %copy-start) | copy-done | bytes 4194328
  5.9 1.0 %copy-done.1 = bf16[256,1024]{1,0:T(8,128)(2,1)S(1)} copy-done((bf16[256,1024]{1,0:T(8,128)(2,1)S(1)}, bf16[256,1024]{1,0:T(8,128)(2,1)}, u32[]{:S(2)}) %copy-start.1) | copy-done | bytes 524312
  7.0 0.7 copy-done.2
  7.7 0.7 copy-done.3
  8.4 0.7 copy-done.4
  9.0 0.7 copy-done.5
  9.7 5.9 %load.1 = (s32[18]{0:T(128)S(1)}, bf16[256,1024]{1,0:T(8,128)(2,1)S(1)}, f32[1,2048]{1,0:T(1,128)S(1)}, f32[1,2048]{1,0:T(1,128)S(1)}, f32[256,128]{1,0:T(8,128)...) custom-call(s32[3]{0:T(128)S(1)} %copy-done.5, ...), custom_call_target="tpu_custom_call" | custom-call | flops 2100000000 | tf_op jit(solution)/shard_map/load/pallas_call | solution.py:125
  15.8 2.9 %queries.1 = (bf16[256,256]{1,0:T(8,128)(2,1)S(1)}, bf16[256,256]{1,0:T(8,128)(2,1)S(1)}, bf16[256,256]{1,0:T(8,128)(2,1)S(1)}, bf16[256,256]{1,0:T(8,128)(2,1)S(1)}, bf16[256,2048]{1,0:T(8,128)(2,1)S(1)}) custom-call(s32[18]{0:T(128)S(1)} %get-tuple-element.79.info, bf16[256,1024]{1,0:T(8,128)(2,1)S(1)} %get-tuple-element.44.own, ...), custom_call_target="tpu_custom_call" | custom-call | flops 1224999936 | tf_op jit(solution)/shard_map/queries/pallas_call | solution.py:202
  18.7 1.8 %collective-permute-start.1 = (bf16[512,1024]{1,0:T(8,128)(2,1)S(1)}, bf16[512,1024]{1,0:T(8,128)(2,1)S(1)}, u32[]{:S(2)}, u32[]{:S(2)}) collective-permute-start(bf16[512,1024]{1,0:T(8,128)(2,1)S(1)} %get-tuple-element.52), channel_id=1, source_target_pairs={{0,1},{1,0},{2,3},{3,2},{4,5},{5,4},{6,7},{7,6},{8,9},{9,8},{10,11... | collective-permute-start | bytes 3145736 | tf_op jit(solution)/shard_map/ppermute | solution.py:529
  20.5 1.5 %collective-permute-start.5 = (bf16[256,256]{1,0:T(8,128)(2,1)S(1)}, bf16[256,256]{1,0:T(8,128)(2,1)S(1)}, u32[]{:S(2)}, u32[]{:S(2)}) collective-permute-start(bf16[256,256]{1,0:T(8,128)(2,1)S(1)} %get-tuple-element.57), channel_id=1, source_target_pairs={{0,4},{1,5},{2,6},{3,7},{4,0},{5,1},{6,2},{7,3},{8,12},{9,13},{10,... | collective-permute-start | bytes 393224 | tf_op jit(solution)/shard_map/ppermute | solution.py:529
  22.0 1.6 %collective-permute-start.6 = (bf16[256,256]{1,0:T(8,128)(2,1)S(1)}, bf16[256,256]{1,0:T(8,128)(2,1)S(1)}, u32[]{:S(2)}, u32[]{:S(2)}) collective-permute-start(bf16[256,256]{1,0:T(8,128)(2,1)S(1)} %get-tuple-element.58), channel_id=1, source_target_pairs={{0,8},{1,9},{2,10},{3,11},{4,12},{5,13},{6,14},{7,15},{8,0},{9,1},... | collective-permute-start | bytes 393224 | tf_op jit(solution)/shard_map/ppermute | solution.py:529
  24.0 3.1 %pairs.1 = (bf16[256,512]{1,0:T(8,128)(2,1)S(1)}, bf16[256,512]{1,0:T(8,128)(2,1)S(1)}, bf16[256,512]{1,0:T(8,128)(2,1)S(1)}, bf16[256,512]{1,0:T(8,128)(2,1)S(1)}, bf16[4,128,512]{2,1,0:T(8,128)(2,1)S(1)}) custom-call(s32[18]{0:T(128)S(1)} %get-tuple-element.79.info, bf16[256,2048]{1,0:T(8,128)(2,1)S(1)} %get-tuple-element.51.normed, ...), custom_call_target="tpu_custom_call" | custom-call | flops 2100000000 | tf_op jit(solution)/shard_map/pairs/pallas_call | solution.py:202
  27.0 1.6 %collective-permute-start.2 = (bf16[256,512]{1,0:T(8,128)(2,1)S(1)}, bf16[256,512]{1,0:T(8,128)(2,1)S(1)}, u32[]{:S(2)}, u32[]{:S(2)}) collective-permute-start(bf16[256,512]{1,0:T(8,128)(2,1)S(1)} %get-tuple-element.53.refs_1_), channel_id=1, source_target_pairs={{0,4},{1,5},{2,6},{3,7},{4,0},{5,1},{6,2},{7,3},{8,12},{9,13},{10,... | collective-permute-start | bytes 786440 | tf_op jit(solution)/shard_map/ppermute | solution.py:529
  28.6 1.6 %collective-permute-start.3 = (bf16[256,512]{1,0:T(8,128)(2,1)S(1)}, bf16[256,512]{1,0:T(8,128)(2,1)S(1)}, u32[]{:S(2)}, u32[]{:S(2)}) collective-permute-start(bf16[256,512]{1,0:T(8,128)(2,1)S(1)} %get-tuple-element.54.refs_2_), channel_id=1, source_target_pairs={{0,8},{1,9},{2,10},{3,11},{4,12},{5,13},{6,14},{7,15},{8,0},{9,1},... | collective-permute-start | bytes 786440 | tf_op jit(solution)/shard_map/ppermute | solution.py:529
  30.6 0.6 pick.1
  31.2 1.3 %collective-permute-start.8 = (bf16[256,256]{1,0:T(8,128)(2,1)S(1)}, bf16[256,256]{1,0:T(8,128)(2,1)S(1)}, u32[]{:S(2)}, u32[]{:S(2)}) collective-permute-start(bf16[256,256]{1,0:T(8,128)(2,1)S(1)} %pick.1), channel_id=1, source_target_pairs={{16,0},{20,4},{24,8},{28,12},{17,1},{21,5},{25,9},{29,13}} | collective-permute-start | bytes 393224 | tf_op jit(solution)/shard_map/ppermute | solution.py:571
  32.5 4.1 %pages.1.refs_5_ = bf16[5,128,2,1024]{3,2,1,0:T(2,128)(2,1)} custom-call(s32[18]{0:T(128)S(1)} %get-tuple-element.79.info, bf16[256,512]{1,0:T(8,128)(2,1)S(1)} %get-tuple-element.61.refs_0_.refs_1_.refs_4_, bf16[256,512]{1,0:T(8,128)(2,1)S(1)} %get-tuple-element.53.refs_1_, bf16[256,512]{1,0:T(8,128)(2,1)S(1)} %get-tuple-element.54.refs_2_, ...), custom_call_target="tpu_custom_call" | custom-call | flops 105000000 | tf_op jit(solution)/shard_map/pages/pallas_call | solution.py:412
  37.2 4.9 %collective-permute-done.4.refs_4_.refs_7_ = bf16[256,512]{1,0:T(8,128)(2,1)S(1)} collective-permute-done((bf16[256,512]{1,0:T(8,128)(2,1)S(1)}, bf16[256,512]{1,0:T(8,128)(2,1)S(1)}, u32[]{:S(2)}, u32[]{:S(2)}) %collective-permute-start.4) | collective-permute-done | bytes 262176 | tf_op jit(solution)/shard_map/ppermute | solution.py:529
  42.6 1.0 %collective-permute-done.10.refs_6_.refs_9_ = bf16[256,512]{1,0:T(8,128)(2,1)S(1)} collective-permute-done((bf16[256,512]{1,0:T(8,128)(2,1)S(1)}, bf16[256,512]{1,0:T(8,128)(2,1)S(1)}, u32[]{:S(2)}, u32[]{:S(2)}) %collective-permute-start.10) | collective-permute-done | bytes 262176 | tf_op jit(solution)/shard_map/ppermute | solution.py:529
  44.4 2.0 %tail.1 = bf16[256,384]{1,0:T(8,128)(2,1)S(1)} custom-call(s32[18]{0:T(128)S(1)} %get-tuple-element.79.info, bf16[256,256]{1,0:T(8,128)(2,1)S(1)} %collective-permute-done.8.refs_0_, bf16[256,512]{1,0:T(8,128)(2,1)S(1)} %get-tuple-element.61.refs_0_.refs_1_.refs_4_, bf16[256,512]{1,0:T(8,128)(2,1)S(1)} %collective-permute-done.2.refs_2_.refs_5_, ...), custom_call_target="tpu_custom_call" | custom-call | flops 945000000 | tf_op jit(solution)/shard_map/tail/pallas_call | solution.py:507
  46.5 1.3 %collective-permute-start.22 = (bf16[4,128,512]{2,1,0:T(8,128)(2,1)S(1)}, bf16[4,128,512]{2,1,0:T(8,128)(2,1)S(1)}, u32[]{:S(2)}, u32[]{:S(2)}) collective-permute-start(bf16[4,128,512]{2,1,0:T(8,128)(2,1)S(1)} %get-tuple-element.81), channel_id=1, source_target_pairs={{2,0},{4,2},{6,4},{8,6},{10,8},{12,10},{14,12},{16,14},{18,16},{20... | collective-permute-start | bytes 1572872 | tf_op jit(solution)/shard_map/ppermute | solution.py:583
  47.8 6.8 %collective-permute-start.14 = (bf16[256,384]{1,0:T(8,128)(2,1)S(1)}, bf16[256,384]{1,0:T(8,128)(2,1)S(1)}, u32[]{:S(2)}, u32[]{:S(2)}) collective-permute-start(bf16[256,384]{1,0:T(8,128)(2,1)S(1)} %tail.1), channel_id=1, source_target_pairs={{0,16},{4,20},{8,24},{12,28},{1,17},{5,21},{9,25},{13,29}} | collective-permute-start | bytes 589832 | tf_op jit(solution)/shard_map/ppermute | solution.py:581
  54.7 5.6 %main.1 = (bf16[1024,256]{1,0:T(8,128)(2,1)S(1)}, f32[256,256]{1,0:T(8,128)S(1)}, f32[256,128]{1,0:T(8,128)S(1)}) custom-call(s32[18]{0:T(128)S(1)} %get-tuple-element.79.info, bf16[256,256]{1,0:T(8,128)(2,1)S(1)} %get-tuple-element.56.refs_0_, bf16[256,256]{1,0:T(8,128)(2,1)S(1)} %collective-permute-done.5.refs_1_, ...), custom_call_target="tpu_custom_call" | custom-call | flops 1680000000 | tf_op jit(solution)/shard_map/main/pallas_call | solution.py:453
  60.3 0.6 merge.1
  61.0 3.4 %collective-permute-start.21 = (bf16[256,256]{1,0:T(8,128)(2,1)S(1)}, bf16[256,256]{1,0:T(8,128)(2,1)S(1)}, u32[]{:S(2)}, u32[]{:S(2)}) collective-permute-start(bf16[256,256]{1,0:T(8,128)(2,1)S(1)} %get-tuple-element.77), channel_id=1, source_target_pairs={{0,12},{1,13},{2,14},{3,15},{4,8},{5,9},{6,10},{7,11},{8,4},{9,5},... | collective-permute-start | bytes 393224 | tf_op jit(solution)/shard_map/ppermute | solution.py:529
  64.6 1.3 %collective-permute-start.17 = (bf16[256,256]{1,0:T(8,128)(2,1)S(1)}, bf16[256,256]{1,0:T(8,128)(2,1)S(1)}, u32[]{:S(2)}, u32[]{:S(2)}) collective-permute-start(bf16[256,256]{1,0:T(8,128)(2,1)S(1)} %get-tuple-element.76), channel_id=1, source_target_pairs={{0,9},{1,8},{2,11},{3,10},{4,13},{5,12},{6,15},{7,14},{8,1},{9,0},... | collective-permute-start | bytes 393224 | tf_op jit(solution)/shard_map/ppermute | solution.py:529
  66.4 2.5 %collective-permute-start.18 = (bf16[256,256]{1,0:T(8,128)(2,1)S(1)}, bf16[256,256]{1,0:T(8,128)(2,1)S(1)}, u32[]{:S(2)}, u32[]{:S(2)}) collective-permute-start(bf16[256,256]{1,0:T(8,128)(2,1)S(1)} %get-tuple-element.77), channel_id=1, source_target_pairs={{0,13},{1,12},{2,15},{3,14},{4,9},{5,8},{6,11},{7,10},{8,5},{9,4},... | collective-permute-start | bytes 393224 | tf_op jit(solution)/shard_map/ppermute | solution.py:529
  68.9 1.4 %collective-permute-start.15 = (bf16[256,256]{1,0:T(8,128)(2,1)S(1)}, bf16[256,256]{1,0:T(8,128)(2,1)S(1)}, u32[]{:S(2)}, u32[]{:S(2)}) collective-permute-start(bf16[256,256]{1,0:T(8,128)(2,1)S(1)} %get-tuple-element.74.refs_0_), channel_id=1, source_target_pairs={{0,1},{1,0},{2,3},{3,2},{4,5},{5,4},{6,7},{7,6},{8,9},{9,8},{10,11... | collective-permute-start | bytes 393224 | tf_op jit(solution)/shard_map/ppermute | solution.py:529
  70.3 2.0 %crossing.1 = bf16[5,128,2,1024]{3,2,1,0:T(2,128)(2,1)} custom-call(s32[18]{0:T(128)S(1)} %get-tuple-element.79.info, bf16[256,512]{1,0:T(8,128)(2,1)S(1)} %get-tuple-element.61.refs_0_.refs_1_.refs_4_, bf16[256,512]{1,0:T(8,128)(2,1)S(1)} %get-tuple-element.53.refs_1_, ...), custom_call_target="tpu_custom_call", output_to_operand_aliasing={{}: (6, {})} | custom-call | flops 525000000 | tf_op jit(solution)/shard_map/crossing/pallas_call | solution.py:434
  72.3 1.3 %out_own.1.refs_6_ = f32[256,1024]{1,0:T(8,128)S(1)} custom-call(s32[18]{0:T(128)S(1)} %get-tuple-element.79.info, bf16[256,256]{1,0:T(8,128)(2,1)S(1)} %get-tuple-element.74.refs_0_, bf16[256,256]{1,0:T(8,128)(2,1)S(1)} %collective-permute-done.19.refs_1_, bf16[256,256]{1,0:T(8,128)(2,1)S(1)} %collective-permute-done.20.refs_2_, ...), custom_call_target="tpu_custom_call" | custom-call | flops 490000000 | tf_op jit(solution)/shard_map/out_own/pallas_call | solution.py:507
  74.1 2.0 %out_theirs.1 = bf16[256,1024]{1,0:T(8,128)(2,1)} custom-call(s32[18]{0:T(128)S(1)} %get-tuple-element.79.info, bf16[256,256]{1,0:T(8,128)(2,1)S(1)} %collective-permute-done.15.refs_0_, bf16[256,256]{1,0:T(8,128)(2,1)S(1)} %collective-permute-done.16.refs_1_, bf16[256,256]{1,0:T(8,128)(2,1)S(1)} %collective-permute-done.17.refs_2_, ...), custom_call_target="tpu_custom_call" | custom-call | flops 700000000 | tf_op jit(solution)/shard_map/out_theirs/pallas_call | solution.py:507
  (40 shorter events, 4.3 us)
Async XLA Ops:
  0.6 15.1 %collective-permute-start = (bf16[256,1024]{1,0:T(8,128)(2,1)}, bf16[256,1024]{1,0:T(8,128)(2,1)S(1)}, u32[]{:S(2)}, u32[]{:S(2)}) collective-permute-start(bf16[256,1024]{1,0:T(8,128)(2,1)} %own.1), channel_id=1, source_target_pairs={{0,1},{1,0},{2,3},{3,2},{4,5},{5,4},{6,7},{7,6},{8,9},{9,8},{10,11... | collective-permute-start | bytes 1572872 | tf_op jit(solution)/shard_map/ppermute | solution.py:529
  3.7 2.2 %copy-start = (bf16[1024,2048]{1,0:T(8,128)(2,1)S(1)}, bf16[1024,2048]{1,0:T(8,128)(2,1)}, u32[]{:S(2)}) copy-start(bf16[1024,2048]{1,0:T(8,128)(2,1)} %w_out.1) | copy-start | bytes 12582916
  5.9 1.0 %copy-start.1 = (bf16[256,1024]{1,0:T(8,128)(2,1)S(1)}, bf16[256,1024]{1,0:T(8,128)(2,1)}, u32[]{:S(2)}) copy-start(bf16[256,1024]{1,0:T(8,128)(2,1)} %own.1) | copy-start | bytes 1572868
  7.0 0.7 copy-start.2
  7.7 0.7 copy-start.3
  8.4 0.7 copy-start.4
  9.0 0.7 copy-start.5
  18.7 27.7 %collective-permute-start.1 = (bf16[512,1024]{1,0:T(8,128)(2,1)S(1)}, bf16[512,1024]{1,0:T(8,128)(2,1)S(1)}, u32[]{:S(2)}, u32[]{:S(2)}) collective-permute-start(bf16[512,1024]{1,0:T(8,128)(2,1)S(1)} %get-tuple-element.52), channel_id=1, source_target_pairs={{0,1},{1,0},{2,3},{3,2},{4,5},{5,4},{6,7},{7,6},{8,9},{9,8},{10,11... | collective-permute-start | bytes 3145736 | tf_op jit(solution)/shard_map/ppermute | solution.py:529
  20.5 8.1 %collective-permute-start.5 = (bf16[256,256]{1,0:T(8,128)(2,1)S(1)}, bf16[256,256]{1,0:T(8,128)(2,1)S(1)}, u32[]{:S(2)}, u32[]{:S(2)}) collective-permute-start(bf16[256,256]{1,0:T(8,128)(2,1)S(1)} %get-tuple-element.57), channel_id=1, source_target_pairs={{0,4},{1,5},{2,6},{3,7},{4,0},{5,1},{6,2},{7,3},{8,12},{9,13},{10,... | collective-permute-start | bytes 393224 | tf_op jit(solution)/shard_map/ppermute | solution.py:529
  22.0 8.2 %collective-permute-start.6 = (bf16[256,256]{1,0:T(8,128)(2,1)S(1)}, bf16[256,256]{1,0:T(8,128)(2,1)S(1)}, u32[]{:S(2)}, u32[]{:S(2)}) collective-permute-start(bf16[256,256]{1,0:T(8,128)(2,1)S(1)} %get-tuple-element.58), channel_id=1, source_target_pairs={{0,8},{1,9},{2,10},{3,11},{4,12},{5,13},{6,14},{7,15},{8,0},{9,1},... | collective-permute-start | bytes 393224 | tf_op jit(solution)/shard_map/ppermute | solution.py:529
  23.6 7.0 %collective-permute-start.7 = (bf16[256,256]{1,0:T(8,128)(2,1)S(1)}, bf16[256,256]{1,0:T(8,128)(2,1)S(1)}, u32[]{:S(2)}, u32[]{:S(2)}) collective-permute-start(bf16[256,256]{1,0:T(8,128)(2,1)S(1)} %get-tuple-element.59), channel_id=1, source_target_pairs={{0,12},{1,13},{2,14},{3,15},{4,8},{5,9},{6,10},{7,11},{8,4},{9,5},... | collective-permute-start | bytes 393224 | tf_op jit(solution)/shard_map/ppermute | solution.py:529
  27.0 9.9 %collective-permute-start.2 = (bf16[256,512]{1,0:T(8,128)(2,1)S(1)}, bf16[256,512]{1,0:T(8,128)(2,1)S(1)}, u32[]{:S(2)}, u32[]{:S(2)}) collective-permute-start(bf16[256,512]{1,0:T(8,128)(2,1)S(1)} %get-tuple-element.53.refs_1_), channel_id=1, source_target_pairs={{0,4},{1,5},{2,6},{3,7},{4,0},{5,1},{6,2},{7,3},{8,12},{9,13},{10,... | collective-permute-start | bytes 786440 | tf_op jit(solution)/shard_map/ppermute | solution.py:529
  28.6 8.6 %collective-permute-start.3 = (bf16[256,512]{1,0:T(8,128)(2,1)S(1)}, bf16[256,512]{1,0:T(8,128)(2,1)S(1)}, u32[]{:S(2)}, u32[]{:S(2)}) collective-permute-start(bf16[256,512]{1,0:T(8,128)(2,1)S(1)} %get-tuple-element.54.refs_2_), channel_id=1, source_target_pairs={{0,8},{1,9},{2,10},{3,11},{4,12},{5,13},{6,14},{7,15},{8,0},{9,1},... | collective-permute-start | bytes 786440 | tf_op jit(solution)/shard_map/ppermute | solution.py:529
  30.2 11.9 %collective-permute-start.4 = (bf16[256,512]{1,0:T(8,128)(2,1)S(1)}, bf16[256,512]{1,0:T(8,128)(2,1)S(1)}, u32[]{:S(2)}, u32[]{:S(2)}) collective-permute-start(bf16[256,512]{1,0:T(8,128)(2,1)S(1)} %get-tuple-element.55.refs_3_), channel_id=1, source_target_pairs={{0,12},{1,13},{2,14},{3,15},{4,8},{5,9},{6,10},{7,11},{8,4},{9,5},... | collective-permute-start | bytes 786440 | tf_op jit(solution)/shard_map/ppermute | solution.py:529
  31.2 10.9 %collective-permute-start.8 = (bf16[256,256]{1,0:T(8,128)(2,1)S(1)}, bf16[256,256]{1,0:T(8,128)(2,1)S(1)}, u32[]{:S(2)}, u32[]{:S(2)}) collective-permute-start(bf16[256,256]{1,0:T(8,128)(2,1)S(1)} %pick.1), channel_id=1, source_target_pairs={{16,0},{20,4},{24,8},{28,12},{17,1},{21,5},{25,9},{29,13}} | collective-permute-start | bytes 393224 | tf_op jit(solution)/shard_map/ppermute | solution.py:571
  36.9 5.6 %collective-permute-start.9 = (bf16[256,512]{1,0:T(8,128)(2,1)S(1)}, bf16[256,512]{1,0:T(8,128)(2,1)S(1)}, u32[]{:S(2)}, u32[]{:S(2)}) collective-permute-start(bf16[256,512]{1,0:T(8,128)(2,1)S(1)} %get-tuple-element.61.refs_0_.refs_1_.refs_4_), channel_id=1, source_target_pairs={{0,2},{1,3},{2,0},{3,1},{4,6},{5,7},{6,4},{7,5},{8,10},{9,11},{10,... | collective-permute-start | bytes 786440 | tf_op jit(solution)/shard_map/ppermute | solution.py:529
  42.1 1.5 %collective-permute-start.10 = (bf16[256,512]{1,0:T(8,128)(2,1)S(1)}, bf16[256,512]{1,0:T(8,128)(2,1)S(1)}, u32[]{:S(2)}, u32[]{:S(2)}) collective-permute-start(bf16[256,512]{1,0:T(8,128)(2,1)S(1)} %collective-permute-done.2.refs_2_.refs_5_), channel_id=1, source_target_pairs={{0,2},{1,3},{2,0},{3,1},{4,6},{5,7},{6,4},{7,5},{8,10},{9,11},{10,... | collective-permute-start | bytes 786440 | tf_op jit(solution)/shard_map/ppermute | solution.py:529
  42.1 1.9 %collective-permute-start.11 = (bf16[256,512]{1,0:T(8,128)(2,1)S(1)}, bf16[256,512]{1,0:T(8,128)(2,1)S(1)}, u32[]{:S(2)}, u32[]{:S(2)}) collective-permute-start(bf16[256,512]{1,0:T(8,128)(2,1)S(1)} %collective-permute-done.3.refs_3_.refs_6_), channel_id=1, source_target_pairs={{0,2},{1,3},{2,0},{3,1},{4,6},{5,7},{6,4},{7,5},{8,10},{9,11},{10,... | collective-permute-start | bytes 786440 | tf_op jit(solution)/shard_map/ppermute | solution.py:529
  42.6 1.8 %collective-permute-start.12 = (bf16[256,512]{1,0:T(8,128)(2,1)S(1)}, bf16[256,512]{1,0:T(8,128)(2,1)S(1)}, u32[]{:S(2)}, u32[]{:S(2)}) collective-permute-start(bf16[256,512]{1,0:T(8,128)(2,1)S(1)} %collective-permute-done.4.refs_4_.refs_7_), channel_id=1, source_target_pairs={{0,2},{1,3},{2,0},{3,1},{4,6},{5,7},{6,4},{7,5},{8,10},{9,11},{10,... | collective-permute-start | bytes 786440 | tf_op jit(solution)/shard_map/ppermute | solution.py:529
  46.4 13.8 %collective-permute-start.13 = (bf16[512,1024]{1,0:T(8,128)(2,1)S(1)}, bf16[512,1024]{1,0:T(8,128)(2,1)S(1)}, u32[]{:S(2)}, u32[]{:S(2)}) collective-permute-start(bf16[512,1024]{1,0:T(8,128)(2,1)S(1)} %collective-permute-done.1.refs_4_), channel_id=1, source_target_pairs={{0,2},{1,3},{2,0},{3,1},{4,6},{5,7},{6,4},{7,5},{8,10},{9,11},{10,... | collective-permute-start | bytes 3145736 | tf_op jit(solution)/shard_map/ppermute | solution.py:529
  46.5 18.1 %collective-permute-start.22 = (bf16[4,128,512]{2,1,0:T(8,128)(2,1)S(1)}, bf16[4,128,512]{2,1,0:T(8,128)(2,1)S(1)}, u32[]{:S(2)}, u32[]{:S(2)}) collective-permute-start(bf16[4,128,512]{2,1,0:T(8,128)(2,1)S(1)} %get-tuple-element.81), channel_id=1, source_target_pairs={{2,0},{4,2},{6,4},{8,6},{10,8},{12,10},{14,12},{16,14},{18,16},{20... | collective-permute-start | bytes 1572872 | tf_op jit(solution)/shard_map/ppermute | solution.py:583
  47.8 12.5 %collective-permute-start.14 = (bf16[256,384]{1,0:T(8,128)(2,1)S(1)}, bf16[256,384]{1,0:T(8,128)(2,1)S(1)}, u32[]{:S(2)}, u32[]{:S(2)}) collective-permute-start(bf16[256,384]{1,0:T(8,128)(2,1)S(1)} %tail.1), channel_id=1, source_target_pairs={{0,16},{4,20},{8,24},{12,28},{1,17},{5,21},{9,25},{13,29}} | collective-permute-start | bytes 589832 | tf_op jit(solution)/shard_map/ppermute | solution.py:581
  60.9 5.5 %collective-permute-start.19 = (bf16[256,256]{1,0:T(8,128)(2,1)S(1)}, bf16[256,256]{1,0:T(8,128)(2,1)S(1)}, u32[]{:S(2)}, u32[]{:S(2)}) collective-permute-start(bf16[256,256]{1,0:T(8,128)(2,1)S(1)} %get-tuple-element.75), channel_id=1, source_target_pairs={{0,4},{1,5},{2,6},{3,7},{4,0},{5,1},{6,2},{7,3},{8,12},{9,13},{10,... | collective-permute-start | bytes 393224 | tf_op jit(solution)/shard_map/ppermute | solution.py:529
  61.0 8.0 %collective-permute-start.20 = (bf16[256,256]{1,0:T(8,128)(2,1)S(1)}, bf16[256,256]{1,0:T(8,128)(2,1)S(1)}, u32[]{:S(2)}, u32[]{:S(2)}) collective-permute-start(bf16[256,256]{1,0:T(8,128)(2,1)S(1)} %get-tuple-element.76), channel_id=1, source_target_pairs={{0,8},{1,9},{2,10},{3,11},{4,12},{5,13},{6,14},{7,15},{8,0},{9,1},... | collective-permute-start | bytes 393224 | tf_op jit(solution)/shard_map/ppermute | solution.py:529
  61.0 11.3 %collective-permute-start.21 = (bf16[256,256]{1,0:T(8,128)(2,1)S(1)}, bf16[256,256]{1,0:T(8,128)(2,1)S(1)}, u32[]{:S(2)}, u32[]{:S(2)}) collective-permute-start(bf16[256,256]{1,0:T(8,128)(2,1)S(1)} %get-tuple-element.77), channel_id=1, source_target_pairs={{0,12},{1,13},{2,14},{3,15},{4,8},{5,9},{6,10},{7,11},{8,4},{9,5},... | collective-permute-start | bytes 393224 | tf_op jit(solution)/shard_map/ppermute | solution.py:529
  64.4 9.2 %collective-permute-start.16 = (bf16[256,256]{1,0:T(8,128)(2,1)S(1)}, bf16[256,256]{1,0:T(8,128)(2,1)S(1)}, u32[]{:S(2)}, u32[]{:S(2)}) collective-permute-start(bf16[256,256]{1,0:T(8,128)(2,1)S(1)} %get-tuple-element.75), channel_id=1, source_target_pairs={{0,5},{1,4},{2,7},{3,6},{4,1},{5,0},{6,3},{7,2},{8,13},{9,12},{10,... | collective-permute-start | bytes 393224 | tf_op jit(solution)/shard_map/ppermute | solution.py:529
  64.6 9.1 %collective-permute-start.17 = (bf16[256,256]{1,0:T(8,128)(2,1)S(1)}, bf16[256,256]{1,0:T(8,128)(2,1)S(1)}, u32[]{:S(2)}, u32[]{:S(2)}) collective-permute-start(bf16[256,256]{1,0:T(8,128)(2,1)S(1)} %get-tuple-element.76), channel_id=1, source_target_pairs={{0,9},{1,8},{2,11},{3,10},{4,13},{5,12},{6,15},{7,14},{8,1},{9,0},... | collective-permute-start | bytes 393224 | tf_op jit(solution)/shard_map/ppermute | solution.py:529
  66.4 7.3 %collective-permute-start.18 = (bf16[256,256]{1,0:T(8,128)(2,1)S(1)}, bf16[256,256]{1,0:T(8,128)(2,1)S(1)}, u32[]{:S(2)}, u32[]{:S(2)}) collective-permute-start(bf16[256,256]{1,0:T(8,128)(2,1)S(1)} %get-tuple-element.77), channel_id=1, source_target_pairs={{0,13},{1,12},{2,15},{3,14},{4,9},{5,8},{6,11},{7,10},{8,5},{9,4},... | collective-permute-start | bytes 393224 | tf_op jit(solution)/shard_map/ppermute | solution.py:529
  68.9 5.2 %collective-permute-start.15 = (bf16[256,256]{1,0:T(8,128)(2,1)S(1)}, bf16[256,256]{1,0:T(8,128)(2,1)S(1)}, u32[]{:S(2)}, u32[]{:S(2)}) collective-permute-start(bf16[256,256]{1,0:T(8,128)(2,1)S(1)} %get-tuple-element.74.refs_0_), channel_id=1, source_target_pairs={{0,1},{1,0},{2,3},{3,2},{4,5},{5,4},{6,7},{7,6},{8,9},{9,8},{10,11... | collective-permute-start | bytes 393224 | tf_op jit(solution)/shard_map/ppermute | solution.py:529

commit v4 on v3

--- a/solution.py
+++ b/solution.py
@@ -286,26 +286,20 @@
 
 
 def main_kernel(info, *refs):
-    splits = (len(refs) - 6) // 3
+    splits = (len(refs) - 5) // 3
     queries, mine, theirs = refs[:splits], refs[splits : 2 * splits], refs[2 * splits : 3 * splits]
-    gathered, near_mixed, near_level, pairs, asked, sems = refs[3 * splits :]
+    gathered, near_mixed, near_level, pairs, asked = refs[3 * splits :]
     rows = near_mixed.shape[0]
 
     def at(block):
         return pl.ds(pl.multiple_of(block * rows, rows), rows)
 
-    def fetch(ref, target, block, sem):
-        return pltpu.make_async_copy(ref, target.at[at(block), :], sems.at[sem])
-
     for split in range(splits):
         place = info[0] ^ split
-        fetch(queries[split], asked, place, 2 * splits + place).start()
+        asked[at(place), :] = queries[split][...]
         for refs_of, core in ((mine, info[2]), (theirs, 1 - info[2])):
-            fetch(refs_of[split], pairs, 2 * place + core, 2 * place + core).start()
+            pairs[at(2 * place + core), :] = refs_of[split][...]
     for place in range(splits):
-        fetch(queries[0], asked, place, 2 * splits + place).wait()
-        for block in (2 * place, 2 * place + 1):
-            fetch(mine[0], pairs, block, block).wait()
         row = info[6] + (2 * place + info[2]) * rows + lax.broadcasted_iota(jnp.int32, (rows, 1), 0)
         here = slice(place * rows, (place + 1) * rows)
         mixed, level = soft_attend(
@@ -448,31 +442,6 @@
     )(info, *pairs, following, written)
 
 
-def on_core(kernel, out_shape, scratch, name, microseconds, direct):
-    def call(info, *operands):
-        return pl.pallas_call(
-            kernel,
-            grid_spec=pltpu.PrefetchScalarGridSpec(
-                num_scalar_prefetch=1,
-                grid=(1,),
-                in_specs=[
-                    pl.BlockSpec(memory_space=pl.ANY)
-                    if number in direct
-                    else pl.BlockSpec(value.shape, lambda i, info: (0, 0))
-                    for number, value in enumerate(operands)
-                ],
-                out_specs=[pl.BlockSpec(out.shape, lambda i, info: (0, 0)) for out in out_shape],
-                scratch_shapes=scratch,
-            ),
-            out_shape=out_shape,
-            compiler_params=pltpu.CompilerParams(vmem_limit_bytes=16 * 2**20),
-            cost_estimate=cost(microseconds),
-            name=name,
-        )(info, *operands)
-
-    return call
-
-
 def out_own_kernel(info, *refs):
     splits = len(refs) - 2
     blocks, (w_own, out) = refs[:splits], refs[splits:]
@@ -484,31 +453,35 @@
 
 
 def out_theirs_kernel(info, *refs):
-    splits = len(refs) - 4
-    blocks, (w_same, w_swap, ours, out) = refs[:splits], refs[splits:]
+    splits = len(refs) - 5
+    blocks, (w_same, w_swap, ours, out, ordered) = refs[:splits], refs[splits:]
+    rows = out.shape[0]
     half = splits // 2
+
+    def at(head):
+        return pl.ds(pl.multiple_of(head * rows, rows), rows)
+
+    for split, block in enumerate(blocks):
+        ordered[at(info[0] ^ split), :] = block[...]
     total = ours[...]
     for weight, core in ((w_same, info[2]), (w_swap, 1 - info[2])):
         for number in range(half):
-            split = info[0] ^ (core * half + number)
-            block = blocks[0][...]
-            for other in range(1, splits):
-                block = jnp.where(split == other, blocks[other][...], block)
             total += jnp.dot(
-                block,
+                ordered[at(core * half + number), :],
                 weight[number * HD : (number + 1) * HD, :],
                 preferred_element_type=jnp.float32,
             )
     out[...] = total.astype(jnp.bfloat16)
 
 
-def on_chip(kernel, out, name, microseconds):
+def on_chip(kernel, out, name, microseconds, scratch=()):
     here = pl.BlockSpec(memory_space=pltpu.VMEM)
     return lambda info, *operands: pl.pallas_call(
         kernel,
         in_specs=[pl.BlockSpec(memory_space=pltpu.SMEM)] + [here] * len(operands),
-        out_specs=here,
+        out_specs=jax.tree.map(lambda _: here, out),
         out_shape=out,
+        scratch_shapes=scratch,
         compiler_params=pltpu.CompilerParams(vmem_limit_bytes=16 * 2**20),
         cost_estimate=cost(microseconds),
         name=name,
@@ -581,24 +554,22 @@
     far = lax.ppermute(tail, "ctx", [(2 * s, group + 2 * s) for s in range(splits)])
     page_head = after(page_head, tail)
     following = lax.ppermute(page_head, "ctx", [(i, i - 1) for i in range(1, count)])
-    gathered, near_mixed, near_level = on_core(
+    gathered, near_mixed, near_level = on_chip(
         main_kernel,
         [
             jax.ShapeDtypeStruct((splits * rows, HD), jnp.bfloat16),
             jax.ShapeDtypeStruct((rows, HD), jnp.float32),
             jax.ShapeDtypeStruct((rows, LANES), jnp.float32),
         ],
+        "main",
+        4.8,
         [
             VMEM((group * rows, 2 * HD), jnp.bfloat16),
             VMEM((splits * rows, HD), jnp.bfloat16),
-            pltpu.SemaphoreType.DMA((group + splits,)),
         ],
-        "main",
-        4.8,
-        range(3 * splits),
     )(after(info, tail), *q_mine, *kv_mine, *kv_theirs)
     block = jax.ShapeDtypeStruct((rows, HD), jnp.bfloat16)
-    blocks = on_core(merge_kernel, [block] * splits, [], "merge", 0.6, ())(
+    blocks = on_chip(merge_kernel, [block] * splits, "merge", 0.6)(
         after(info, w_swap), gathered, near_mixed, near_level, far
     )
     near = [blocks[0]] + [across(blocks[s], 2 * s) for s in range(1, splits)]
@@ -608,7 +579,11 @@
         out_own_kernel, jax.ShapeDtypeStruct((rows, width), jnp.float32), "out_own", 1.4
     )(info, *near, own_columns)
     attn_out = on_chip(
-        out_theirs_kernel, jax.ShapeDtypeStruct((rows, width), jnp.bfloat16), "out_theirs", 2
+        out_theirs_kernel,
+        jax.ShapeDtypeStruct((rows, width), jnp.bfloat16),
+        "out_theirs",
+        2,
+        [VMEM((splits * rows, HD), jnp.bfloat16)],
     )(info, *beyond, w_same, w_swap, ours)
     return attn_out, kv_cache
 

time: 76.5 us -> 76.2 us (level)
  Pallas kernels: 30.1 us -> 27.9 us
  waiting for transfers between devices: 8.4 us -> 10.1 us
    pallas_call x2 -> x0, Pallas kernels: 6.19 us -> none  [call(): pl.pallas_call(kernel, grid_spec=pltpu.PrefetchScalarGridSpec(num_scalar_...]
    pallas_call x4 -> x6, Pallas kernels: 5.91 us -> 9.96 us  [on_chip(): pl.pallas_call(kernel, in_specs=[pl.BlockSpec(memory_space=pltpu.SMEM)] +...]
    ppermute x20, waiting for transfers between devices: 8.4 us -> 9.85 us  [across(): return lax.ppermute(value, ('ctx', 'tp'), pairs)]
  transfers between devices with their start and end apart: 23 -> 23, of which waited for: 10 -> 11; matrix products, arithmetic and copies ran while one was open for 0% -> 0% of each run, Pallas kernels for 33% -> 30%
where the time goes in v4:
time: 76.2 us; the launch traced here: 75.8 us
  starting transfers between devices  31 us (41%)
  Pallas kernels  27.9 us (37%)
  waiting for transfers between devices  10.1 us (13%)
  local copies, waits for them, and re-layouts  6.05 us (8%)
  between operations  0.78 us (1%)
    ppermute x20, starting transfers between devices, across(): return lax.ppermute(value, ('ctx', 'tp'), pairs)  21.6 us
    pallas_call x6, Pallas kernels, on_chip(): pl.pallas_call(kernel, in_specs=[pl.BlockSpec(memory_space=pltpu.SMEM)] +...  9.96 us
    ppermute x20, waiting for transfers between devices, across(): return lax.ppermute(value, ('ctx', 'tp'), pairs)  9.85 us
    ppermute x1, starting transfers between devices, split_heads(): lax.ppermute(tail, 'ctx', [(2 * s, group + 2 * s) for s in range(splits)])  6.85 us
    unnamed x12, local copies, waits for them, and re-layouts  5.96 us
    pallas_call x2, Pallas kernels, project(): pl.pallas_call(kernel, in_specs=[pl.BlockSpec(memory_space=pltpu.SMEM)] +...  5.96 us
    pallas_call x1, Pallas kernels, load(): pl.pallas_call(functools.partial(load_kernel, splits), in_specs=[smem] *...  5.86 us
    pallas_call x1, Pallas kernels, write_pages(): pl.pallas_call(page_kernel, grid_spec=pltpu.PrefetchScalarGridSpec(num_sc...  4.13 us
  transfers between devices with their start and end apart: 23, of which 11 were waited for; matrix products, arithmetic and copies ran while one was open for 0% of the time, Pallas kernels for 30%

profile of v4, /device:TPU:0, one launch (start us, length us, event | category | flops | bytes accessed | tf_op | source)
XLA Modules:
  0.0 75.8 jit_solution(10195117136963707192)
XLA Ops:
  0.6 3.0 %collective-permute-start = (bf16[256,1024]{1,0:T(8,128)(2,1)}, bf16[256,1024]{1,0:T(8,128)(2,1)S(1)}, u32[]{:S(2)}, u32[]{:S(2)}) collective-permute-start(bf16[256,1024]{1,0:T(8,128)(2,1)} %own.1), channel_id=1, source_target_pairs={{0,1},{1,0},{2,3},{3,2},{4,5},{5,4},{6,7},{7,6},{8,9},{9,8},{10,11... | collective-permute-start | bytes 1572872 | tf_op jit(solution)/shard_map/ppermute | solution.py:502
  3.7 2.2 %copy-done = bf16[1024,2048]{1,0:T(8,128)(2,1)S(1)} copy-done((bf16[1024,2048]{1,0:T(8,128)(2,1)S(1)}, bf16[1024,2048]{1,0:T(8,128)(2,1)}, u32[]{:S(2)}) %copy-start) | copy-done | bytes 4194328
  5.9 1.0 %copy-done.1 = bf16[256,1024]{1,0:T(8,128)(2,1)S(1)} copy-done((bf16[256,1024]{1,0:T(8,128)(2,1)S(1)}, bf16[256,1024]{1,0:T(8,128)(2,1)}, u32[]{:S(2)}) %copy-start.1) | copy-done | bytes 524312
  7.0 0.7 copy-done.2
  7.7 0.7 copy-done.3
  8.4 0.7 copy-done.4
  9.0 0.7 copy-done.5
  9.7 5.9 %load.1 = (s32[18]{0:T(128)S(1)}, bf16[256,1024]{1,0:T(8,128)(2,1)S(1)}, f32[1,2048]{1,0:T(1,128)S(1)}, f32[1,2048]{1,0:T(1,128)S(1)}, f32[256,128]{1,0:T(8,128)...) custom-call(s32[3]{0:T(128)S(1)} %copy-done.5, ...), custom_call_target="tpu_custom_call" | custom-call | flops 2100000000 | tf_op jit(solution)/shard_map/load/pallas_call | solution.py:125
  15.8 2.9 %queries.1 = (bf16[256,256]{1,0:T(8,128)(2,1)S(1)}, bf16[256,256]{1,0:T(8,128)(2,1)S(1)}, bf16[256,256]{1,0:T(8,128)(2,1)S(1)}, bf16[256,256]{1,0:T(8,128)(2,1)S(1)}, bf16[256,2048]{1,0:T(8,128)(2,1)S(1)}) custom-call(s32[18]{0:T(128)S(1)} %get-tuple-element.79.info, bf16[256,1024]{1,0:T(8,128)(2,1)S(1)} %get-tuple-element.44.own, ...), custom_call_target="tpu_custom_call" | custom-call | flops 1224999936 | tf_op jit(solution)/shard_map/queries/pallas_call | solution.py:202
  18.7 1.8 %collective-permute-start.1 = (bf16[512,1024]{1,0:T(8,128)(2,1)S(1)}, bf16[512,1024]{1,0:T(8,128)(2,1)S(1)}, u32[]{:S(2)}, u32[]{:S(2)}) collective-permute-start(bf16[512,1024]{1,0:T(8,128)(2,1)S(1)} %get-tuple-element.52), channel_id=1, source_target_pairs={{0,1},{1,0},{2,3},{3,2},{4,5},{5,4},{6,7},{7,6},{8,9},{9,8},{10,11... | collective-permute-start | bytes 3145736 | tf_op jit(solution)/shard_map/ppermute | solution.py:502
  20.5 1.5 %collective-permute-start.5 = (bf16[256,256]{1,0:T(8,128)(2,1)S(1)}, bf16[256,256]{1,0:T(8,128)(2,1)S(1)}, u32[]{:S(2)}, u32[]{:S(2)}) collective-permute-start(bf16[256,256]{1,0:T(8,128)(2,1)S(1)} %get-tuple-element.57), channel_id=1, source_target_pairs={{0,4},{1,5},{2,6},{3,7},{4,0},{5,1},{6,2},{7,3},{8,12},{9,13},{10,... | collective-permute-start | bytes 393224 | tf_op jit(solution)/shard_map/ppermute | solution.py:502
  22.0 1.6 %collective-permute-start.6 = (bf16[256,256]{1,0:T(8,128)(2,1)S(1)}, bf16[256,256]{1,0:T(8,128)(2,1)S(1)}, u32[]{:S(2)}, u32[]{:S(2)}) collective-permute-start(bf16[256,256]{1,0:T(8,128)(2,1)S(1)} %get-tuple-element.58), channel_id=1, source_target_pairs={{0,8},{1,9},{2,10},{3,11},{4,12},{5,13},{6,14},{7,15},{8,0},{9,1},... | collective-permute-start | bytes 393224 | tf_op jit(solution)/shard_map/ppermute | solution.py:502
  24.0 3.1 %pairs.1 = (bf16[256,512]{1,0:T(8,128)(2,1)S(1)}, bf16[256,512]{1,0:T(8,128)(2,1)S(1)}, bf16[256,512]{1,0:T(8,128)(2,1)S(1)}, bf16[256,512]{1,0:T(8,128)(2,1)S(1)}, bf16[4,128,512]{2,1,0:T(8,128)(2,1)S(1)}) custom-call(s32[18]{0:T(128)S(1)} %get-tuple-element.79.info, bf16[256,2048]{1,0:T(8,128)(2,1)S(1)} %get-tuple-element.51.normed, ...), custom_call_target="tpu_custom_call" | custom-call | flops 2100000000 | tf_op jit(solution)/shard_map/pairs/pallas_call | solution.py:202
  27.0 1.6 %collective-permute-start.2 = (bf16[256,512]{1,0:T(8,128)(2,1)S(1)}, bf16[256,512]{1,0:T(8,128)(2,1)S(1)}, u32[]{:S(2)}, u32[]{:S(2)}) collective-permute-start(bf16[256,512]{1,0:T(8,128)(2,1)S(1)} %get-tuple-element.53.refs_1_), channel_id=1, source_target_pairs={{0,4},{1,5},{2,6},{3,7},{4,0},{5,1},{6,2},{7,3},{8,12},{9,13},{10,... | collective-permute-start | bytes 786440 | tf_op jit(solution)/shard_map/ppermute | solution.py:502
  28.6 1.6 %collective-permute-start.3 = (bf16[256,512]{1,0:T(8,128)(2,1)S(1)}, bf16[256,512]{1,0:T(8,128)(2,1)S(1)}, u32[]{:S(2)}, u32[]{:S(2)}) collective-permute-start(bf16[256,512]{1,0:T(8,128)(2,1)S(1)} %get-tuple-element.54.refs_2_), channel_id=1, source_target_pairs={{0,8},{1,9},{2,10},{3,11},{4,12},{5,13},{6,14},{7,15},{8,0},{9,1},... | collective-permute-start | bytes 786440 | tf_op jit(solution)/shard_map/ppermute | solution.py:502
  31.2 1.3 %collective-permute-start.8 = (bf16[256,256]{1,0:T(8,128)(2,1)S(1)}, bf16[256,256]{1,0:T(8,128)(2,1)S(1)}, u32[]{:S(2)}, u32[]{:S(2)}) collective-permute-start(bf16[256,256]{1,0:T(8,128)(2,1)S(1)} %pick.1), channel_id=1, source_target_pairs={{16,0},{20,4},{24,8},{28,12},{17,1},{21,5},{25,9},{29,13}} | collective-permute-start | bytes 393224 | tf_op jit(solution)/shard_map/ppermute | solution.py:544
  32.5 4.1 %pages.1.refs_5_ = bf16[5,128,2,1024]{3,2,1,0:T(2,128)(2,1)} custom-call(s32[18]{0:T(128)S(1)} %get-tuple-element.79.info, bf16[256,512]{1,0:T(8,128)(2,1)S(1)} %get-tuple-element.61.refs_0_.refs_1_.refs_4_, bf16[256,512]{1,0:T(8,128)(2,1)S(1)} %get-tuple-element.53.refs_1_, bf16[256,512]{1,0:T(8,128)(2,1)S(1)} %get-tuple-element.54.refs_2_, ...), custom_call_target="tpu_custom_call" | custom-call | flops 105000000 | tf_op jit(solution)/shard_map/pages/pallas_call | solution.py:406
  37.2 4.9 %collective-permute-done.4.refs_4_.refs_7_ = bf16[256,512]{1,0:T(8,128)(2,1)S(1)} collective-permute-done((bf16[256,512]{1,0:T(8,128)(2,1)S(1)}, bf16[256,512]{1,0:T(8,128)(2,1)S(1)}, u32[]{:S(2)}, u32[]{:S(2)}) %collective-permute-start.4) | collective-permute-done | bytes 262176 | tf_op jit(solution)/shard_map/ppermute | solution.py:502
  42.6 1.0 %collective-permute-done.10.refs_6_.refs_9_ = bf16[256,512]{1,0:T(8,128)(2,1)S(1)} collective-permute-done((bf16[256,512]{1,0:T(8,128)(2,1)S(1)}, bf16[256,512]{1,0:T(8,128)(2,1)S(1)}, u32[]{:S(2)}, u32[]{:S(2)}) %collective-permute-start.10) | collective-permute-done | bytes 262176 | tf_op jit(solution)/shard_map/ppermute | solution.py:502
  44.4 2.0 %tail.1 = bf16[256,384]{1,0:T(8,128)(2,1)S(1)} custom-call(s32[18]{0:T(128)S(1)} %get-tuple-element.79.info, bf16[256,256]{1,0:T(8,128)(2,1)S(1)} %collective-permute-done.8.refs_0_, bf16[256,512]{1,0:T(8,128)(2,1)S(1)} %get-tuple-element.61.refs_0_.refs_1_.refs_4_, bf16[256,512]{1,0:T(8,128)(2,1)S(1)} %collective-permute-done.2.refs_2_.refs_5_, ...), custom_call_target="tpu_custom_call" | custom-call | flops 945000000 | tf_op jit(solution)/shard_map/tail/pallas_call | solution.py:479
  46.5 1.3 %collective-permute-start.22 = (bf16[4,128,512]{2,1,0:T(8,128)(2,1)S(1)}, bf16[4,128,512]{2,1,0:T(8,128)(2,1)S(1)}, u32[]{:S(2)}, u32[]{:S(2)}) collective-permute-start(bf16[4,128,512]{2,1,0:T(8,128)(2,1)S(1)} %get-tuple-element.81), channel_id=1, source_target_pairs={{2,0},{4,2},{6,4},{8,6},{10,8},{12,10},{14,12},{16,14},{18,16},{20... | collective-permute-start | bytes 1572872 | tf_op jit(solution)/shard_map/ppermute | solution.py:556
  47.8 6.8 %collective-permute-start.14 = (bf16[256,384]{1,0:T(8,128)(2,1)S(1)}, bf16[256,384]{1,0:T(8,128)(2,1)S(1)}, u32[]{:S(2)}, u32[]{:S(2)}) collective-permute-start(bf16[256,384]{1,0:T(8,128)(2,1)S(1)} %tail.1), channel_id=1, source_target_pairs={{0,16},{4,20},{8,24},{12,28},{1,17},{5,21},{9,25},{13,29}} | collective-permute-start | bytes 589832 | tf_op jit(solution)/shard_map/ppermute | solution.py:554
  54.7 3.5 %main.1 = (bf16[1024,256]{1,0:T(8,128)(2,1)S(1)}, f32[256,256]{1,0:T(8,128)S(1)}, f32[256,128]{1,0:T(8,128)S(1)}) custom-call(s32[18]{0:T(128)S(1)} %get-tuple-element.79.info, bf16[256,256]{1,0:T(8,128)(2,1)S(1)} %get-tuple-element.56.refs_0_, bf16[256,256]{1,0:T(8,128)(2,1)S(1)} %collective-permute-done.5.refs_1_, ...), custom_call_target="tpu_custom_call" | custom-call | flops 1680000000 | tf_op jit(solution)/shard_map/main/pallas_call | solution.py:479
  59.6 2.9 %collective-permute-start.21 = (bf16[256,256]{1,0:T(8,128)(2,1)S(1)}, bf16[256,256]{1,0:T(8,128)(2,1)S(1)}, u32[]{:S(2)}, u32[]{:S(2)}) collective-permute-start(bf16[256,256]{1,0:T(8,128)(2,1)S(1)} %get-tuple-element.77), channel_id=1, source_target_pairs={{0,12},{1,13},{2,14},{3,15},{4,8},{5,9},{6,10},{7,11},{8,4},{9,5},... | collective-permute-start | bytes 393224 | tf_op jit(solution)/shard_map/ppermute | solution.py:502
  62.6 1.3 %collective-permute-start.17 = (bf16[256,256]{1,0:T(8,128)(2,1)S(1)}, bf16[256,256]{1,0:T(8,128)(2,1)S(1)}, u32[]{:S(2)}, u32[]{:S(2)}) collective-permute-start(bf16[256,256]{1,0:T(8,128)(2,1)S(1)} %get-tuple-element.76), channel_id=1, source_target_pairs={{0,9},{1,8},{2,11},{3,10},{4,13},{5,12},{6,15},{7,14},{8,1},{9,0},... | collective-permute-start | bytes 393224 | tf_op jit(solution)/shard_map/ppermute | solution.py:502
  64.2 2.7 %collective-permute-start.18 = (bf16[256,256]{1,0:T(8,128)(2,1)S(1)}, bf16[256,256]{1,0:T(8,128)(2,1)S(1)}, u32[]{:S(2)}, u32[]{:S(2)}) collective-permute-start(bf16[256,256]{1,0:T(8,128)(2,1)S(1)} %get-tuple-element.77), channel_id=1, source_target_pairs={{0,13},{1,12},{2,15},{3,14},{4,9},{5,8},{6,11},{7,10},{8,5},{9,4},... | collective-permute-start | bytes 393224 | tf_op jit(solution)/shard_map/ppermute | solution.py:502
  66.9 1.4 %collective-permute-start.15 = (bf16[256,256]{1,0:T(8,128)(2,1)S(1)}, bf16[256,256]{1,0:T(8,128)(2,1)S(1)}, u32[]{:S(2)}, u32[]{:S(2)}) collective-permute-start(bf16[256,256]{1,0:T(8,128)(2,1)S(1)} %get-tuple-element.74.refs_0_), channel_id=1, source_target_pairs={{0,1},{1,0},{2,3},{3,2},{4,5},{5,4},{6,7},{7,6},{8,9},{9,8},{10,11... | collective-permute-start | bytes 393224 | tf_op jit(solution)/shard_map/ppermute | solution.py:502
  68.3 2.0 %crossing.1 = bf16[5,128,2,1024]{3,2,1,0:T(2,128)(2,1)} custom-call(s32[18]{0:T(128)S(1)} %get-tuple-element.79.info, bf16[256,512]{1,0:T(8,128)(2,1)S(1)} %get-tuple-element.61.refs_0_.refs_1_.refs_4_, bf16[256,512]{1,0:T(8,128)(2,1)S(1)} %get-tuple-element.53.refs_1_, ...), custom_call_target="tpu_custom_call", output_to_operand_aliasing={{}: (6, {})} | custom-call | flops 525000000 | tf_op jit(solution)/shard_map/crossing/pallas_call | solution.py:428
  70.4 1.3 %out_own.1.refs_6_ = f32[256,1024]{1,0:T(8,128)S(1)} custom-call(s32[18]{0:T(128)S(1)} %get-tuple-element.79.info, bf16[256,256]{1,0:T(8,128)(2,1)S(1)} %get-tuple-element.74.refs_0_, bf16[256,256]{1,0:T(8,128)(2,1)S(1)} %collective-permute-done.19.refs_1_, bf16[256,256]{1,0:T(8,128)(2,1)S(1)} %collective-permute-done.20.refs_2_, ...), custom_call_target="tpu_custom_call" | custom-call | flops 490000000 | tf_op jit(solution)/shard_map/out_own/pallas_call | solution.py:479
  71.6 0.8 %collective-permute-done.16.refs_1_ = bf16[256,256]{1,0:T(8,128)(2,1)S(1)} collective-permute-done((bf16[256,256]{1,0:T(8,128)(2,1)S(1)}, bf16[256,256]{1,0:T(8,128)(2,1)S(1)}, u32[]{:S(2)}, u32[]{:S(2)}) %collective-permute-start.16) | collective-permute-done | bytes 131104 | tf_op jit(solution)/shard_map/ppermute | solution.py:502
  72.4 1.4 %collective-permute-done.15.refs_0_ = bf16[256,256]{1,0:T(8,128)(2,1)S(1)} collective-permute-done((bf16[256,256]{1,0:T(8,128)(2,1)S(1)}, bf16[256,256]{1,0:T(8,128)(2,1)S(1)}, u32[]{:S(2)}, u32[]{:S(2)}) %collective-permute-start.15) | collective-permute-done | bytes 131104 | tf_op jit(solution)/shard_map/ppermute | solution.py:502
  73.8 2.1 %out_theirs.1 = bf16[256,1024]{1,0:T(8,128)(2,1)} custom-call(s32[18]{0:T(128)S(1)} %get-tuple-element.79.info, bf16[256,256]{1,0:T(8,128)(2,1)S(1)} %collective-permute-done.15.refs_0_, bf16[256,256]{1,0:T(8,128)(2,1)S(1)} %collective-permute-done.16.refs_1_, bf16[256,256]{1,0:T(8,128)(2,1)S(1)} %collective-permute-done.17.refs_2_, ...), custom_call_target="tpu_custom_call" | custom-call | flops 700000000 | tf_op jit(solution)/shard_map/out_theirs/pallas_call | solution.py:479
  (40 shorter events, 5.5 us)
Async XLA Ops:
  0.6 15.1 %collective-permute-start = (bf16[256,1024]{1,0:T(8,128)(2,1)}, bf16[256,1024]{1,0:T(8,128)(2,1)S(1)}, u32[]{:S(2)}, u32[]{:S(2)}) collective-permute-start(bf16[256,1024]{1,0:T(8,128)(2,1)} %own.1), channel_id=1, source_target_pairs={{0,1},{1,0},{2,3},{3,2},{4,5},{5,4},{6,7},{7,6},{8,9},{9,8},{10,11... | collective-permute-start | bytes 1572872 | tf_op jit(solution)/shard_map/ppermute | solution.py:502
  3.7 2.2 %copy-start = (bf16[1024,2048]{1,0:T(8,128)(2,1)S(1)}, bf16[1024,2048]{1,0:T(8,128)(2,1)}, u32[]{:S(2)}) copy-start(bf16[1024,2048]{1,0:T(8,128)(2,1)} %w_out.1) | copy-start | bytes 12582916
  5.9 1.0 %copy-start.1 = (bf16[256,1024]{1,0:T(8,128)(2,1)S(1)}, bf16[256,1024]{1,0:T(8,128)(2,1)}, u32[]{:S(2)}) copy-start(bf16[256,1024]{1,0:T(8,128)(2,1)} %own.1) | copy-start | bytes 1572868
  7.0 0.7 copy-start.2
  7.7 0.7 copy-start.3
  8.4 0.7 copy-start.4
  9.0 0.7 copy-start.5
  18.7 27.7 %collective-permute-start.1 = (bf16[512,1024]{1,0:T(8,128)(2,1)S(1)}, bf16[512,1024]{1,0:T(8,128)(2,1)S(1)}, u32[]{:S(2)}, u32[]{:S(2)}) collective-permute-start(bf16[512,1024]{1,0:T(8,128)(2,1)S(1)} %get-tuple-element.52), channel_id=1, source_target_pairs={{0,1},{1,0},{2,3},{3,2},{4,5},{5,4},{6,7},{7,6},{8,9},{9,8},{10,11... | collective-permute-start | bytes 3145736 | tf_op jit(solution)/shard_map/ppermute | solution.py:502
  20.5 8.1 %collective-permute-start.5 = (bf16[256,256]{1,0:T(8,128)(2,1)S(1)}, bf16[256,256]{1,0:T(8,128)(2,1)S(1)}, u32[]{:S(2)}, u32[]{:S(2)}) collective-permute-start(bf16[256,256]{1,0:T(8,128)(2,1)S(1)} %get-tuple-element.57), channel_id=1, source_target_pairs={{0,4},{1,5},{2,6},{3,7},{4,0},{5,1},{6,2},{7,3},{8,12},{9,13},{10,... | collective-permute-start | bytes 393224 | tf_op jit(solution)/shard_map/ppermute | solution.py:502
  22.0 8.2 %collective-permute-start.6 = (bf16[256,256]{1,0:T(8,128)(2,1)S(1)}, bf16[256,256]{1,0:T(8,128)(2,1)S(1)}, u32[]{:S(2)}, u32[]{:S(2)}) collective-permute-start(bf16[256,256]{1,0:T(8,128)(2,1)S(1)} %get-tuple-element.58), channel_id=1, source_target_pairs={{0,8},{1,9},{2,10},{3,11},{4,12},{5,13},{6,14},{7,15},{8,0},{9,1},... | collective-permute-start | bytes 393224 | tf_op jit(solution)/shard_map/ppermute | solution.py:502
  23.6 7.0 %collective-permute-start.7 = (bf16[256,256]{1,0:T(8,128)(2,1)S(1)}, bf16[256,256]{1,0:T(8,128)(2,1)S(1)}, u32[]{:S(2)}, u32[]{:S(2)}) collective-permute-start(bf16[256,256]{1,0:T(8,128)(2,1)S(1)} %get-tuple-element.59), channel_id=1, source_target_pairs={{0,12},{1,13},{2,14},{3,15},{4,8},{5,9},{6,10},{7,11},{8,4},{9,5},... | collective-permute-start | bytes 393224 | tf_op jit(solution)/shard_map/ppermute | solution.py:502
  27.0 9.9 %collective-permute-start.2 = (bf16[256,512]{1,0:T(8,128)(2,1)S(1)}, bf16[256,512]{1,0:T(8,128)(2,1)S(1)}, u32[]{:S(2)}, u32[]{:S(2)}) collective-permute-start(bf16[256,512]{1,0:T(8,128)(2,1)S(1)} %get-tuple-element.53.refs_1_), channel_id=1, source_target_pairs={{0,4},{1,5},{2,6},{3,7},{4,0},{5,1},{6,2},{7,3},{8,12},{9,13},{10,... | collective-permute-start | bytes 786440 | tf_op jit(solution)/shard_map/ppermute | solution.py:502
  28.6 8.6 %collective-permute-start.3 = (bf16[256,512]{1,0:T(8,128)(2,1)S(1)}, bf16[256,512]{1,0:T(8,128)(2,1)S(1)}, u32[]{:S(2)}, u32[]{:S(2)}) collective-permute-start(bf16[256,512]{1,0:T(8,128)(2,1)S(1)} %get-tuple-element.54.refs_2_), channel_id=1, source_target_pairs={{0,8},{1,9},{2,10},{3,11},{4,12},{5,13},{6,14},{7,15},{8,0},{9,1},... | collective-permute-start | bytes 786440 | tf_op jit(solution)/shard_map/ppermute | solution.py:502
  30.2 11.9 %collective-permute-start.4 = (bf16[256,512]{1,0:T(8,128)(2,1)S(1)}, bf16[256,512]{1,0:T(8,128)(2,1)S(1)}, u32[]{:S(2)}, u32[]{:S(2)}) collective-permute-start(bf16[256,512]{1,0:T(8,128)(2,1)S(1)} %get-tuple-element.55.refs_3_), channel_id=1, source_target_pairs={{0,12},{1,13},{2,14},{3,15},{4,8},{5,9},{6,10},{7,11},{8,4},{9,5},... | collective-permute-start | bytes 786440 | tf_op jit(solution)/shard_map/ppermute | solution.py:502
  31.2 10.9 %collective-permute-start.8 = (bf16[256,256]{1,0:T(8,128)(2,1)S(1)}, bf16[256,256]{1,0:T(8,128)(2,1)S(1)}, u32[]{:S(2)}, u32[]{:S(2)}) collective-permute-start(bf16[256,256]{1,0:T(8,128)(2,1)S(1)} %pick.1), channel_id=1, source_target_pairs={{16,0},{20,4},{24,8},{28,12},{17,1},{21,5},{25,9},{29,13}} | collective-permute-start | bytes 393224 | tf_op jit(solution)/shard_map/ppermute | solution.py:544
  36.9 5.6 %collective-permute-start.9 = (bf16[256,512]{1,0:T(8,128)(2,1)S(1)}, bf16[256,512]{1,0:T(8,128)(2,1)S(1)}, u32[]{:S(2)}, u32[]{:S(2)}) collective-permute-start(bf16[256,512]{1,0:T(8,128)(2,1)S(1)} %get-tuple-element.61.refs_0_.refs_1_.refs_4_), channel_id=1, source_target_pairs={{0,2},{1,3},{2,0},{3,1},{4,6},{5,7},{6,4},{7,5},{8,10},{9,11},{10,... | collective-permute-start | bytes 786440 | tf_op jit(solution)/shard_map/ppermute | solution.py:502
  42.1 1.5 %collective-permute-start.10 = (bf16[256,512]{1,0:T(8,128)(2,1)S(1)}, bf16[256,512]{1,0:T(8,128)(2,1)S(1)}, u32[]{:S(2)}, u32[]{:S(2)}) collective-permute-start(bf16[256,512]{1,0:T(8,128)(2,1)S(1)} %collective-permute-done.2.refs_2_.refs_5_), channel_id=1, source_target_pairs={{0,2},{1,3},{2,0},{3,1},{4,6},{5,7},{6,4},{7,5},{8,10},{9,11},{10,... | collective-permute-start | bytes 786440 | tf_op jit(solution)/shard_map/ppermute | solution.py:502
  42.1 1.9 %collective-permute-start.11 = (bf16[256,512]{1,0:T(8,128)(2,1)S(1)}, bf16[256,512]{1,0:T(8,128)(2,1)S(1)}, u32[]{:S(2)}, u32[]{:S(2)}) collective-permute-start(bf16[256,512]{1,0:T(8,128)(2,1)S(1)} %collective-permute-done.3.refs_3_.refs_6_), channel_id=1, source_target_pairs={{0,2},{1,3},{2,0},{3,1},{4,6},{5,7},{6,4},{7,5},{8,10},{9,11},{10,... | collective-permute-start | bytes 786440 | tf_op jit(solution)/shard_map/ppermute | solution.py:502
  42.6 1.8 %collective-permute-start.12 = (bf16[256,512]{1,0:T(8,128)(2,1)S(1)}, bf16[256,512]{1,0:T(8,128)(2,1)S(1)}, u32[]{:S(2)}, u32[]{:S(2)}) collective-permute-start(bf16[256,512]{1,0:T(8,128)(2,1)S(1)} %collective-permute-done.4.refs_4_.refs_7_), channel_id=1, source_target_pairs={{0,2},{1,3},{2,0},{3,1},{4,6},{5,7},{6,4},{7,5},{8,10},{9,11},{10,... | collective-permute-start | bytes 786440 | tf_op jit(solution)/shard_map/ppermute | solution.py:502
  46.4 11.7 %collective-permute-start.13 = (bf16[512,1024]{1,0:T(8,128)(2,1)S(1)}, bf16[512,1024]{1,0:T(8,128)(2,1)S(1)}, u32[]{:S(2)}, u32[]{:S(2)}) collective-permute-start(bf16[512,1024]{1,0:T(8,128)(2,1)S(1)} %collective-permute-done.1.refs_4_), channel_id=1, source_target_pairs={{0,2},{1,3},{2,0},{3,1},{4,6},{5,7},{6,4},{7,5},{8,10},{9,11},{10,... | collective-permute-start | bytes 3145736 | tf_op jit(solution)/shard_map/ppermute | solution.py:502
  46.5 16.1 %collective-permute-start.22 = (bf16[4,128,512]{2,1,0:T(8,128)(2,1)S(1)}, bf16[4,128,512]{2,1,0:T(8,128)(2,1)S(1)}, u32[]{:S(2)}, u32[]{:S(2)}) collective-permute-start(bf16[4,128,512]{2,1,0:T(8,128)(2,1)S(1)} %get-tuple-element.81), channel_id=1, source_target_pairs={{2,0},{4,2},{6,4},{8,6},{10,8},{12,10},{14,12},{16,14},{18,16},{20... | collective-permute-start | bytes 1572872 | tf_op jit(solution)/shard_map/ppermute | solution.py:556
  47.8 10.5 %collective-permute-start.14 = (bf16[256,384]{1,0:T(8,128)(2,1)S(1)}, bf16[256,384]{1,0:T(8,128)(2,1)S(1)}, u32[]{:S(2)}, u32[]{:S(2)}) collective-permute-start(bf16[256,384]{1,0:T(8,128)(2,1)S(1)} %tail.1), channel_id=1, source_target_pairs={{0,16},{4,20},{8,24},{12,28},{1,17},{5,21},{9,25},{13,29}} | collective-permute-start | bytes 589832 | tf_op jit(solution)/shard_map/ppermute | solution.py:554
  58.9 5.3 %collective-permute-start.19 = (bf16[256,256]{1,0:T(8,128)(2,1)S(1)}, bf16[256,256]{1,0:T(8,128)(2,1)S(1)}, u32[]{:S(2)}, u32[]{:S(2)}) collective-permute-start(bf16[256,256]{1,0:T(8,128)(2,1)S(1)} %get-tuple-element.75), channel_id=1, source_target_pairs={{0,4},{1,5},{2,6},{3,7},{4,0},{5,1},{6,2},{7,3},{8,12},{9,13},{10,... | collective-permute-start | bytes 393224 | tf_op jit(solution)/shard_map/ppermute | solution.py:502
  59.0 8.0 %collective-permute-start.20 = (bf16[256,256]{1,0:T(8,128)(2,1)S(1)}, bf16[256,256]{1,0:T(8,128)(2,1)S(1)}, u32[]{:S(2)}, u32[]{:S(2)}) collective-permute-start(bf16[256,256]{1,0:T(8,128)(2,1)S(1)} %get-tuple-element.76), channel_id=1, source_target_pairs={{0,8},{1,9},{2,10},{3,11},{4,12},{5,13},{6,14},{7,15},{8,0},{9,1},... | collective-permute-start | bytes 393224 | tf_op jit(solution)/shard_map/ppermute | solution.py:502
  59.6 10.8 %collective-permute-start.21 = (bf16[256,256]{1,0:T(8,128)(2,1)S(1)}, bf16[256,256]{1,0:T(8,128)(2,1)S(1)}, u32[]{:S(2)}, u32[]{:S(2)}) collective-permute-start(bf16[256,256]{1,0:T(8,128)(2,1)S(1)} %get-tuple-element.77), channel_id=1, source_target_pairs={{0,12},{1,13},{2,14},{3,15},{4,8},{5,9},{6,10},{7,11},{8,4},{9,5},... | collective-permute-start | bytes 393224 | tf_op jit(solution)/shard_map/ppermute | solution.py:502
  62.5 10.0 %collective-permute-start.16 = (bf16[256,256]{1,0:T(8,128)(2,1)S(1)}, bf16[256,256]{1,0:T(8,128)(2,1)S(1)}, u32[]{:S(2)}, u32[]{:S(2)}) collective-permute-start(bf16[256,256]{1,0:T(8,128)(2,1)S(1)} %get-tuple-element.75), channel_id=1, source_target_pairs={{0,5},{1,4},{2,7},{3,6},{4,1},{5,0},{6,3},{7,2},{8,13},{9,12},{10,... | collective-permute-start | bytes 393224 | tf_op jit(solution)/shard_map/ppermute | solution.py:502
  62.6 9.8 %collective-permute-start.17 = (bf16[256,256]{1,0:T(8,128)(2,1)S(1)}, bf16[256,256]{1,0:T(8,128)(2,1)S(1)}, u32[]{:S(2)}, u32[]{:S(2)}) collective-permute-start(bf16[256,256]{1,0:T(8,128)(2,1)S(1)} %get-tuple-element.76), channel_id=1, source_target_pairs={{0,9},{1,8},{2,11},{3,10},{4,13},{5,12},{6,15},{7,14},{8,1},{9,0},... | collective-permute-start | bytes 393224 | tf_op jit(solution)/shard_map/ppermute | solution.py:502
  64.2 8.2 %collective-permute-start.18 = (bf16[256,256]{1,0:T(8,128)(2,1)S(1)}, bf16[256,256]{1,0:T(8,128)(2,1)S(1)}, u32[]{:S(2)}, u32[]{:S(2)}) collective-permute-start(bf16[256,256]{1,0:T(8,128)(2,1)S(1)} %get-tuple-element.77), channel_id=1, source_target_pairs={{0,13},{1,12},{2,15},{3,14},{4,9},{5,8},{6,11},{7,10},{8,5},{9,4},... | collective-permute-start | bytes 393224 | tf_op jit(solution)/shard_map/ppermute | solution.py:502
  66.9 6.8 %collective-permute-start.15 = (bf16[256,256]{1,0:T(8,128)(2,1)S(1)}, bf16[256,256]{1,0:T(8,128)(2,1)S(1)}, u32[]{:S(2)}, u32[]{:S(2)}) collective-permute-start(bf16[256,256]{1,0:T(8,128)(2,1)S(1)} %get-tuple-element.74.refs_0_), channel_id=1, source_target_pairs={{0,1},{1,0},{2,3},{3,2},{4,5},{5,4},{6,7},{7,6},{8,9},{9,8},{10,11... | collective-permute-start | bytes 393224 | tf_op jit(solution)/shard_map/ppermute | solution.py:502

commit v5 on v4

--- a/solution.py
+++ b/solution.py
@@ -13,6 +13,7 @@
 EPSILON = 1e-05
 ROT = HD // 4
 LANES = 128
+PARTS = 16
 VMEM = pltpu.VMEM
 MASKED = -1e30
 LOG2E = 1.4426950408889634
@@ -259,7 +260,7 @@
     splits = (len(refs) - 2) // 2
     query_ref, out = refs[0], refs[-1]
     mine, theirs = refs[1 : splits + 1], refs[splits + 1 : 2 * splits + 1]
-    rows = out.shape[0]
+    rows = query_ref.shape[0]
 
     @pl.when((info[6] == 0) & (info[2] == 0))
     def _():
@@ -275,13 +276,14 @@
         scores += [score(query, ref[:, :HD]) for ref in theirs]
         mixed, level = softmax_mix(scores, [ref.at[:, HD:] for ref in (*mine, *theirs)])
         level = jnp.where(first < group_rows, level, MASKED)
-        out[:, :HD] = mixed.astype(jnp.bfloat16)
-        lane = lax.broadcasted_iota(jnp.int32, (rows, LANES), 1)
+        out[:rows, :] = mixed.astype(jnp.bfloat16)
+        level = jnp.broadcast_to(level, (rows, LANES)).T[:PARTS, :]
+        part = lax.broadcasted_iota(jnp.int32, (PARTS, rows), 0)
         high = level.astype(jnp.bfloat16).astype(jnp.float32)
         middle = (level - high).astype(jnp.bfloat16).astype(jnp.float32)
         low = level - high - middle
-        out[:, HD:] = jnp.where(
-            lane == 0, high, jnp.where(lane == 1, middle, jnp.where(lane == 2, low, 0.0))
+        out[rows:, :] = jnp.where(
+            part == 0, high, jnp.where(part == 1, middle, jnp.where(part == 2, low, 0.0))
         ).astype(jnp.bfloat16)
 
 
@@ -326,12 +328,13 @@
 
     @pl.when((info[6] > 0) & (info[2] == 0))
     def _():
-        parts = far[:, HD:].astype(jnp.float32)
-        far_level = parts[:, :1] + parts[:, 1:2] + parts[:, 2:3]
+        parts = far[rows:, :].astype(jnp.float32)
+        far_level = parts[:1, :] + parts[1:2, :] + parts[2:3, :]
+        far_level = jnp.broadcast_to(far_level, (LANES, rows)).T[:, :1]
         level = near_level[:, :1]
         highest = jnp.maximum(level, far_level)
         near_weight, far_weight = jnp.exp2(level - highest), jnp.exp2(far_level - highest)
-        mixed = near_mixed[...] * near_weight + far[:, :HD].astype(jnp.float32) * far_weight
+        mixed = near_mixed[...] * near_weight + far[:rows, :].astype(jnp.float32) * far_weight
         mixed = mixed / (near_weight + far_weight)
         row = group_rows + lax.broadcasted_iota(jnp.int32, (rows, 1), 0)
         mixed = jnp.where(row < info[5], mixed, near_mixed[...]).astype(jnp.bfloat16)
@@ -548,12 +551,12 @@
     w_same = across(after(outgoing, normed), 0, 1)
 
     tail = on_chip(
-        tail_kernel, jax.ShapeDtypeStruct((rows, HD + LANES), jnp.bfloat16), "tail", 2.7
+        tail_kernel, jax.ShapeDtypeStruct((rows + PARTS, HD), jnp.bfloat16), "tail", 2.7
     )(after(info, kv_cache), q_tail, *kv_mine, *kv_theirs)
-    w_swap = across(after(w_same, tail), 1)
-    far = lax.ppermute(tail, "ctx", [(2 * s, group + 2 * s) for s in range(splits)])
     page_head = after(page_head, tail)
     following = lax.ppermute(page_head, "ctx", [(i, i - 1) for i in range(1, count)])
+    far = lax.ppermute(tail, "ctx", [(2 * s, group + 2 * s) for s in range(splits)])
+    w_swap = across(after(w_same, tail), 1)
     gathered, near_mixed, near_level = on_chip(
         main_kernel,
         [

time: 76.2 us -> 76.4 us (level)
  transfers between devices with their start and end apart: 23 -> 23, of which waited for: 11 -> 10; matrix products, arithmetic and copies ran while one was open for 0% -> 0% of each run, Pallas kernels for 30% -> 30%
where the time goes in v5:
time: 76.4 us; the launch traced here: 76 us
  starting transfers between devices  30.9 us (40%)
  Pallas kernels  27.9 us (37%)
  waiting for transfers between devices  10.3 us (13%)
  local copies, waits for them, and re-layouts  6.05 us (8%)
  between operations  0.79 us (1%)
    ppermute x20, starting transfers between devices, across(): return lax.ppermute(value, ('ctx', 'tp'), pairs)  21.5 us
    ppermute x20, waiting for transfers between devices, across(): return lax.ppermute(value, ('ctx', 'tp'), pairs)  10.3 us
    pallas_call x6, Pallas kernels, on_chip(): pl.pallas_call(kernel, in_specs=[pl.BlockSpec(memory_space=pltpu.SMEM)] +...  9.96 us
    ppermute x1, starting transfers between devices, split_heads(): lax.ppermute(tail, 'ctx', [(2 * s, group + 2 * s) for s in range(splits)])  6.84 us
    unnamed x12, local copies, waits for them, and re-layouts  5.96 us
    pallas_call x2, Pallas kernels, project(): pl.pallas_call(kernel, in_specs=[pl.BlockSpec(memory_space=pltpu.SMEM)] +...  5.96 us
    pallas_call x1, Pallas kernels, load(): pl.pallas_call(functools.partial(load_kernel, splits), in_specs=[smem] *...  5.86 us
    pallas_call x1, Pallas kernels, write_pages(): pl.pallas_call(page_kernel, grid_spec=pltpu.PrefetchScalarGridSpec(num_sc...  4.13 us
  transfers between devices with their start and end apart: 23, of which 10 were waited for; matrix products, arithmetic and copies ran while one was open for 0% of the time, Pallas kernels for 30%

profile of v5, /device:TPU:0, one launch (start us, length us, event | category | flops | bytes accessed | tf_op | source)
XLA Modules:
  0.0 76.0 jit_solution(5343903805471927776)
XLA Ops:
  0.6 3.0 %collective-permute-start = (bf16[256,1024]{1,0:T(8,128)(2,1)}, bf16[256,1024]{1,0:T(8,128)(2,1)S(1)}, u32[]{:S(2)}, u32[]{:S(2)}) collective-permute-start(bf16[256,1024]{1,0:T(8,128)(2,1)} %own.1), channel_id=1, source_target_pairs={{0,1},{1,0},{2,3},{3,2},{4,5},{5,4},{6,7},{7,6},{8,9},{9,8},{10,11... | collective-permute-start | bytes 1572872 | tf_op jit(solution)/shard_map/ppermute | solution.py:505
  3.7 2.2 %copy-done = bf16[1024,2048]{1,0:T(8,128)(2,1)S(1)} copy-done((bf16[1024,2048]{1,0:T(8,128)(2,1)S(1)}, bf16[1024,2048]{1,0:T(8,128)(2,1)}, u32[]{:S(2)}) %copy-start) | copy-done | bytes 4194328
  5.9 1.0 %copy-done.1 = bf16[256,1024]{1,0:T(8,128)(2,1)S(1)} copy-done((bf16[256,1024]{1,0:T(8,128)(2,1)S(1)}, bf16[256,1024]{1,0:T(8,128)(2,1)}, u32[]{:S(2)}) %copy-start.1) | copy-done | bytes 524312
  7.0 0.7 copy-done.2
  7.7 0.7 copy-done.3
  8.4 0.7 copy-done.4
  9.0 0.7 copy-done.5
  9.7 5.9 %load.1 = (s32[18]{0:T(128)S(1)}, bf16[256,1024]{1,0:T(8,128)(2,1)S(1)}, f32[1,2048]{1,0:T(1,128)S(1)}, f32[1,2048]{1,0:T(1,128)S(1)}, f32[256,128]{1,0:T(8,128)...) custom-call(s32[3]{0:T(128)S(1)} %copy-done.5, ...), custom_call_target="tpu_custom_call" | custom-call | flops 2100000000 | tf_op jit(solution)/shard_map/load/pallas_call | solution.py:126
  15.8 2.9 %queries.1 = (bf16[256,256]{1,0:T(8,128)(2,1)S(1)}, bf16[256,256]{1,0:T(8,128)(2,1)S(1)}, bf16[256,256]{1,0:T(8,128)(2,1)S(1)}, bf16[256,256]{1,0:T(8,128)(2,1)S(1)}, bf16[256,2048]{1,0:T(8,128)(2,1)S(1)}) custom-call(s32[18]{0:T(128)S(1)} %get-tuple-element.79.info, bf16[256,1024]{1,0:T(8,128)(2,1)S(1)} %get-tuple-element.44.own, ...), custom_call_target="tpu_custom_call" | custom-call | flops 1224999936 | tf_op jit(solution)/shard_map/queries/pallas_call | solution.py:203
  18.7 1.8 %collective-permute-start.1 = (bf16[512,1024]{1,0:T(8,128)(2,1)S(1)}, bf16[512,1024]{1,0:T(8,128)(2,1)S(1)}, u32[]{:S(2)}, u32[]{:S(2)}) collective-permute-start(bf16[512,1024]{1,0:T(8,128)(2,1)S(1)} %get-tuple-element.52), channel_id=1, source_target_pairs={{0,1},{1,0},{2,3},{3,2},{4,5},{5,4},{6,7},{7,6},{8,9},{9,8},{10,11... | collective-permute-start | bytes 3145736 | tf_op jit(solution)/shard_map/ppermute | solution.py:505
  20.5 1.5 %collective-permute-start.5 = (bf16[256,256]{1,0:T(8,128)(2,1)S(1)}, bf16[256,256]{1,0:T(8,128)(2,1)S(1)}, u32[]{:S(2)}, u32[]{:S(2)}) collective-permute-start(bf16[256,256]{1,0:T(8,128)(2,1)S(1)} %get-tuple-element.57), channel_id=1, source_target_pairs={{0,4},{1,5},{2,6},{3,7},{4,0},{5,1},{6,2},{7,3},{8,12},{9,13},{10,... | collective-permute-start | bytes 393224 | tf_op jit(solution)/shard_map/ppermute | solution.py:505
  22.0 1.6 %collective-permute-start.6 = (bf16[256,256]{1,0:T(8,128)(2,1)S(1)}, bf16[256,256]{1,0:T(8,128)(2,1)S(1)}, u32[]{:S(2)}, u32[]{:S(2)}) collective-permute-start(bf16[256,256]{1,0:T(8,128)(2,1)S(1)} %get-tuple-element.58), channel_id=1, source_target_pairs={{0,8},{1,9},{2,10},{3,11},{4,12},{5,13},{6,14},{7,15},{8,0},{9,1},... | collective-permute-start | bytes 393224 | tf_op jit(solution)/shard_map/ppermute | solution.py:505
  24.0 3.1 %pairs.1 = (bf16[256,512]{1,0:T(8,128)(2,1)S(1)}, bf16[256,512]{1,0:T(8,128)(2,1)S(1)}, bf16[256,512]{1,0:T(8,128)(2,1)S(1)}, bf16[256,512]{1,0:T(8,128)(2,1)S(1)}, bf16[4,128,512]{2,1,0:T(8,128)(2,1)S(1)}) custom-call(s32[18]{0:T(128)S(1)} %get-tuple-element.79.info, bf16[256,2048]{1,0:T(8,128)(2,1)S(1)} %get-tuple-element.51.normed, ...), custom_call_target="tpu_custom_call" | custom-call | flops 2100000000 | tf_op jit(solution)/shard_map/pairs/pallas_call | solution.py:203
  27.0 1.6 %collective-permute-start.2 = (bf16[256,512]{1,0:T(8,128)(2,1)S(1)}, bf16[256,512]{1,0:T(8,128)(2,1)S(1)}, u32[]{:S(2)}, u32[]{:S(2)}) collective-permute-start(bf16[256,512]{1,0:T(8,128)(2,1)S(1)} %get-tuple-element.53.refs_1_), channel_id=1, source_target_pairs={{0,4},{1,5},{2,6},{3,7},{4,0},{5,1},{6,2},{7,3},{8,12},{9,13},{10,... | collective-permute-start | bytes 786440 | tf_op jit(solution)/shard_map/ppermute | solution.py:505
  28.6 1.6 %collective-permute-start.3 = (bf16[256,512]{1,0:T(8,128)(2,1)S(1)}, bf16[256,512]{1,0:T(8,128)(2,1)S(1)}, u32[]{:S(2)}, u32[]{:S(2)}) collective-permute-start(bf16[256,512]{1,0:T(8,128)(2,1)S(1)} %get-tuple-element.54.refs_2_), channel_id=1, source_target_pairs={{0,8},{1,9},{2,10},{3,11},{4,12},{5,13},{6,14},{7,15},{8,0},{9,1},... | collective-permute-start | bytes 786440 | tf_op jit(solution)/shard_map/ppermute | solution.py:505
  31.2 1.3 %collective-permute-start.8 = (bf16[256,256]{1,0:T(8,128)(2,1)S(1)}, bf16[256,256]{1,0:T(8,128)(2,1)S(1)}, u32[]{:S(2)}, u32[]{:S(2)}) collective-permute-start(bf16[256,256]{1,0:T(8,128)(2,1)S(1)} %pick.1), channel_id=1, source_target_pairs={{16,0},{20,4},{24,8},{28,12},{17,1},{21,5},{25,9},{29,13}} | collective-permute-start | bytes 393224 | tf_op jit(solution)/shard_map/ppermute | solution.py:547
  32.5 4.1 %pages.1.refs_5_ = bf16[5,128,2,1024]{3,2,1,0:T(2,128)(2,1)} custom-call(s32[18]{0:T(128)S(1)} %get-tuple-element.79.info, bf16[256,512]{1,0:T(8,128)(2,1)S(1)} %get-tuple-element.61.refs_0_.refs_1_.refs_4_, bf16[256,512]{1,0:T(8,128)(2,1)S(1)} %get-tuple-element.53.refs_1_, bf16[256,512]{1,0:T(8,128)(2,1)S(1)} %get-tuple-element.54.refs_2_, ...), custom_call_target="tpu_custom_call" | custom-call | flops 105000000 | tf_op jit(solution)/shard_map/pages/pallas_call | solution.py:409
  37.2 4.9 %collective-permute-done.4.refs_4_.refs_7_ = bf16[256,512]{1,0:T(8,128)(2,1)S(1)} collective-permute-done((bf16[256,512]{1,0:T(8,128)(2,1)S(1)}, bf16[256,512]{1,0:T(8,128)(2,1)S(1)}, u32[]{:S(2)}, u32[]{:S(2)}) %collective-permute-start.4) | collective-permute-done | bytes 262176 | tf_op jit(solution)/shard_map/ppermute | solution.py:505
  42.6 1.0 %collective-permute-done.10.refs_6_.refs_9_ = bf16[256,512]{1,0:T(8,128)(2,1)S(1)} collective-permute-done((bf16[256,512]{1,0:T(8,128)(2,1)S(1)}, bf16[256,512]{1,0:T(8,128)(2,1)S(1)}, u32[]{:S(2)}, u32[]{:S(2)}) %collective-permute-start.10) | collective-permute-done | bytes 262176 | tf_op jit(solution)/shard_map/ppermute | solution.py:505
  44.4 2.0 %tail.1 = bf16[272,256]{1,0:T(8,128)(2,1)S(1)} custom-call(s32[18]{0:T(128)S(1)} %get-tuple-element.79.info, bf16[256,256]{1,0:T(8,128)(2,1)S(1)} %collective-permute-done.8.refs_0_, bf16[256,512]{1,0:T(8,128)(2,1)S(1)} %get-tuple-element.61.refs_0_.refs_1_.refs_4_, bf16[256,512]{1,0:T(8,128)(2,1)S(1)} %collective-permute-done.2.refs_2_.refs_5_, ...), custom_call_target="tpu_custom_call" | custom-call | flops 945000000 | tf_op jit(solution)/shard_map/tail/pallas_call | solution.py:482
  46.5 1.3 %collective-permute-start.22 = (bf16[4,128,512]{2,1,0:T(8,128)(2,1)S(1)}, bf16[4,128,512]{2,1,0:T(8,128)(2,1)S(1)}, u32[]{:S(2)}, u32[]{:S(2)}) collective-permute-start(bf16[4,128,512]{2,1,0:T(8,128)(2,1)S(1)} %get-tuple-element.81), channel_id=1, source_target_pairs={{2,0},{4,2},{6,4},{8,6},{10,8},{12,10},{14,12},{16,14},{18,16},{20... | collective-permute-start | bytes 1572872 | tf_op jit(solution)/shard_map/ppermute | solution.py:557
  47.8 6.8 %collective-permute-start.14 = (bf16[272,256]{1,0:T(8,128)(2,1)S(1)}, bf16[272,256]{1,0:T(8,128)(2,1)S(1)}, u32[]{:S(2)}, u32[]{:S(2)}) collective-permute-start(bf16[272,256]{1,0:T(8,128)(2,1)S(1)} %tail.1), channel_id=1, source_target_pairs={{0,16},{4,20},{8,24},{12,28},{1,17},{5,21},{9,25},{13,29}} | collective-permute-start | bytes 417800 | tf_op jit(solution)/shard_map/ppermute | solution.py:558
  54.6 3.5 %main.1 = (bf16[1024,256]{1,0:T(8,128)(2,1)S(1)}, f32[256,256]{1,0:T(8,128)S(1)}, f32[256,128]{1,0:T(8,128)S(1)}) custom-call(s32[18]{0:T(128)S(1)} %get-tuple-element.79.info, bf16[256,256]{1,0:T(8,128)(2,1)S(1)} %get-tuple-element.56.refs_0_, bf16[256,256]{1,0:T(8,128)(2,1)S(1)} %collective-permute-done.5.refs_1_, ...), custom_call_target="tpu_custom_call" | custom-call | flops 1680000000 | tf_op jit(solution)/shard_map/main/pallas_call | solution.py:482
  58.9 3.4 %collective-permute-start.21 = (bf16[256,256]{1,0:T(8,128)(2,1)S(1)}, bf16[256,256]{1,0:T(8,128)(2,1)S(1)}, u32[]{:S(2)}, u32[]{:S(2)}) collective-permute-start(bf16[256,256]{1,0:T(8,128)(2,1)S(1)} %get-tuple-element.77), channel_id=1, source_target_pairs={{0,12},{1,13},{2,14},{3,15},{4,8},{5,9},{6,10},{7,11},{8,4},{9,5},... | collective-permute-start | bytes 393224 | tf_op jit(solution)/shard_map/ppermute | solution.py:505
  62.4 1.3 %collective-permute-start.17 = (bf16[256,256]{1,0:T(8,128)(2,1)S(1)}, bf16[256,256]{1,0:T(8,128)(2,1)S(1)}, u32[]{:S(2)}, u32[]{:S(2)}) collective-permute-start(bf16[256,256]{1,0:T(8,128)(2,1)S(1)} %get-tuple-element.76), channel_id=1, source_target_pairs={{0,9},{1,8},{2,11},{3,10},{4,13},{5,12},{6,15},{7,14},{8,1},{9,0},... | collective-permute-start | bytes 393224 | tf_op jit(solution)/shard_map/ppermute | solution.py:505
  64.2 2.7 %collective-permute-start.18 = (bf16[256,256]{1,0:T(8,128)(2,1)S(1)}, bf16[256,256]{1,0:T(8,128)(2,1)S(1)}, u32[]{:S(2)}, u32[]{:S(2)}) collective-permute-start(bf16[256,256]{1,0:T(8,128)(2,1)S(1)} %get-tuple-element.77), channel_id=1, source_target_pairs={{0,13},{1,12},{2,15},{3,14},{4,9},{5,8},{6,11},{7,10},{8,5},{9,4},... | collective-permute-start | bytes 393224 | tf_op jit(solution)/shard_map/ppermute | solution.py:505
  66.9 1.4 %collective-permute-start.15 = (bf16[256,256]{1,0:T(8,128)(2,1)S(1)}, bf16[256,256]{1,0:T(8,128)(2,1)S(1)}, u32[]{:S(2)}, u32[]{:S(2)}) collective-permute-start(bf16[256,256]{1,0:T(8,128)(2,1)S(1)} %get-tuple-element.74.refs_0_), channel_id=1, source_target_pairs={{0,1},{1,0},{2,3},{3,2},{4,5},{5,4},{6,7},{7,6},{8,9},{9,8},{10,11... | collective-permute-start | bytes 393224 | tf_op jit(solution)/shard_map/ppermute | solution.py:505
  68.2 2.0 %crossing.1 = bf16[5,128,2,1024]{3,2,1,0:T(2,128)(2,1)} custom-call(s32[18]{0:T(128)S(1)} %get-tuple-element.79.info, bf16[256,512]{1,0:T(8,128)(2,1)S(1)} %get-tuple-element.61.refs_0_.refs_1_.refs_4_, bf16[256,512]{1,0:T(8,128)(2,1)S(1)} %get-tuple-element.53.refs_1_, ...), custom_call_target="tpu_custom_call", output_to_operand_aliasing={{}: (6, {})} | custom-call | flops 525000000 | tf_op jit(solution)/shard_map/crossing/pallas_call | solution.py:431
  70.3 1.3 %out_own.1.refs_6_ = f32[256,1024]{1,0:T(8,128)S(1)} custom-call(s32[18]{0:T(128)S(1)} %get-tuple-element.79.info, bf16[256,256]{1,0:T(8,128)(2,1)S(1)} %get-tuple-element.74.refs_0_, bf16[256,256]{1,0:T(8,128)(2,1)S(1)} %collective-permute-done.19.refs_1_, bf16[256,256]{1,0:T(8,128)(2,1)S(1)} %collective-permute-done.20.refs_2_, ...), custom_call_target="tpu_custom_call" | custom-call | flops 490000000 | tf_op jit(solution)/shard_map/out_own/pallas_call | solution.py:482
  71.5 1.6 %collective-permute-done.16.refs_1_ = bf16[256,256]{1,0:T(8,128)(2,1)S(1)} collective-permute-done((bf16[256,256]{1,0:T(8,128)(2,1)S(1)}, bf16[256,256]{1,0:T(8,128)(2,1)S(1)}, u32[]{:S(2)}, u32[]{:S(2)}) %collective-permute-start.16) | collective-permute-done | bytes 131104 | tf_op jit(solution)/shard_map/ppermute | solution.py:505
  73.1 0.8 %collective-permute-done.15.refs_0_ = bf16[256,256]{1,0:T(8,128)(2,1)S(1)} collective-permute-done((bf16[256,256]{1,0:T(8,128)(2,1)S(1)}, bf16[256,256]{1,0:T(8,128)(2,1)S(1)}, u32[]{:S(2)}, u32[]{:S(2)}) %collective-permute-start.15) | collective-permute-done | bytes 131104 | tf_op jit(solution)/shard_map/ppermute | solution.py:505
  73.9 2.1 %out_theirs.1 = bf16[256,1024]{1,0:T(8,128)(2,1)} custom-call(s32[18]{0:T(128)S(1)} %get-tuple-element.79.info, bf16[256,256]{1,0:T(8,128)(2,1)S(1)} %collective-permute-done.15.refs_0_, bf16[256,256]{1,0:T(8,128)(2,1)S(1)} %collective-permute-done.16.refs_1_, bf16[256,256]{1,0:T(8,128)(2,1)S(1)} %collective-permute-done.17.refs_2_, ...), custom_call_target="tpu_custom_call" | custom-call | flops 700000000 | tf_op jit(solution)/shard_map/out_theirs/pallas_call | solution.py:482
  (40 shorter events, 5.0 us)
Async XLA Ops:
  0.6 15.1 %collective-permute-start = (bf16[256,1024]{1,0:T(8,128)(2,1)}, bf16[256,1024]{1,0:T(8,128)(2,1)S(1)}, u32[]{:S(2)}, u32[]{:S(2)}) collective-permute-start(bf16[256,1024]{1,0:T(8,128)(2,1)} %own.1), channel_id=1, source_target_pairs={{0,1},{1,0},{2,3},{3,2},{4,5},{5,4},{6,7},{7,6},{8,9},{9,8},{10,11... | collective-permute-start | bytes 1572872 | tf_op jit(solution)/shard_map/ppermute | solution.py:505
  3.7 2.2 %copy-start = (bf16[1024,2048]{1,0:T(8,128)(2,1)S(1)}, bf16[1024,2048]{1,0:T(8,128)(2,1)}, u32[]{:S(2)}) copy-start(bf16[1024,2048]{1,0:T(8,128)(2,1)} %w_out.1) | copy-start | bytes 12582916
  5.9 1.0 %copy-start.1 = (bf16[256,1024]{1,0:T(8,128)(2,1)S(1)}, bf16[256,1024]{1,0:T(8,128)(2,1)}, u32[]{:S(2)}) copy-start(bf16[256,1024]{1,0:T(8,128)(2,1)} %own.1) | copy-start | bytes 1572868
  7.0 0.7 copy-start.2
  7.7 0.7 copy-start.3
  8.4 0.7 copy-start.4
  9.0 0.7 copy-start.5
  18.7 27.7 %collective-permute-start.1 = (bf16[512,1024]{1,0:T(8,128)(2,1)S(1)}, bf16[512,1024]{1,0:T(8,128)(2,1)S(1)}, u32[]{:S(2)}, u32[]{:S(2)}) collective-permute-start(bf16[512,1024]{1,0:T(8,128)(2,1)S(1)} %get-tuple-element.52), channel_id=1, source_target_pairs={{0,1},{1,0},{2,3},{3,2},{4,5},{5,4},{6,7},{7,6},{8,9},{9,8},{10,11... | collective-permute-start | bytes 3145736 | tf_op jit(solution)/shard_map/ppermute | solution.py:505
  20.5 8.1 %collective-permute-start.5 = (bf16[256,256]{1,0:T(8,128)(2,1)S(1)}, bf16[256,256]{1,0:T(8,128)(2,1)S(1)}, u32[]{:S(2)}, u32[]{:S(2)}) collective-permute-start(bf16[256,256]{1,0:T(8,128)(2,1)S(1)} %get-tuple-element.57), channel_id=1, source_target_pairs={{0,4},{1,5},{2,6},{3,7},{4,0},{5,1},{6,2},{7,3},{8,12},{9,13},{10,... | collective-permute-start | bytes 393224 | tf_op jit(solution)/shard_map/ppermute | solution.py:505
  22.0 8.2 %collective-permute-start.6 = (bf16[256,256]{1,0:T(8,128)(2,1)S(1)}, bf16[256,256]{1,0:T(8,128)(2,1)S(1)}, u32[]{:S(2)}, u32[]{:S(2)}) collective-permute-start(bf16[256,256]{1,0:T(8,128)(2,1)S(1)} %get-tuple-element.58), channel_id=1, source_target_pairs={{0,8},{1,9},{2,10},{3,11},{4,12},{5,13},{6,14},{7,15},{8,0},{9,1},... | collective-permute-start | bytes 393224 | tf_op jit(solution)/shard_map/ppermute | solution.py:505
  23.6 7.0 %collective-permute-start.7 = (bf16[256,256]{1,0:T(8,128)(2,1)S(1)}, bf16[256,256]{1,0:T(8,128)(2,1)S(1)}, u32[]{:S(2)}, u32[]{:S(2)}) collective-permute-start(bf16[256,256]{1,0:T(8,128)(2,1)S(1)} %get-tuple-element.59), channel_id=1, source_target_pairs={{0,12},{1,13},{2,14},{3,15},{4,8},{5,9},{6,10},{7,11},{8,4},{9,5},... | collective-permute-start | bytes 393224 | tf_op jit(solution)/shard_map/ppermute | solution.py:505
  27.0 9.9 %collective-permute-start.2 = (bf16[256,512]{1,0:T(8,128)(2,1)S(1)}, bf16[256,512]{1,0:T(8,128)(2,1)S(1)}, u32[]{:S(2)}, u32[]{:S(2)}) collective-permute-start(bf16[256,512]{1,0:T(8,128)(2,1)S(1)} %get-tuple-element.53.refs_1_), channel_id=1, source_target_pairs={{0,4},{1,5},{2,6},{3,7},{4,0},{5,1},{6,2},{7,3},{8,12},{9,13},{10,... | collective-permute-start | bytes 786440 | tf_op jit(solution)/shard_map/ppermute | solution.py:505
  28.6 8.6 %collective-permute-start.3 = (bf16[256,512]{1,0:T(8,128)(2,1)S(1)}, bf16[256,512]{1,0:T(8,128)(2,1)S(1)}, u32[]{:S(2)}, u32[]{:S(2)}) collective-permute-start(bf16[256,512]{1,0:T(8,128)(2,1)S(1)} %get-tuple-element.54.refs_2_), channel_id=1, source_target_pairs={{0,8},{1,9},{2,10},{3,11},{4,12},{5,13},{6,14},{7,15},{8,0},{9,1},... | collective-permute-start | bytes 786440 | tf_op jit(solution)/shard_map/ppermute | solution.py:505
  30.2 11.9 %collective-permute-start.4 = (bf16[256,512]{1,0:T(8,128)(2,1)S(1)}, bf16[256,512]{1,0:T(8,128)(2,1)S(1)}, u32[]{:S(2)}, u32[]{:S(2)}) collective-permute-start(bf16[256,512]{1,0:T(8,128)(2,1)S(1)} %get-tuple-element.55.refs_3_), channel_id=1, source_target_pairs={{0,12},{1,13},{2,14},{3,15},{4,8},{5,9},{6,10},{7,11},{8,4},{9,5},... | collective-permute-start | bytes 786440 | tf_op jit(solution)/shard_map/ppermute | solution.py:505
  31.2 10.9 %collective-permute-start.8 = (bf16[256,256]{1,0:T(8,128)(2,1)S(1)}, bf16[256,256]{1,0:T(8,128)(2,1)S(1)}, u32[]{:S(2)}, u32[]{:S(2)}) collective-permute-start(bf16[256,256]{1,0:T(8,128)(2,1)S(1)} %pick.1), channel_id=1, source_target_pairs={{16,0},{20,4},{24,8},{28,12},{17,1},{21,5},{25,9},{29,13}} | collective-permute-start | bytes 393224 | tf_op jit(solution)/shard_map/ppermute | solution.py:547
  36.9 5.6 %collective-permute-start.9 = (bf16[256,512]{1,0:T(8,128)(2,1)S(1)}, bf16[256,512]{1,0:T(8,128)(2,1)S(1)}, u32[]{:S(2)}, u32[]{:S(2)}) collective-permute-start(bf16[256,512]{1,0:T(8,128)(2,1)S(1)} %get-tuple-element.61.refs_0_.refs_1_.refs_4_), channel_id=1, source_target_pairs={{0,2},{1,3},{2,0},{3,1},{4,6},{5,7},{6,4},{7,5},{8,10},{9,11},{10,... | collective-permute-start | bytes 786440 | tf_op jit(solution)/shard_map/ppermute | solution.py:505
  42.1 1.5 %collective-permute-start.10 = (bf16[256,512]{1,0:T(8,128)(2,1)S(1)}, bf16[256,512]{1,0:T(8,128)(2,1)S(1)}, u32[]{:S(2)}, u32[]{:S(2)}) collective-permute-start(bf16[256,512]{1,0:T(8,128)(2,1)S(1)} %collective-permute-done.2.refs_2_.refs_5_), channel_id=1, source_target_pairs={{0,2},{1,3},{2,0},{3,1},{4,6},{5,7},{6,4},{7,5},{8,10},{9,11},{10,... | collective-permute-start | bytes 786440 | tf_op jit(solution)/shard_map/ppermute | solution.py:505
  42.1 1.9 %collective-permute-start.11 = (bf16[256,512]{1,0:T(8,128)(2,1)S(1)}, bf16[256,512]{1,0:T(8,128)(2,1)S(1)}, u32[]{:S(2)}, u32[]{:S(2)}) collective-permute-start(bf16[256,512]{1,0:T(8,128)(2,1)S(1)} %collective-permute-done.3.refs_3_.refs_6_), channel_id=1, source_target_pairs={{0,2},{1,3},{2,0},{3,1},{4,6},{5,7},{6,4},{7,5},{8,10},{9,11},{10,... | collective-permute-start | bytes 786440 | tf_op jit(solution)/shard_map/ppermute | solution.py:505
  42.6 1.8 %collective-permute-start.12 = (bf16[256,512]{1,0:T(8,128)(2,1)S(1)}, bf16[256,512]{1,0:T(8,128)(2,1)S(1)}, u32[]{:S(2)}, u32[]{:S(2)}) collective-permute-start(bf16[256,512]{1,0:T(8,128)(2,1)S(1)} %collective-permute-done.4.refs_4_.refs_7_), channel_id=1, source_target_pairs={{0,2},{1,3},{2,0},{3,1},{4,6},{5,7},{6,4},{7,5},{8,10},{9,11},{10,... | collective-permute-start | bytes 786440 | tf_op jit(solution)/shard_map/ppermute | solution.py:505
  46.4 11.7 %collective-permute-start.13 = (bf16[512,1024]{1,0:T(8,128)(2,1)S(1)}, bf16[512,1024]{1,0:T(8,128)(2,1)S(1)}, u32[]{:S(2)}, u32[]{:S(2)}) collective-permute-start(bf16[512,1024]{1,0:T(8,128)(2,1)S(1)} %collective-permute-done.1.refs_4_), channel_id=1, source_target_pairs={{0,2},{1,3},{2,0},{3,1},{4,6},{5,7},{6,4},{7,5},{8,10},{9,11},{10,... | collective-permute-start | bytes 3145736 | tf_op jit(solution)/shard_map/ppermute | solution.py:505
  46.5 15.9 %collective-permute-start.22 = (bf16[4,128,512]{2,1,0:T(8,128)(2,1)S(1)}, bf16[4,128,512]{2,1,0:T(8,128)(2,1)S(1)}, u32[]{:S(2)}, u32[]{:S(2)}) collective-permute-start(bf16[4,128,512]{2,1,0:T(8,128)(2,1)S(1)} %get-tuple-element.81), channel_id=1, source_target_pairs={{2,0},{4,2},{6,4},{8,6},{10,8},{12,10},{14,12},{16,14},{18,16},{20... | collective-permute-start | bytes 1572872 | tf_op jit(solution)/shard_map/ppermute | solution.py:557
  47.8 10.3 %collective-permute-start.14 = (bf16[272,256]{1,0:T(8,128)(2,1)S(1)}, bf16[272,256]{1,0:T(8,128)(2,1)S(1)}, u32[]{:S(2)}, u32[]{:S(2)}) collective-permute-start(bf16[272,256]{1,0:T(8,128)(2,1)S(1)} %tail.1), channel_id=1, source_target_pairs={{0,16},{4,20},{8,24},{12,28},{1,17},{5,21},{9,25},{13,29}} | collective-permute-start | bytes 417800 | tf_op jit(solution)/shard_map/ppermute | solution.py:558
  58.7 5.5 %collective-permute-start.19 = (bf16[256,256]{1,0:T(8,128)(2,1)S(1)}, bf16[256,256]{1,0:T(8,128)(2,1)S(1)}, u32[]{:S(2)}, u32[]{:S(2)}) collective-permute-start(bf16[256,256]{1,0:T(8,128)(2,1)S(1)} %get-tuple-element.75), channel_id=1, source_target_pairs={{0,4},{1,5},{2,6},{3,7},{4,0},{5,1},{6,2},{7,3},{8,12},{9,13},{10,... | collective-permute-start | bytes 393224 | tf_op jit(solution)/shard_map/ppermute | solution.py:505
  58.8 8.1 %collective-permute-start.20 = (bf16[256,256]{1,0:T(8,128)(2,1)S(1)}, bf16[256,256]{1,0:T(8,128)(2,1)S(1)}, u32[]{:S(2)}, u32[]{:S(2)}) collective-permute-start(bf16[256,256]{1,0:T(8,128)(2,1)S(1)} %get-tuple-element.76), channel_id=1, source_target_pairs={{0,8},{1,9},{2,10},{3,11},{4,12},{5,13},{6,14},{7,15},{8,0},{9,1},... | collective-permute-start | bytes 393224 | tf_op jit(solution)/shard_map/ppermute | solution.py:505
  58.9 11.4 %collective-permute-start.21 = (bf16[256,256]{1,0:T(8,128)(2,1)S(1)}, bf16[256,256]{1,0:T(8,128)(2,1)S(1)}, u32[]{:S(2)}, u32[]{:S(2)}) collective-permute-start(bf16[256,256]{1,0:T(8,128)(2,1)S(1)} %get-tuple-element.77), channel_id=1, source_target_pairs={{0,12},{1,13},{2,14},{3,15},{4,8},{5,9},{6,10},{7,11},{8,4},{9,5},... | collective-permute-start | bytes 393224 | tf_op jit(solution)/shard_map/ppermute | solution.py:505
  62.3 10.8 %collective-permute-start.16 = (bf16[256,256]{1,0:T(8,128)(2,1)S(1)}, bf16[256,256]{1,0:T(8,128)(2,1)S(1)}, u32[]{:S(2)}, u32[]{:S(2)}) collective-permute-start(bf16[256,256]{1,0:T(8,128)(2,1)S(1)} %get-tuple-element.75), channel_id=1, source_target_pairs={{0,5},{1,4},{2,7},{3,6},{4,1},{5,0},{6,3},{7,2},{8,13},{9,12},{10,... | collective-permute-start | bytes 393224 | tf_op jit(solution)/shard_map/ppermute | solution.py:505
  62.4 10.7 %collective-permute-start.17 = (bf16[256,256]{1,0:T(8,128)(2,1)S(1)}, bf16[256,256]{1,0:T(8,128)(2,1)S(1)}, u32[]{:S(2)}, u32[]{:S(2)}) collective-permute-start(bf16[256,256]{1,0:T(8,128)(2,1)S(1)} %get-tuple-element.76), channel_id=1, source_target_pairs={{0,9},{1,8},{2,11},{3,10},{4,13},{5,12},{6,15},{7,14},{8,1},{9,0},... | collective-permute-start | bytes 393224 | tf_op jit(solution)/shard_map/ppermute | solution.py:505
  64.2 8.9 %collective-permute-start.18 = (bf16[256,256]{1,0:T(8,128)(2,1)S(1)}, bf16[256,256]{1,0:T(8,128)(2,1)S(1)}, u32[]{:S(2)}, u32[]{:S(2)}) collective-permute-start(bf16[256,256]{1,0:T(8,128)(2,1)S(1)} %get-tuple-element.77), channel_id=1, source_target_pairs={{0,13},{1,12},{2,15},{3,14},{4,9},{5,8},{6,11},{7,10},{8,5},{9,4},... | collective-permute-start | bytes 393224 | tf_op jit(solution)/shard_map/ppermute | solution.py:505
  66.9 7.1 %collective-permute-start.15 = (bf16[256,256]{1,0:T(8,128)(2,1)S(1)}, bf16[256,256]{1,0:T(8,128)(2,1)S(1)}, u32[]{:S(2)}, u32[]{:S(2)}) collective-permute-start(bf16[256,256]{1,0:T(8,128)(2,1)S(1)} %get-tuple-element.74.refs_0_), channel_id=1, source_target_pairs={{0,1},{1,0},{2,3},{3,2},{4,5},{5,4},{6,7},{7,6},{8,9},{9,8},{10,11... | collective-permute-start | bytes 393224 | tf_op jit(solution)/shard_map/ppermute | solution.py:505
